TPU v7x, 32 devices: a whole 2x2x4 slice. The times are simulated.
32 devices in a mesh: img: 2 (over core), rows: 16 (over z, y, x).
Axes of the slice: x: 2, y: 2, z: 4, core: 2. Of those that a mesh axis runs over, the one named last changes fastest.
Arguments:
- tokens: bfloat16 [672, 42, 768], P(('img', 'rows')), may hold values from -6 to 6
- extent: int32 [16, 2], replicated, may hold values from 16 to 32, as said below
- pre_gain: bfloat16 [768], P(('img', 'rows')), may hold values from 0.099609375 to 1.8984375
- pre_bias: bfloat16 [768], P(('img', 'rows')), may hold values from -1.75 to 1.75
- triple_weight: bfloat16 [768, 2304], P(('img', 'rows')), may hold values from -0.21875 to 0.21875
- triple_bias: bfloat16 [1536], P(('img', 'rows')), may hold values from -3 to 3
- height_table: bfloat16 [27, 64], replicated, may hold values from -0.5 to 0.5
- width_table: bfloat16 [27, 64], replicated, may hold values from -0.5 to 0.5
- output_weight: bfloat16 [768, 768], P(('img', 'rows')), may hold values from -0.875 to 0.875
- output_bias: bfloat16 [768], P(('img', 'rows')), may hold values from -1.75 to 1.75
- post_gain: bfloat16 [768], P(('img', 'rows')), may hold values from 0.099609375 to 1.8984375
- post_bias: bfloat16 [768], P(('img', 'rows')), may hold values from -1.75 to 1.75
- expand_weight: bfloat16 [768, 3072], P(('img', 'rows')), may hold values from -0.21875 to 0.21875
- expand_bias: bfloat16 [3072], P(('img', 'rows')), may hold values from -3 to 3
- reduce_weight: bfloat16 [3072, 768], P(('img', 'rows')), may hold values from -0.109375 to 0.109375
- reduce_bias: bfloat16 [768], P(('img', 'rows')), may hold values from -1.75 to 1.75
- cotangent: bfloat16 [672, 42, 768], P(('img', 'rows')), may hold values from -6 to 6
Outputs:
- block_output: bfloat16 [672, 42, 768], P(('img', 'rows'))
- input_grad: bfloat16 [672, 42, 768], P(('img', 'rows'))
- pre_gain_grad: float32 [768], P(('img', 'rows'))
- pre_bias_grad: float32 [768], P(('img', 'rows'))
- triple_weight_grad: float32 [768, 2304], P(('img', 'rows'))
- triple_bias_grad: float32 [1536], P(('img', 'rows'))
- height_table_grad: float32 [27, 64], replicated
- width_table_grad: float32 [27, 64], replicated
- output_weight_grad: float32 [768, 768], P(('img', 'rows'))
- output_bias_grad: float32 [768], P(('img', 'rows'))
- post_gain_grad: float32 [768], P(('img', 'rows'))
- post_bias_grad: float32 [768], P(('img', 'rows'))
- expand_weight_grad: float32 [768, 3072], P(('img', 'rows'))
- expand_bias_grad: float32 [3072], P(('img', 'rows'))
- reduce_weight_grad: float32 [3072, 768], P(('img', 'rows'))
- reduce_bias_grad: float32 [768], P(('img', 'rows'))
Inputs may be any that keep to these rules, and one draw needn't show every extreme that they name: extent[i] is image i's real height and width; the larger of the two is 32, and some image has a side of 16.
All inputs are finite; a program needn't handle non-finite values.
Results may differ from a plain program's by a relative error of at most 0.012.
Values may be sent and summed in bfloat16 or wider, within the bound.
No kernel may reach another device: no remote copies, remote signals or barrier semaphores. Data moves between devices by JAX's collectives and lax.ppermute only.
A program may use at most 448 MiB of HBM per device.

v0:
```python
from functools import partial

import jax
import jax.numpy as jnp
from jax import lax
from jax.sharding import PartitionSpec as P

HEADS = 12
HEAD_DIM = 64


FINEST = lax.Precision.HIGHEST


def swapped(block, axis, bit):
    count = lax.axis_size(axis)
    route = []
    for low in range(count):
        high = low | 1 << bit
        if high != low and high < count:
            route += [(low, high), (high, low)]
    return lax.ppermute(block, axis, route)


def layer_norm(value, gain, bias):
    center = jnp.mean(value, axis=-1, keepdims=True)
    centred = value - center
    variance = jnp.mean(centred * centred, axis=-1, keepdims=True)
    return centred * lax.rsqrt(variance + 1e-06) * gain + bias


def contract_first(left, right):
    return lax.dot_general(
        left, right, (((0,), (0,)), ((), ())), preferred_element_type=jnp.float32
    )


def contract_last(left, right):
    return lax.dot_general(
        left, right, (((1,), (1,)), ((), ())), preferred_element_type=jnp.float32
    )


def band_tables(table, rows_count, offset, span):
    query_pos = jnp.arange(rows_count, dtype=jnp.int32)[:, None, None] + offset
    key_pos = jnp.arange(span, dtype=jnp.int32)[None, :, None]
    slots = jnp.arange(table.shape[0], dtype=jnp.int32)[None, None, :]
    onehot = (query_pos - key_pos + span - 1 == slots).astype(jnp.bfloat16)
    picked = jnp.einsum("rsj,jd->rsd", onehot, table, preferred_element_type=jnp.float32)
    return (onehot, picked)


def split_heads(array, span):
    return array.reshape(array.shape[0], array.shape[1] // span, span, HEADS, HEAD_DIM)


def band_scores(query_five, key_five, height_pick, width_pick):
    scores = jnp.einsum(
        "rnchd,snkhd->nhrcsk", query_five, key_five, preferred_element_type=jnp.float32
    ) * HEAD_DIM ** (-0.5)
    along_rows = jnp.einsum(
        "rnchd,rsd->nhrcs",
        query_five,
        height_pick.astype(jnp.bfloat16),
        preferred_element_type=jnp.float32,
    )
    along_cols = jnp.einsum(
        "rnchd,ckd->nhrck",
        query_five,
        width_pick.astype(jnp.bfloat16),
        preferred_element_type=jnp.float32,
    )
    scores = scores + along_rows[..., None] + along_cols[..., None, :]
    shape = scores.shape
    return scores.reshape(shape[:4] + (shape[4] * shape[5],))


def band_forward(queries, keys, values, height_pick, width_pick):
    span = keys.shape[0]
    query_five = split_heads(queries, span)
    key_five = split_heads(keys, span)
    value_five = split_heads(values, span)
    scores = band_scores(query_five, key_five, height_pick, width_pick)
    top = jnp.max(scores, axis=-1, keepdims=True)
    weights = jnp.exp(scores - top)
    total = jnp.sum(weights, axis=-1, keepdims=True)
    probs = (weights / total).astype(jnp.bfloat16)
    log_total = top + jnp.log(total)
    probs_six = probs.reshape(probs.shape[:4] + (span, span))
    mixed = jnp.einsum(
        "nhrcsk,snkhd->rnchd", probs_six, value_five, preferred_element_type=jnp.float32
    )
    return (mixed.reshape(queries.shape), log_total)


def band_backward(queries, keys, values, height_pick, width_pick, log_total, grad_mixed):
    span = keys.shape[0]
    query_five = split_heads(queries, span)
    key_five = split_heads(keys, span)
    value_five = split_heads(values, span)
    grad_five = split_heads(grad_mixed, span)
    scores = band_scores(query_five, key_five, height_pick, width_pick)
    probs = jnp.exp(scores - log_total)
    six = probs.shape[:4] + (span, span)
    grad_probs = jnp.einsum(
        "rnchd,snkhd->nhrcsk", grad_five, value_five, preferred_element_type=jnp.float32
    ).reshape(probs.shape)
    grad_scores = probs * (grad_probs - jnp.sum(probs * grad_probs, axis=-1, keepdims=True))
    grad_round = grad_scores.astype(jnp.bfloat16).reshape(six)
    probs_round = probs.astype(jnp.bfloat16).reshape(six)
    grad_values = jnp.einsum(
        "nhrcsk,rnchd->snkhd", probs_round, grad_five, preferred_element_type=jnp.float32
    )
    grad_keys = jnp.einsum(
        "nhrcsk,rnchd->snkhd", grad_round, query_five, preferred_element_type=jnp.float32
    ) * HEAD_DIM ** (-0.5)
    grad_queries = jnp.einsum(
        "nhrcsk,snkhd->rnchd", grad_round, key_five, preferred_element_type=jnp.float32
    ) * HEAD_DIM ** (-0.5)
    row_sums = jnp.sum(grad_round, axis=5, dtype=jnp.float32)
    col_sums = jnp.sum(grad_round, axis=4, dtype=jnp.float32)
    grad_queries = grad_queries + jnp.einsum(
        "nhrcs,rsd->rnchd",
        row_sums,
        height_pick,
        precision=FINEST,
        preferred_element_type=jnp.float32,
    )
    grad_queries = grad_queries + jnp.einsum(
        "nhrck,ckd->rnchd",
        col_sums,
        width_pick,
        precision=FINEST,
        preferred_element_type=jnp.float32,
    )
    query_wide = query_five.astype(jnp.float32)
    height_part = jnp.einsum(
        "nhrcs,rnchd->rsd",
        row_sums,
        query_wide,
        precision=FINEST,
        preferred_element_type=jnp.float32,
    )
    width_part = jnp.einsum(
        "nhrck,rnchd->ckd",
        col_sums,
        query_wide,
        precision=FINEST,
        preferred_element_type=jnp.float32,
    )
    return (
        grad_queries.reshape(queries.shape),
        grad_keys.reshape(keys.shape),
        grad_values.reshape(values.shape),
        height_part,
        width_part,
    )


def local(
    tokens,
    extent,
    pre_gain,
    pre_bias,
    triple_weight,
    triple_bias,
    height_table,
    width_table,
    output_weight,
    output_bias,
    post_gain,
    post_bias,
    expand_weight,
    expand_bias,
    reduce_weight,
    reduce_bias,
    cotangent,
):
    rows_dev, grid, width = tokens.shape
    span = grid // 3
    half = span // 2
    flat_rows = rows_dev * grid
    parity = lax.axis_index("rows") % 2
    image = lax.axis_index("img") * (lax.axis_size("rows") // 2) + lax.axis_index("rows") // 2
    sides = lax.dynamic_slice(extent, (image, 0), (1, 2))
    row_pos = parity * rows_dev + jnp.arange(rows_dev, dtype=jnp.int32)
    col_pos = jnp.arange(grid, dtype=jnp.int32)
    mask = ((row_pos[:, None] < sides[0, 0]) & (col_pos[None, :] < sides[0, 1])).astype(
        jnp.float32
    )[..., None]
    mask_flat = mask.reshape(flat_rows, 1)
    gathered = (
        lax.all_gather(pre_gain, ("img", "rows"), axis=0, tiled=True),
        lax.all_gather(pre_bias, ("img", "rows"), axis=0, tiled=True),
        lax.all_gather(triple_weight, ("img", "rows"), axis=0, tiled=True),
        lax.all_gather(triple_bias, ("img", "rows"), axis=0, tiled=True),
        lax.all_gather(output_weight, ("img", "rows"), axis=0, tiled=True),
        lax.all_gather(output_bias, ("img", "rows"), axis=0, tiled=True),
        lax.all_gather(post_gain, ("img", "rows"), axis=0, tiled=True),
        lax.all_gather(post_bias, ("img", "rows"), axis=0, tiled=True),
        lax.all_gather(expand_weight, ("img", "rows"), axis=0, tiled=True),
        lax.all_gather(expand_bias, ("img", "rows"), axis=0, tiled=True),
        lax.all_gather(reduce_weight, ("img", "rows"), axis=0, tiled=True),
        lax.all_gather(reduce_bias, ("img", "rows"), axis=0, tiled=True),
    )
    pre_gain_all = gathered[0].astype(jnp.float32)
    pre_bias_all = gathered[1].astype(jnp.float32)
    triple_all = gathered[2]
    triple_bias_all = gathered[3].astype(jnp.float32)
    output_all = gathered[4]
    output_bias_all = gathered[5].astype(jnp.float32)
    post_gain_all = gathered[6].astype(jnp.float32)
    post_bias_all = gathered[7].astype(jnp.float32)
    expand_all = gathered[8]
    expand_bias_all = gathered[9].astype(jnp.float32)
    reduce_all = gathered[10]
    reduce_bias_all = gathered[11].astype(jnp.float32)
    flat = tokens.reshape(flat_rows, width).astype(jnp.float32)
    normed, pre_back = jax.vjp(layer_norm, flat, pre_gain_all, pre_bias_all)
    entry = (mask_flat * normed).astype(jnp.bfloat16)
    joint = jnp.dot(entry, triple_all, preferred_element_type=jnp.float32)
    queries = (
        (joint[:, :width] + triple_bias_all[:width])
        .astype(jnp.bfloat16)
        .reshape(rows_dev, grid, width)
    )
    keys = joint[:, width : 2 * width].astype(jnp.bfloat16).reshape(rows_dev, grid, width)
    values = (
        (joint[:, 2 * width :] + triple_bias_all[width:])
        .astype(jnp.bfloat16)
        .reshape(rows_dev, grid, width)
    )
    own_start = (1 - parity) * span
    full_start = parity * half
    own_keys = lax.dynamic_slice_in_dim(keys, own_start, half, 0)
    own_values = lax.dynamic_slice_in_dim(values, own_start, half, 0)
    far_keys, far_values = swapped((own_keys, own_values), "rows", 0)

    def arrange(own_part, far_part):
        return jnp.where(
            parity == 0,
            jnp.concatenate([own_part, far_part], 0),
            jnp.concatenate([far_part, own_part], 0),
        )

    cut_keys = arrange(own_keys, far_keys)
    cut_values = arrange(own_values, far_values)
    cut_queries = lax.dynamic_slice_in_dim(queries, own_start, half, 0)
    full_queries = lax.dynamic_slice_in_dim(queries, full_start, span, 0)
    full_keys = lax.dynamic_slice_in_dim(keys, full_start, span, 0)
    full_values = lax.dynamic_slice_in_dim(values, full_start, span, 0)
    onehot_full, pick_full = band_tables(height_table, span, 0, span)
    onehot_cut, pick_cut = band_tables(height_table, half, parity * half, span)
    onehot_across, pick_across = band_tables(width_table, span, 0, span)
    full_mixed, full_total = band_forward(
        full_queries, full_keys, full_values, pick_full, pick_across
    )
    cut_mixed, cut_total = band_forward(cut_queries, cut_keys, cut_values, pick_cut, pick_across)
    mixed = jnp.zeros((rows_dev, grid, width), jnp.float32)
    mixed = lax.dynamic_update_slice_in_dim(mixed, full_mixed, full_start, 0)
    mixed = lax.dynamic_update_slice_in_dim(mixed, cut_mixed, own_start, 0)
    mixed_round = mixed.astype(jnp.bfloat16).reshape(flat_rows, width)
    branch = jnp.dot(mixed_round, output_all, preferred_element_type=jnp.float32) + output_bias_all
    middle = flat + mask_flat * branch
    normed_two, post_back = jax.vjp(layer_norm, middle, post_gain_all, post_bias_all)
    entry_two = normed_two.astype(jnp.bfloat16)
    hidden = jnp.dot(entry_two, expand_all, preferred_element_type=jnp.float32) + expand_bias_all
    active, gelu_back = jax.vjp(partial(jax.nn.gelu, approximate=False), hidden)
    active_round = active.astype(jnp.bfloat16)
    result = jnp.dot(active_round, reduce_all, preferred_element_type=jnp.float32) + reduce_bias_all
    block_output = (
        (mask_flat * (middle + result)).astype(jnp.bfloat16).reshape(rows_dev, grid, width)
    )
    triple_back, output_back, expand_back, reduce_back = (
        lax.all_gather(triple_weight, ("img", "rows"), axis=0, tiled=True),
        lax.all_gather(output_weight, ("img", "rows"), axis=0, tiled=True),
        lax.all_gather(expand_weight, ("img", "rows"), axis=0, tiled=True),
        lax.all_gather(reduce_weight, ("img", "rows"), axis=0, tiled=True),
    )
    incoming = mask_flat * cotangent.reshape(flat_rows, width).astype(jnp.float32)
    incoming_round = incoming.astype(jnp.bfloat16)
    reduce_weight_grad = contract_first(active_round, incoming_round)
    reduce_bias_grad = jnp.sum(incoming, axis=0)
    grad_active = contract_last(incoming_round, reduce_back)
    (grad_hidden,) = gelu_back(grad_active)
    grad_hidden_round = grad_hidden.astype(jnp.bfloat16)
    expand_weight_grad = contract_first(entry_two, grad_hidden_round)
    expand_bias_grad = jnp.sum(grad_hidden_round, axis=0, dtype=jnp.float32)
    grad_entry_two = contract_last(grad_hidden_round, expand_back)
    grad_middle_norm, post_gain_grad, post_bias_grad = post_back(grad_entry_two)
    grad_middle = incoming + grad_middle_norm
    grad_branch = (mask_flat * grad_middle).astype(jnp.bfloat16)
    output_weight_grad = contract_first(mixed_round, grad_branch)
    output_bias_grad = jnp.sum(grad_branch, axis=0, dtype=jnp.float32)
    grad_mixed = (
        contract_last(grad_branch, output_back).astype(jnp.bfloat16).reshape(rows_dev, grid, width)
    )
    full_grad_mixed = lax.dynamic_slice_in_dim(grad_mixed, full_start, span, 0)
    cut_grad_mixed = lax.dynamic_slice_in_dim(grad_mixed, own_start, half, 0)
    full_parts = band_backward(
        full_queries, full_keys, full_values, pick_full, pick_across, full_total, full_grad_mixed
    )
    cut_parts = band_backward(
        cut_queries, cut_keys, cut_values, pick_cut, pick_across, cut_total, cut_grad_mixed
    )
    own_offset = parity * half
    far_offset = (1 - parity) * half
    far_keys_grad = lax.dynamic_slice_in_dim(cut_parts[1], far_offset, half, 0)
    far_values_grad = lax.dynamic_slice_in_dim(cut_parts[2], far_offset, half, 0)
    back_keys, back_values = (
        swapped(far_keys_grad.astype(jnp.bfloat16), "rows", 0).astype(far_keys_grad.dtype),
        swapped(far_values_grad.astype(jnp.bfloat16), "rows", 0).astype(far_values_grad.dtype),
    )
    own_keys_grad = lax.dynamic_slice_in_dim(cut_parts[1], own_offset, half, 0) + back_keys
    own_values_grad = lax.dynamic_slice_in_dim(cut_parts[2], own_offset, half, 0) + back_values
    empty = jnp.zeros((rows_dev, grid, width), jnp.float32)
    grad_queries = lax.dynamic_update_slice_in_dim(empty, full_parts[0], full_start, 0)
    grad_queries = lax.dynamic_update_slice_in_dim(grad_queries, cut_parts[0], own_start, 0)
    grad_keys = lax.dynamic_update_slice_in_dim(empty, full_parts[1], full_start, 0)
    grad_keys = lax.dynamic_update_slice_in_dim(grad_keys, own_keys_grad, own_start, 0)
    grad_values = lax.dynamic_update_slice_in_dim(empty, full_parts[2], full_start, 0)
    grad_values = lax.dynamic_update_slice_in_dim(grad_values, own_values_grad, own_start, 0)
    height_grad = jnp.einsum(
        "rsj,rsd->jd",
        onehot_full.astype(jnp.float32),
        full_parts[3],
        precision=FINEST,
        preferred_element_type=jnp.float32,
    )
    height_grad = height_grad + jnp.einsum(
        "rsj,rsd->jd",
        onehot_cut.astype(jnp.float32),
        cut_parts[3],
        precision=FINEST,
        preferred_element_type=jnp.float32,
    )
    across_grad = jnp.einsum(
        "rsj,rsd->jd",
        onehot_across.astype(jnp.float32),
        full_parts[4] + cut_parts[4],
        precision=FINEST,
        preferred_element_type=jnp.float32,
    )
    height_table_grad, width_table_grad = lax.psum((height_grad, across_grad), ("img", "rows"))
    grad_joint = (
        jnp.concatenate([grad_queries, grad_keys, grad_values], axis=-1)
        .astype(jnp.bfloat16)
        .reshape(flat_rows, 3 * width)
    )
    triple_weight_grad = contract_first(entry, grad_joint)
    joint_sums = jnp.sum(grad_joint, axis=0, dtype=jnp.float32)
    triple_bias_grad = jnp.concatenate([joint_sums[:width], joint_sums[2 * width :]])
    grad_entry = contract_last(grad_joint, triple_back)
    grad_flat_norm, pre_gain_grad, pre_bias_grad = pre_back(mask_flat * grad_entry)
    input_grad = (grad_middle + grad_flat_norm).astype(jnp.bfloat16).reshape(rows_dev, grid, width)
    shards = (
        lax.psum_scatter(pre_gain_grad, ("img", "rows"), scatter_dimension=0, tiled=True),
        lax.psum_scatter(pre_bias_grad, ("img", "rows"), scatter_dimension=0, tiled=True),
        lax.psum_scatter(triple_weight_grad, ("img", "rows"), scatter_dimension=0, tiled=True),
        lax.psum_scatter(triple_bias_grad, ("img", "rows"), scatter_dimension=0, tiled=True),
        lax.psum_scatter(output_weight_grad, ("img", "rows"), scatter_dimension=0, tiled=True),
        lax.psum_scatter(output_bias_grad, ("img", "rows"), scatter_dimension=0, tiled=True),
        lax.psum_scatter(post_gain_grad, ("img", "rows"), scatter_dimension=0, tiled=True),
        lax.psum_scatter(post_bias_grad, ("img", "rows"), scatter_dimension=0, tiled=True),
        lax.psum_scatter(expand_weight_grad, ("img", "rows"), scatter_dimension=0, tiled=True),
        lax.psum_scatter(expand_bias_grad, ("img", "rows"), scatter_dimension=0, tiled=True),
        lax.psum_scatter(reduce_weight_grad, ("img", "rows"), scatter_dimension=0, tiled=True),
        lax.psum_scatter(reduce_bias_grad, ("img", "rows"), scatter_dimension=0, tiled=True),
    )
    return (
        block_output,
        input_grad,
        shards[0],
        shards[1],
        shards[2],
        shards[3],
        height_table_grad,
        width_table_grad,
        shards[4],
        shards[5],
        shards[6],
        shards[7],
        shards[8],
        shards[9],
        shards[10],
        shards[11],
    )


def solution(mesh):
    in_specs = (
        P(("img", "rows"), None, None),
        P(),
        P(("img", "rows")),
        P(("img", "rows")),
        P(("img", "rows"), None),
        P(("img", "rows")),
        P(),
        P(),
        P(("img", "rows"), None),
        P(("img", "rows")),
        P(("img", "rows")),
        P(("img", "rows")),
        P(("img", "rows"), None),
        P(("img", "rows")),
        P(("img", "rows"), None),
        P(("img", "rows")),
        P(("img", "rows"), None, None),
    )
    out_specs = (
        P(("img", "rows"), None, None),
        P(("img", "rows"), None, None),
        P(("img", "rows")),
        P(("img", "rows")),
        P(("img", "rows"), None),
        P(("img", "rows")),
        P(),
        P(),
        P(("img", "rows"), None),
        P(("img", "rows")),
        P(("img", "rows")),
        P(("img", "rows")),
        P(("img", "rows"), None),
        P(("img", "rows")),
        P(("img", "rows"), None),
        P(("img", "rows")),
    )
    return jax.shard_map(local, mesh=mesh, in_specs=in_specs, out_specs=out_specs, check_vma=False)
```

profile of v0, /device:TPU:0, one launch (start us, length us, event | category | flops | bytes accessed | tf_op | source)
XLA Modules:
  0.0 1139.4 jit_solution(15306280458702961966)
XLA Ops:
  18.4 43.0 %all-reduce.17 = (bf16[768]{0:T(1024)(128)(2,1)S(1)}, bf16[768]{0:T(1024)(128)(2,1)S(1)}, bf16[1536]{0:T(1024)(128)(2,1)S(1)}, bf16[768]{0:T(1024)(128)(2,1)S(1)...) all-reduce(bf16[768]{0:T(1024)(128)(2,1)S(1)} %dynamic-update-slice, ...), channel_id=1, replica_groups=mesh['img'=2,'rows'=16] {'img','rows'}, use_global_device_ids=true, to_apply=%add.1 | all-reduce | flops 9216 | bytes 36864
  131.1 26.3 %fusion.134 = (f32[3,12,14,14]{3,2,1,0:T(8,128)S(1)}, f32[3,12,14,14,14,14]{3,5,4,2,1,0:T(8,128)}) fusion(f32[3,12,14,14,14]{3,4,2,1,0:T(8,128)} %copy.108, bf16[14,3,14,12,64,1]{4,3,2,1,0,5:T(8,128)(2,1)} %bitcast.189, bf16[14,3,14,12,64,1]{4,3,2,1,0,5:T(8,128)(2,1)S(1)} %bitcast.185, f32[3,12,14,14,14]{3,4,1,0,2:T(8,128)} %convolution_bitcast_fusion.1), kind=kOutput, calls=%fused_computation.220 | convolution fusion | flops 182545776 | bytes 8156736 | tf_op jit(solution)/shard_map/rnchd,snkhd->nhrcsk/dot_general | solution.py:58
  157.4 18.9 %fusion = f32[3,12,14,14]{3,2,1,0:T(8,128)S(1)} fusion(f32[3,12,14,14,14,14]{3,5,4,2,1,0:T(8,128)} %get-tuple-element.65, f32[3,12,14,14]{3,2,1,0:T(8,128)S(1)} %get-tuple-element.64), kind=kLoop, calls=%fused_computation.8 | loop fusion | flops 2758896 | bytes 5588352 | tf_op jit(solution)/shard_map/reduce_sum | solution.py:86
  176.3 23.0 %fusion.40 = bf16[14,3,14,12,64]{4,2,0,3,1:T(8,128)(2,1)} fusion(f32[3,12,14,14,14,14]{3,5,4,2,1,0:T(8,128)} %get-tuple-element.65, f32[3,12,14,14]{3,2,1,0:T(8,128)S(1)} %fusion, f32[3,12,14,14]{3,2,1,0:T(8,128)S(1)} %get-tuple-element.64, bf16[14,3,14,12,64,1]{4,3,2,1,0,5:T(8,128)(2,1)S(1)} %bitcast.191), kind=kOutput, calls=%fused_computation.92 | convolution fusion | flops 181169856 | bytes 7394688 | tf_op jit(solution)/shard_map/nhrcsk,snkhd->rnchd/dot_general | solution.py:90
  232.5 15.9 %fusion.135 = (f32[3,12,7,14]{3,2,1,0:T(8,128)S(1)}, f32[3,12,7,14,14,14]{3,5,4,2,1,0:T(8,128)}) fusion(f32[3,12,7,14,14]{3,4,2,1,0:T(8,128)} %copy.117, bf16[14,3,14,12,64,1]{4,3,2,1,0,5:T(8,128)(2,1)} %get-tuple-element.80, bf16[7,3,14,12,64,1]{4,3,2,1,0,5:T(8,128)(2,1)S(1)} %bitcast.187, f32[3,12,7,14,14]{3,4,1,0,2:T(8,128)S(1)} %convolution_bitcast_fusion.3), kind=kOutput, calls=%fused_computation.221 | convolution fusion | flops 91272888 | bytes 4529952 | tf_op jit(solution)/shard_map/rnchd,snkhd->nhrcsk/dot_general | solution.py:58
  248.4 12.9 %fusion.7 = f32[3,12,7,14]{3,2,1,0:T(8,128)S(1)} fusion(f32[3,12,7,14,14,14]{3,5,4,2,1,0:T(8,128)} %get-tuple-element.67, f32[3,12,7,14]{3,2,1,0:T(8,128)S(1)} %get-tuple-element.66), kind=kLoop, calls=%fused_computation.23 | loop fusion | flops 1379448 | bytes 2794176 | tf_op jit(solution)/shard_map/reduce_sum | solution.py:86
  261.3 13.3 %fusion.62 = bf16[7,3,14,12,64]{4,2,0,3,1:T(8,128)(2,1)} fusion(f32[3,12,7,14,14,14]{3,5,4,2,1,0:T(8,128)} %get-tuple-element.67, f32[3,12,7,14]{3,2,1,0:T(8,128)S(1)} %fusion.7, f32[3,12,7,14]{3,2,1,0:T(8,128)S(1)} %get-tuple-element.66, bf16[14,3,14,12,64,1]{4,3,2,1,0,5:T(8,128)(2,1)S(1)} %copy-done.31), kind=kOutput, calls=%fused_computation.118 | convolution fusion | flops 90584928 | bytes 4148928 | tf_op jit(solution)/shard_map/nhrcsk,snkhd->rnchd/dot_general | solution.py:90
  286.5 31.6 %multiply_convert_fusion.2 = (bf16[882,3072]{1,0:T(8,128)(2,1)}, f32[882,3072]{1,0:T(8,128)}, f32[882,3072]{1,0:T(8,128)}) fusion(f32[3072]{0:T(1024)S(1)} %copy-done.83, bf16[768,3072]{1,0:T(8,128)(2,1)} %all-gather.9.cloned.1.call-done, f32[882,768]{1,0:T(8,128)S(1)} %get-tuple-element.69, f32[768]{0:T(1024)S(1)} %copy-done.73, f32[768]{0:T(1024)S(1)} %copy-done.71, ...), kind=kOutput, calls=%fused_computation.34 | convolution fusion | flops 4344012288 | bytes 34548624 | tf_op jit(solution)/shard_map/dot_general | solution.py:267
  318.1 16.1 %convert_reduce_fusion.4 = (f32[3072]{0:T(1024)}, bf16[882,3072]{1,0:T(8,128)(2,1)S(1)}) fusion(f32[882,3072]{1,0:T(8,128)} %get-tuple-element.53, bf16[3072,768]{1,0:T(8,128)(2,1)} %all-gather.11.cloned.1.call-done, f32[882,768]{1,0:T(8,128)} %reshape.356, f32[882]{0:T(1024)S(1)} %copy-done.53, f32[882,3072]{1,0:T(8,128)} %get-tuple-element.70, ...), kind=kOutput, calls=%fused_computation.32 | convolution fusion | flops 4209211392 | bytes 34551240 | tf_op jit(solution)/shard_map/dot_general | solution.py:39
  361.1 50.8 %multiply_reduce_fusion = (f32[3,12,14,14]{3,2,1,0:T(8,128)S(1)}, f32[3,12,14,14,14,14]{3,5,4,2,1,0:T(8,128)}) fusion(f32[3,12,14,14,14,14]{3,5,4,2,1,0:T(8,128)} %get-tuple-element.65, f32[3,12,14,14]{3,2,1,0:T(8,128)S(1)} %copy-done.38, bf16[14,3,14,12,64,1]{4,3,2,1,0,5:T(8,128)(2,1)S(1)} %bitcast.192, bf16[14,3,14,12,64,1]{4,3,2,1,0,5:T(8,128)(2,1)} %bitcast.193), kind=kOutput, calls=%fused_computation.3 | convolution fusion | flops 181162800 | bytes 12926592 | tf_op jit(solution)/shard_map/rnchd,snkhd->nhrcsk/dot_general | solution.py:105
  411.9 69.3 %convert_reduce_fusion.1 = (f32[3,12,14,14,14]{3,4,2,1,0:T(8,128)}, f32[3,12,14,14,14]{3,4,2,1,0:T(8,128)}, bf16[3,12,14,14,14,14]{3,5,4,2,1,0:T(8,128)(2,1)}, bf16[3,12,14,14,14,14]{3,5,4,2,1,0:T(8,128)(2,1)}) fusion(f32[3,12,14,14,14,14]{3,5,4,2,1,0:T(8,128)} %get-tuple-element.73, f32[3,12,14,14]{3,2,1,0:T(8,128)S(1)} %get-tuple-element.72, ...), kind=kLoop, calls=%fused_computation.1 | loop fusion | flops 10866240 | bytes 17442432 | tf_op jit(solution)/shard_map/reduce_sum | solution.py:120
  481.1 15.5 %fusion.57 = f32[3,12,64,14,14,1]{2,4,5,3,1,0:T(8,128)} fusion(bf16[3,12,14,14,14,14]{3,5,4,2,1,0:T(8,128)(2,1)} %get-tuple-element.49, bf16[14,3,14,12,64,1]{4,3,2,1,0,5:T(8,128)(2,1)} %bitcast.190), kind=kOutput, calls=%fused_computation.113 | convolution fusion | flops 177020928 | bytes 5475456 | tf_op jit(solution)/shard_map/nhrcsk,snkhd->rnchd/dot_general | solution.py:117
  496.7 15.0 %fusion.23 = bf16[14,3,14,12,64]{4,2,0,3,1:T(8,128)(2,1)} fusion(bf16[3,12,14,14,14,14]{3,5,4,2,1,0:T(8,128)(2,1)} %get-tuple-element.49, bf16[14,3,14,12,64,1]{4,3,2,1,0,5:T(8,128)(2,1)S(1)} %bitcast.186), kind=kOutput, calls=%fused_computation.54 | convolution fusion | flops 177924096 | bytes 4572288 | tf_op jit(solution)/shard_map/nhrcsk,rnchd->snkhd/dot_general | solution.py:114
  513.5 22.8 %multiply_reduce_fusion.1 = (f32[3,12,7,14]{3,2,1,0:T(8,128)S(1)}, f32[3,12,7,14,14,14]{3,5,4,2,1,0:T(8,128)}) fusion(f32[3,12,7,14,14,14]{3,5,4,2,1,0:T(8,128)} %get-tuple-element.67, f32[3,12,7,14]{3,2,1,0:T(8,128)S(1)} %copy-done.47, bf16[14,3,14,12,64,1]{4,3,2,1,0,5:T(8,128)(2,1)S(1)} %copy-done.32, bf16[7,3,14,12,64,1]{4,3,2,1,0,5:T(8,128)(2,1)} %bitcast.195), kind=kOutput, calls=%fused_computation.17 | convolution fusion | flops 90581400 | bytes 6914880 | tf_op jit(solution)/shard_map/rnchd,snkhd->nhrcsk/dot_general | solution.py:105
  536.3 36.6 %convert_reduce_fusion.2 = (f32[3,12,7,14,14]{3,4,2,1,0:T(8,128)}, f32[3,12,7,14,14]{3,4,2,1,0:T(8,128)S(1)}, bf16[3,12,7,14,14,14]{3,5,4,2,1,0:T(8,128)(2,1)}, bf16[3,12,7,14,14,14]{3,5,4,2,1,0:T(8,128)(2,1)}) fusion(f32[3,12,7,14,14,14]{3,5,4,2,1,0:T(8,128)} %get-tuple-element.75, f32[3,12,7,14]{3,2,1,0:T(8,128)S(1)} %get-tuple-element.74, ...), kind=kLoop, calls=%fused_computation.10 | loop fusion | flops 5433120 | bytes 8721216 | tf_op jit(solution)/shard_map/reduce_sum | solution.py:121
  587.1 11.5 %fusion.22 = f32[14,3,14,12,64]{4,2,0,3,1:T(8,128)} fusion(bf16[3,12,7,14,14,14]{3,5,4,2,1,0:T(8,128)(2,1)} %get-tuple-element.48, bf16[7,3,14,12,64,1]{4,3,2,1,0,5:T(8,128)(2,1)S(1)} %bitcast.188), kind=kOutput, calls=%fused_computation.52 | convolution fusion | flops 88962048 | bytes 3640896 | tf_op jit(solution)/shard_map/nhrcsk,rnchd->snkhd/dot_general | solution.py:114
  612.1 11.3 fusion.32
  637.3 14.5 %fusion.37 = bf16[14,3,14,12,64]{4,2,0,3,1:T(8,128)(2,1)} fusion(bf16[3,12,14,14,14,14]{3,5,4,2,1,0:T(8,128)(2,1)} %get-tuple-element.54, bf16[14,3,14,12,64,1]{4,3,2,1,0,5:T(8,128)(2,1)S(1)} %bitcast.194), kind=kOutput, calls=%fused_computation.89 | convolution fusion | flops 177020928 | bytes 4572288 | tf_op jit(solution)/shard_map/nhrcsk,rnchd->snkhd/dot_general | solution.py:111
  669.4 10.5 bitcast_add_fusion.2
  731.8 10.6 fusion.124
  742.5 10.6 fusion.122
  802.9 42.4 %all-reduce.16 = (f32[768]{0:T(1024)S(1)}, f32[768]{0:T(1024)S(1)}, f32[1536]{0:T(1024)S(1)}, f32[27,64]{1,0:T(8,128)}, f32[27,64]{1,0:T(8,128)}, /*index=5*/f32...) all-reduce(f32[768]{0:T(1024)S(1)} %get-tuple-element.20, ...), channel_id=2, replica_groups=mesh['img'=2,'rows'=16] {'img','rows'}, use_global_device_ids=true, to_apply=%region_19.20.clone | all-reduce | flops 12672 | bytes 101376
  855.5 134.8 %reduce-scatter.9.cloned.1.call-done = f32[24,3072]{1,0:T(8,128)} async-done(((f32[768,3072]{1,0:T(8,128)}), f32[24,3072]{1,0:T(8,128)}) %reduce-scatter.9.cloned.1.call-update) | async-done | bytes 294928 | tf_op jit(solution)/shard_map/reduce_scatter | solution.py:365
  990.3 142.1 %reduce-scatter.11.cloned.1.call-done = f32[96,768]{1,0:T(8,128)} async-done(((f32[3072,768]{1,0:T(8,128)}), f32[96,768]{1,0:T(8,128)}) %reduce-scatter.11.cloned.1.call-update) | async-done | bytes 294928 | tf_op jit(solution)/shard_map/reduce_scatter | solution.py:367
  (390 shorter events, 324.5 us)
Async XLA Ops:
  7.2 57.6 %copy-start = (bf16[27,64]{1,0:T(8,128)(2,1)S(1)}, bf16[27,64]{1,0:T(8,128)(2,1)}, u32[]{:S(2)}) copy-start(bf16[27,64]{1,0:T(8,128)(2,1)} %param.23) | copy-start | bytes 10372
  7.2 66.9 %all-gather.5.cloned.1.call-start = ((), (), s32[]{:S(2)}) async-start(), calls=%async_computation.4 | async-start | bytes 3649536 | tf_op jit(solution)/shard_map/all_gather | solution.py:195
  7.9 273.1 %all-gather.7.cloned.1.call-start = ((), (), s32[]{:S(2)}) async-start(), calls=%async_computation.5 | async-start | bytes 1216512 | tf_op jit(solution)/shard_map/all_gather | solution.py:197
  8.7 277.8 %all-gather.9.cloned.1.call-start = ((), (), s32[]{:S(2)}) async-start(), calls=%async_computation.6 | async-start | bytes 4866048 | tf_op jit(solution)/shard_map/all_gather | solution.py:201
  9.4 308.7 %all-gather.11.cloned.1.call-start = ((), (), s32[]{:S(2)}) async-start(), calls=%async_computation.7 | async-start | bytes 4866048 | tf_op jit(solution)/shard_map/all_gather | solution.py:203
  10.0 845.5 %reduce-scatter.7.cloned.1.call-start = ((), (), s32[]{:S(2)}) async-start(), calls=%async_computation.9 | async-start | bytes 2433024 | tf_op jit(solution)/shard_map/reduce_scatter | solution.py:361
  10.1 55.1 %copy-start.65 = (s32[14,14]{1,0:T(8,128)}, s32[14,14]{1,0:T(8,128)S(1)}, u32[]{:S(2)}) copy-start(s32[14,14]{1,0:T(8,128)S(1)} %subtract_add_fusion) | copy-start | bytes 2356
  11.9 62.2 %copy-start.63 = (f32[882]{0:T(1024)}, f32[882]{0:T(1024)S(1)}, u32[]{:S(2)}) copy-start(f32[882]{0:T(1024)S(1)} %div.68) | copy-start | bytes 10588
  12.6 52.6 %copy-start.84 = (bf16[27,64]{1,0:T(8,128)(2,1)S(1)}, bf16[27,64]{1,0:T(8,128)(2,1)}, u32[]{:S(2)}) copy-start(bf16[27,64]{1,0:T(8,128)(2,1)} %param.24) | copy-start | bytes 10372
  15.0 64.9 %copy-start.16 = (f32[882,768]{1,0:T(8,128)}, f32[882,768]{1,0:T(8,128)S(1)}, u32[]{:S(2)}) copy-start(f32[882,768]{1,0:T(8,128)S(1)} %reshape.355) | copy-start | bytes 8128516
  16.5 63.4 %copy-start.75 = (s32[7,14]{1,0:T(8,128)}, s32[7,14]{1,0:T(8,128)S(1)}, u32[]{:S(2)}) copy-start(s32[7,14]{1,0:T(8,128)S(1)} %subtract_add_fusion.1) | copy-start | bytes 1180
  65.0 153.3 %copy-start.50 = (f32[7,14,64]{2,1,0:T(8,128)}, f32[7,14,64]{2,1,0:T(8,128)S(1)}, u32[]{:S(2)}) copy-start(f32[7,14,64]{2,1,0:T(8,128)S(1)} %fusion.106) | copy-start | bytes 75268
  65.3 59.0 %copy-start.48 = (f32[14,14,64]{2,1,0:T(8,128)}, f32[14,14,64]{2,1,0:T(8,128)S(1)}, u32[]{:S(2)}) copy-start(f32[14,14,64]{2,1,0:T(8,128)S(1)} %fusion.100) | copy-start | bytes 150532
  90.5 132.9 %collective-permute-start = (bf16[7,42,768]{2,1,0:T(8,128)(2,1)}, bf16[7,42,768]{2,1,0:T(8,128)(2,1)}, u32[]{:S(2)}, u32[]{:S(2)}) collective-permute-start(bf16[7,42,768]{2,1,0:T(8,128)(2,1)} %constant_dynamic-slice_fusion.4), channel_id=1, source_target_pairs={{0,1},{1,0},{2,3},{3,2},{4,5},{5,4},{6,7},{7,6},{8,9},{9,8},{10,11... | collective-permute-start | bytes 1354760 | tf_op jit(solution)/shard_map/ppermute | solution.py:22
  91.7 129.2 %collective-permute-start.1 = (bf16[7,42,768]{2,1,0:T(8,128)(2,1)}, bf16[7,42,768]{2,1,0:T(8,128)(2,1)}, u32[]{:S(2)}, u32[]{:S(2)}) collective-permute-start(bf16[7,42,768]{2,1,0:T(8,128)(2,1)} %constant_dynamic-slice_fusion.2), channel_id=1, source_target_pairs={{0,1},{1,0},{2,3},{3,2},{4,5},{5,4},{6,7},{7,6},{8,9},{9,8},{10,11... | collective-permute-start | bytes 1354760 | tf_op jit(solution)/shard_map/ppermute | solution.py:22
  284.9 59.2 %copy-start.10 = (f32[882,768]{1,0:T(8,128)}, f32[882,768]{1,0:T(8,128)S(1)}, u32[]{:S(2)}) copy-start(f32[882,768]{1,0:T(8,128)S(1)} %get-tuple-element.69) | copy-start | bytes 8128516
  285.0 59.2 %copy-start.55 = (f32[882]{0:T(1024)}, f32[882]{0:T(1024)S(1)}, u32[]{:S(2)}) copy-start(f32[882]{0:T(1024)S(1)} %broadcast_multiply_fusion.1) | copy-start | bytes 10588
  285.5 58.7 %copy-start.57 = (f32[882]{0:T(1024)}, f32[882]{0:T(1024)S(1)}, u32[]{:S(2)}) copy-start(f32[882]{0:T(1024)S(1)} %fusion.121) | copy-start | bytes 10588
  511.7 343.8 %reduce-scatter.5.cloned.1.call-start = ((), (), s32[]{:S(2)}) async-start(), calls=%async_computation.8 | async-start | bytes 7299072 | tf_op jit(solution)/shard_map/reduce_scatter | solution.py:359
  610.2 104.5 %collective-permute-start.2 = (bf16[7,42,768]{2,1,0:T(8,128)(2,1)}, bf16[7,42,768]{2,1,0:T(8,128)(2,1)}, u32[]{:S(2)}, u32[]{:S(2)}) collective-permute-start(bf16[7,42,768]{2,1,0:T(8,128)(2,1)} %dynamic-slice_convert_fusion.1), channel_id=1, source_target_pairs={{0,1},{1,0},{2,3},{3,2},{4,5},{5,4},{6,7},{7,6},{8,9},{9,8},{10,11... | collective-permute-start | bytes 1354760 | tf_op jit(solution)/shard_map/ppermute | solution.py:22
  637.3 72.3 %collective-permute-start.3 = (bf16[7,42,768]{2,1,0:T(8,128)(2,1)}, bf16[7,42,768]{2,1,0:T(8,128)(2,1)}, u32[]{:S(2)}, u32[]{:S(2)}) collective-permute-start(bf16[7,42,768]{2,1,0:T(8,128)(2,1)} %dynamic-slice_convert_fusion), channel_id=1, source_target_pairs={{0,1},{1,0},{2,3},{3,2},{4,5},{5,4},{6,7},{7,6},{8,9},{9,8},{10,11... | collective-permute-start | bytes 1354760 | tf_op jit(solution)/shard_map/ppermute | solution.py:22
  730.0 260.2 %reduce-scatter.9.cloned.1.call-start = ((), (), s32[]{:S(2)}) async-start(), calls=%async_computation.10 | async-start | bytes 9732096 | tf_op jit(solution)/shard_map/reduce_scatter | solution.py:365
  742.4 389.9 %reduce-scatter.11.cloned.1.call-start = ((), (), s32[]{:S(2)}) async-start(), calls=%async_computation.11 | async-start | bytes 9732096 | tf_op jit(solution)/shard_map/reduce_scatter | solution.py:367
  852.2 280.2 %copy-start.1 = (bf16[27,64]{1,0:T(8,128)(2,1)S(1)}, bf16[27,64]{1,0:T(8,128)(2,1)}, u32[]{:S(2)}) copy-start(bf16[27,64]{1,0:T(8,128)(2,1)} %param.23) | copy-start | bytes 10372
  (87 other events, 648.1 us)
Sparse Core Ops, SparseCore 0:
  10.9 63.1 all-gather.4
  77.0 53.5 all-gather.6
  133.5 62.4 all-gather.8
  198.8 62.3 all-gather.10
  511.8 98.5 reduce-scatter.6
  730.2 118.7 reduce-scatter.4
  855.4 134.8 reduce-scatter.8
  997.8 134.5 reduce-scatter.10
where the time goes:
time: 1150 us; the launch traced here: 1140 us
  matrix products  416 us (36%)
  waiting for transfers between devices  285 us (25%)
  local copies, waits for them, and re-layouts  167 us (15%)
  other arithmetic  167 us (15%)
  blocking collectives  85.5 us (7%)
  between operations  15.6 us (1%)
    reduce_scatter x1, waiting for transfers between devices, local(): lax.psum_scatter(reduce_weight_grad, ('img', 'rows'), scatter_dimension=0...  142 us
    reduce_scatter x1, waiting for transfers between devices, local(): lax.psum_scatter(expand_weight_grad, ('img', 'rows'), scatter_dimension=0...  135 us
    unnamed x2, blocking collectives  85.5 us
    dot_general x2, matrix products, band_backward(): jnp.einsum('rnchd,snkhd->nhrcsk', grad_five, value_five, preferred_elemen...  73.6 us
    reduce_sum x1, other arithmetic, band_backward(): row_sums = jnp.sum(grad_round, axis=5, dtype=jnp.float32)  69.3 us
    dot_general x2, matrix products, band_scores(): jnp.einsum('rnchd,snkhd->nhrcsk', query_five, key_five, preferred_element...  42.2 us
    reduce_sum x1, other arithmetic, band_backward(): col_sums = jnp.sum(grad_round, axis=4, dtype=jnp.float32)  36.6 us
    dot_general x2, matrix products, band_forward(): jnp.einsum('nhrcsk,snkhd->rnchd', probs_six, value_five, preferred_elemen...  36.3 us
  transfers between devices with their start and end apart: 12, of which 3 were waited for; matrix products, arithmetic and copies ran while one was open for 48% of the time, Pallas kernels for 0%

commit v1 on v0

v1 whole, which is shorter than its diff:
```python
from functools import partial

import jax
import jax.numpy as jnp
import numpy as np
from jax import lax
from jax.experimental import pallas as pl
from jax.experimental.pallas import tpu as pltpu
from jax.sharding import PartitionSpec as P

HEADS = 12
HEAD_DIM = 64
WIN = 14
REAL = 32
KEYS = 208
BF = jnp.bfloat16
F32 = jnp.float32
VMEM_LIMIT = 60 * 2**20

SEGMENTS = []
_offset = 0
for _row, _rows in ((0, WIN), (WIN, REAL - 2 * WIN)):
    for _col, _cols in ((0, WIN), (WIN, WIN), (2 * WIN, REAL - 2 * WIN)):
        _padded = -(-_rows * _cols // 16) * 16
        SEGMENTS.append((_row, _rows, _col, _cols, _padded, _offset))
        _offset += _padded
TOKENS = _offset
BAND = REAL - WIN


def window_constants():
    band_row = np.full((TOKENS,), 0, np.int32)
    column = np.full((TOKENS,), 0, np.int32)
    valid = np.zeros((TOKENS,), np.int32)
    along = np.zeros((TOKENS,), np.int32)
    across = np.zeros((TOKENS,), np.int32)
    onehots = np.zeros((len(SEGMENTS), KEYS, 128), np.float32)
    for number, (row, rows, col, cols, padded, offset) in enumerate(SEGMENTS):
        spots = [(a, b) for a in range(rows) for b in range(cols)]
        for place, (a, b) in enumerate(spots):
            band_row[offset + place] = row + a
            column[offset + place] = col + b
            valid[offset + place] = 1
            along[offset + place] = a
            across[offset + place] = b
        rest = [(s, t) for s in range(WIN) for t in range(WIN) if s >= rows or t >= cols]
        slots = spots + [None] * (padded - len(spots)) + rest
        slots = slots + [None] * (KEYS - len(slots))
        for place, spot in enumerate(slots):
            for head in range(2):
                if spot is None:
                    onehots[number, place, 32 * head + 15] = -1e30
                else:
                    for part in range(2):
                        onehots[number, place, 32 * head + 16 * part + spot[0]] = 1
                        onehots[number, place, 64 + 32 * head + 16 * part + spot[1]] = 1
    return band_row, column, valid, along, across, onehots


BAND_ROW, COLUMN, VALID, ALONG, ACROSS, ONEHOTS = window_constants()


def shift_amounts():
    amounts = np.zeros((TOKENS, 128), np.int32)
    amounts[:, :64] = (WIN - 1 - ALONG)[:, None]
    amounts[:, 64:] = (WIN - 1 - ACROSS)[:, None]
    return amounts


SHIFTS = shift_amounts()


def dot_t(left, right):
    return lax.dot_general(left, right, (((1,), (1,)), ((), ())), preferred_element_type=F32)


def dot_f(left, right):
    return lax.dot_general(left, right, (((0,), (0,)), ((), ())), preferred_element_type=F32)


def dot_n(left, right):
    return lax.dot_general(left, right, (((1,), (0,)), ((), ())), preferred_element_type=F32)


def lanes_of(shape):
    return lax.broadcasted_iota(jnp.int32, shape, len(shape) - 1)


def relative_features(queries, table, shifts):
    terms = dot_n(queries, table)
    for bit in range(4):
        rolled = pltpu.roll(terms, 128 - (1 << bit), 1)
        terms = jnp.where((shifts & (1 << bit)) != 0, rolled, terms)
    high = terms.astype(BF).astype(F32)
    low = pltpu.roll(terms - high, 16, 1)
    lane = lanes_of(terms.shape) & 31
    mixed = jnp.where(lane < WIN, high, jnp.where((lane >= 16) & (lane < 16 + WIN), low, 0.0))
    return jnp.where(lane == 15, 1.0, mixed).astype(BF)


def stacked_queries(queries, features, start, count):
    lane = lanes_of((count, 128))
    first = lane < 64
    even = (lane & 32) == 0
    part = queries[start : start + count] * jnp.asarray(0.125, BF)
    extra = features[start : start + count]
    zero = jnp.zeros_like(part)
    top = jnp.concatenate([jnp.where(first, part, zero), jnp.where(even, extra, zero)], 1)
    low = jnp.concatenate([jnp.where(first, zero, part), jnp.where(even, zero, extra)], 1)
    return jnp.concatenate([top, low], 0)


def window_keys(array, start, count, fill):
    if count == KEYS:
        return array[start : start + count]
    rest = jnp.broadcast_to(fill, (KEYS - count, 128)).astype(BF)
    return jnp.concatenate([array[start : start + count], rest], 0)


def tiles_of(total):
    return [(begin, min(128, total - begin)) for begin in range(0, total, 128)]


def attend_kernel(q_ref, k_ref, v_ref, fill_ref, table_ref, shifts_ref, onehots_ref, mixed_ref, lse_ref):
    queries = q_ref[...]
    features = relative_features(queries, table_ref[...], shifts_ref[...])
    keys, values = k_ref[...], v_ref[...]
    fill = fill_ref[...]
    base = 0
    for number, (_, _, _, _, count, start) in enumerate(SEGMENTS):
        left = stacked_queries(queries, features, start, count)
        right = jnp.concatenate(
            [window_keys(keys, start, count, jnp.zeros((1, 128), BF)), onehots_ref[number]], 1
        )
        held = window_keys(values, start, count, fill)
        outs = []
        for begin, size in tiles_of(2 * count):
            scores = dot_t(right, left[begin : begin + size])
            top = jnp.max(scores, axis=0, keepdims=True)
            weights = jnp.exp(scores - top)
            total = jnp.sum(weights, axis=0, keepdims=True)
            lse_ref[0, 0:1, base + begin : base + begin + size] = top + jnp.log(total)
            out = dot_f(held, weights.astype(BF)) * (1.0 / total)
            outs.append(out.T)
        both = jnp.concatenate(outs, 0)
        lane = lanes_of((count, 128))
        mixed = jnp.where(lane < 64, both[:count], both[count:])
        mixed_ref[start : start + count, :] = mixed.astype(BF)
        base += -(-2 * count // 128) * 128


LSE = sum(-(-2 * segment[4] // 128) * 128 for segment in SEGMENTS)


def attend_back_kernel(
    q_ref, k_ref, v_ref, g_ref, lse_ref, fill_ref, table_ref, shifts_ref, onehots_ref,
    dq_ref, dk_ref, dv_ref, dtable_ref, dbias_ref, probs_ref, dscores_ref, slots_ref,
):
    queries = q_ref[...]
    shifts = shifts_ref[...]
    table = table_ref[...]
    features = relative_features(queries, table, shifts)
    keys, values, grads = k_ref[...], v_ref[...], g_ref[...]
    fill = fill_ref[...]
    base = 0
    bias_sum = jnp.zeros((1, 128), F32)
    for number, (_, _, _, _, count, start) in enumerate(SEGMENTS):
        left = stacked_queries(queries, features, start, count)
        right = jnp.concatenate(
            [window_keys(keys, start, count, jnp.zeros((1, 128), BF)), onehots_ref[number]], 1
        )
        held = window_keys(values, start, count, fill)
        lane = lanes_of((count, 128))
        first = lane < 64
        part = grads[start : start + count]
        zero = jnp.zeros_like(part)
        pulls = jnp.concatenate([jnp.where(first, part, zero), jnp.where(first, zero, part)], 0)
        for begin, size in tiles_of(2 * count):
            scores = dot_t(right, left[begin : begin + size])
            probs = jnp.exp(scores - lse_ref[0, 0:1, base + begin : base + begin + size])
            dprobs = dot_t(held, pulls[begin : begin + size])
            product = probs * dprobs
            delta = jnp.sum(product, axis=0, keepdims=True)
            probs_ref[:, begin : begin + size] = probs.astype(BF)
            dscores_ref[:, begin : begin + size] = (product - probs * delta).astype(BF)
        dscores = dscores_ref[:, : 2 * count]
        dvalues = dot_n(probs_ref[:, : 2 * count], pulls)
        dkeys = dot_n(dscores, left[:, :128])
        dv_ref[start : start + count, :] = dvalues[:count].astype(BF)
        dk_ref[start : start + count, :] = dkeys[:count].astype(BF)
        bias_sum = bias_sum + jnp.sum(dvalues, axis=0, keepdims=True)
        both = dot_f(dscores, right)
        dq = jnp.where(first, both[:count, :128], both[count:, :128]) * 0.125
        even = (lane & 32) == 0
        extra = jnp.where(even, both[:count, 128:], both[count:, 128:])
        slots = jnp.where((lane & 31) < WIN, extra, 0.0)
        amounts = shifts[start : start + count]
        for bit in range(4):
            rolled = pltpu.roll(slots, 1 << bit, 1)
            slots = jnp.where((amounts & (1 << bit)) != 0, rolled, slots)
        high = slots.astype(BF)
        low = (slots - high.astype(F32)).astype(BF)
        slots_ref[start : start + count, :128] = high
        slots_ref[start : start + count, 128:] = low
        dq = dq + dot_t(jnp.concatenate([high, low], 1), jnp.concatenate([table, table], 1))
        dq_ref[start : start + count, :] = dq.astype(BF)
        base += -(-2 * count // 128) * 128
    found = dot_f(slots_ref[...], queries)
    dtable_ref[0] = found[:128] + found[128:]
    dbias_ref[...] = bias_sum


def whole(shape):
    return pl.BlockSpec(shape, lambda step: (0,) * len(shape))


def column(offset, rows=TOKENS):
    return pl.BlockSpec((rows, 128), lambda step: (0, offset + step))


def reversed_table(height_table, width_table):
    slots = height_table.shape[0]
    pad = ((0, 0), (0, 32 - slots))
    height = jnp.pad(height_table[::-1].T, pad)
    width = jnp.pad(width_table[::-1].T, pad)
    none = jnp.zeros_like(height)
    top = jnp.concatenate([height, none, width, none], 1)
    low = jnp.concatenate([none, height, none, width], 1)
    return jnp.concatenate([top, low], 0)


def attend(joint, fill, table):
    pairs = HEADS // 2
    return pl.pallas_call(
        attend_kernel,
        grid=(pairs,),
        in_specs=[
            column(0), column(pairs), column(2 * pairs), column(0, 1),
            whole((128, 128)), whole((TOKENS, 128)), whole((len(SEGMENTS), KEYS, 128)),
        ],
        out_specs=[column(0), pl.BlockSpec((1, 8, LSE), lambda step: (step, 0, 0))],
        out_shape=[
            jax.ShapeDtypeStruct((TOKENS, pairs * 128), BF),
            jax.ShapeDtypeStruct((pairs, 8, LSE), F32),
        ],
        compiler_params=pltpu.CompilerParams(vmem_limit_bytes=VMEM_LIMIT),
        name="attend",
    )(joint, joint, joint, fill, table, jnp.asarray(SHIFTS), jnp.asarray(ONEHOTS, BF))


def attend_back(joint, grad_mixed, lse, fill, table):
    pairs = HEADS // 2
    wide = jax.ShapeDtypeStruct((TOKENS, pairs * 128), BF)
    return pl.pallas_call(
        attend_back_kernel,
        grid=(pairs,),
        in_specs=[
            column(0), column(pairs), column(2 * pairs), column(0),
            pl.BlockSpec((1, 8, LSE), lambda step: (step, 0, 0)), column(0, 1),
            whole((128, 128)), whole((TOKENS, 128)), whole((len(SEGMENTS), KEYS, 128)),
        ],
        out_specs=[
            column(0), column(0), column(0),
            pl.BlockSpec((1, 128, 128), lambda step: (step, 0, 0)), column(0, 1),
        ],
        out_shape=[
            wide, wide, wide,
            jax.ShapeDtypeStruct((pairs, 128, 128), F32),
            jax.ShapeDtypeStruct((1, pairs * 128), F32),
        ],
        scratch_shapes=[
            pltpu.VMEM((KEYS, 512), BF), pltpu.VMEM((KEYS, 512), BF), pltpu.VMEM((TOKENS, 256), BF),
        ],
        compiler_params=pltpu.CompilerParams(vmem_limit_bytes=VMEM_LIMIT),
        name="attend_back",
    )(joint, joint, joint, grad_mixed, lse, fill, table, jnp.asarray(SHIFTS), jnp.asarray(ONEHOTS, BF))


def table_grads(found, slots):
    total = jnp.sum(found, axis=0)
    height = total[0:32, :64] + total[32:64, 64:]
    width = total[64:96, :64] + total[96:128, 64:]
    return height[:slots][::-1], width[:slots][::-1]


def pack_kernel(parity_ref, own_ref, far_ref, out_ref, stage_ref):
    parity = parity_ref[0]
    moved = far_ref.shape[0]
    stage_ref[...] = jnp.zeros_like(stage_ref)
    for row in range(BAND):
        if row < moved:
            line = jnp.where(parity == 0, own_ref[row, :REAL], far_ref[row]).astype(F32)
        else:
            line = own_ref[row - moved * parity, :REAL].astype(F32)
        for first, rows, col, cols, _, offset in SEGMENTS:
            if first <= row < first + rows:
                place = offset + (row - first) * cols
                stage_ref[place : place + cols, :] = line[col : col + cols]
    out_ref[...] = stage_ref[...].astype(out_ref.dtype)


def pack(parity, own, far):
    width = own.shape[2]
    return pl.pallas_call(
        pack_kernel,
        in_specs=[
            pl.BlockSpec(memory_space=pltpu.SMEM),
            pl.BlockSpec(memory_space=pltpu.VMEM),
            pl.BlockSpec(memory_space=pltpu.VMEM),
        ],
        out_specs=pl.BlockSpec(memory_space=pltpu.VMEM),
        out_shape=jax.ShapeDtypeStruct((TOKENS, width), BF),
        scratch_shapes=[pltpu.VMEM((TOKENS, width), F32)],
        compiler_params=pltpu.CompilerParams(vmem_limit_bytes=VMEM_LIMIT),
        name="pack",
    )(parity.reshape(1), own, far)


def unpack_kernel(parity_ref, win_ref, far_ref, out_ref, wide_ref, stage_ref):
    parity = parity_ref[0]
    moved = far_ref.shape[0]
    wide_ref[...] = win_ref[...].astype(F32)
    for row in range(BAND):
        for first, rows, col, cols, _, offset in SEGMENTS:
            if first <= row < first + rows:
                place = offset + (row - first) * cols
                stage_ref[row, col : col + cols, :] = wide_ref[place : place + cols, :]
    out_ref[...] = jnp.zeros_like(out_ref)
    for row in range(out_ref.shape[0]):
        near = stage_ref[row] if row < WIN else far_ref[row - WIN].astype(F32)
        other = stage_ref[row + moved] if row + moved < BAND else jnp.zeros_like(near)
        out_ref[row, :REAL, :] = jnp.where(parity == 0, near, other).astype(out_ref.dtype)


def unpack(parity, win, far, shape):
    width = win.shape[1]
    return pl.pallas_call(
        unpack_kernel,
        in_specs=[
            pl.BlockSpec(memory_space=pltpu.SMEM),
            pl.BlockSpec(memory_space=pltpu.VMEM),
            pl.BlockSpec(memory_space=pltpu.VMEM),
        ],
        out_specs=pl.BlockSpec(memory_space=pltpu.VMEM),
        out_shape=jax.ShapeDtypeStruct(shape, BF),
        scratch_shapes=[pltpu.VMEM((TOKENS, width), F32), pltpu.VMEM((BAND, REAL, width), F32)],
        compiler_params=pltpu.CompilerParams(vmem_limit_bytes=VMEM_LIMIT),
        name="unpack",
    )(parity.reshape(1), win, far)


def send_rows_kernel(win_ref, out_ref, wide_ref, stage_ref):
    wide_ref[...] = win_ref[...].astype(F32)
    for row in range(out_ref.shape[0]):
        for first, rows, col, cols, _, offset in SEGMENTS:
            if first <= row < first + rows:
                place = offset + (row - first) * cols
                stage_ref[row, col : col + cols, :] = wide_ref[place : place + cols, :]
    out_ref[...] = stage_ref[...].astype(out_ref.dtype)


def send_rows(win, moved):
    width = win.shape[1]
    return pl.pallas_call(
        send_rows_kernel,
        in_specs=[pl.BlockSpec(memory_space=pltpu.VMEM)],
        out_specs=pl.BlockSpec(memory_space=pltpu.VMEM),
        out_shape=jax.ShapeDtypeStruct((moved, REAL, width), BF),
        scratch_shapes=[pltpu.VMEM((TOKENS, width), F32), pltpu.VMEM((moved, REAL, width), F32)],
        compiler_params=pltpu.CompilerParams(vmem_limit_bytes=VMEM_LIMIT),
        name="send_rows",
    )(win)


def rows_place():
    me = lax.axis_index("rows")
    return me % 2, me // 2 % 2, me // 4


def swap_rows(block, bit):
    count = lax.axis_size("rows")
    return lax.ppermute(block, "rows", [(place, place ^ (1 << bit)) for place in range(count)])


def swap_img(block):
    return lax.ppermute(block, "img", [(0, 1), (1, 0)])


def shift_depth(block, step):
    count = lax.axis_size("rows")
    return lax.ppermute(
        block, "rows", [(place, (place + 4 * step) % count) for place in range(count)]
    )


def in_order(bit, mine, other, axis):
    return jnp.where(
        bit == 0, jnp.stack([mine, other], axis), jnp.stack([other, mine], axis)
    )


def gather_depth(block):
    depth = lax.axis_size("rows") // 4
    place = rows_place()[2]
    parts = [block] + [shift_depth(block, step) for step in range(1, depth)]
    turned = [parts[-step % depth] for step in range(depth)]
    twice = jnp.stack(turned + turned)
    return lax.dynamic_slice_in_dim(twice, depth - place, depth, 0)


def halves(block):
    cut = block.shape[-1] // 256 * 128
    return block[..., :cut], block[..., cut:]


def gather_blocks(block):
    x, y, _ = rows_place()
    first, second = halves(gather_depth(block))
    first = in_order(x, first, swap_rows(first, 0), 1)
    second = in_order(y, second, swap_rows(second, 1), 1)
    first = in_order(y, first, swap_rows(first, 1), 1)
    second = in_order(x, second, swap_rows(second, 0), 2)
    full = jnp.concatenate([first, second], -1).reshape(-1, block.shape[-1])
    other = swap_img(full)
    both = in_order(lax.axis_index("img"), full, other, 0)
    return both.reshape(-1, block.shape[-1])


def pick(array, place, axis):
    return lax.dynamic_index_in_dim(array, place, axis, keepdims=False)


def fold(block, place, axis, send):
    given = pick(block, 1 - place, axis).astype(BF)
    kept = pick(block, place, axis).astype(F32)
    return (kept + send(given).astype(F32)).astype(BF)


def scatter_blocks(total):
    x, y, z = rows_place()
    count = lax.axis_size("rows")
    depth = count // 4
    columns = total.shape[-1]
    block = fold(total.reshape(2, -1, columns), lax.axis_index("img"), 0, swap_img)
    block = block.reshape(depth, 2, 2, -1, columns)
    first, second = halves(block)
    first = fold(first, x, 2, lambda part: swap_rows(part, 0))
    second = fold(second, y, 1, lambda part: swap_rows(part, 1))
    first = fold(first, y, 1, lambda part: swap_rows(part, 1))
    second = fold(second, x, 1, lambda part: swap_rows(part, 0))
    block = jnp.concatenate([first, second], -1)
    result = pick(block, z, 0).astype(F32)
    for step in range(1, depth):
        given = pick(block, (z + step) % depth, 0)
        result = result + shift_depth(given, step).astype(F32)
    return result


def sum_all(value):
    value = value + swap_img(value)
    value = value + swap_rows(value, 0)
    value = value + swap_rows(value, 1)
    return jnp.sum(gather_depth(value), axis=0)


def layer_norm(value, gain, bias):
    center = jnp.mean(value, axis=-1, keepdims=True)
    centred = value - center
    variance = jnp.mean(centred * centred, axis=-1, keepdims=True)
    return centred * lax.rsqrt(variance + 1e-06) * gain + bias


def to_odd(block):
    count = lax.axis_size("rows")
    return lax.ppermute(block, "rows", [(place, place + 1) for place in range(0, count, 2)])


def to_even(block):
    count = lax.axis_size("rows")
    return lax.ppermute(block, "rows", [(place + 1, place) for place in range(0, count, 2)])


def local(
    tokens,
    extent,
    pre_gain,
    pre_bias,
    triple_weight,
    triple_bias,
    height_table,
    width_table,
    output_weight,
    output_bias,
    post_gain,
    post_bias,
    expand_weight,
    expand_bias,
    reduce_weight,
    reduce_bias,
    cotangent,
):
    rows_dev, _, width = tokens.shape
    moved = rows_dev - WIN
    block = pre_gain.shape[0]
    parity = lax.axis_index("rows") % 2
    image = lax.axis_index("img") * (lax.axis_size("rows") // 2) + lax.axis_index("rows") // 2
    sides = lax.dynamic_slice(extent, (image, 0), (1, 2))

    vectors = [
        vector.reshape(block, -1)
        for vector in (
            pre_gain, pre_bias, triple_bias, output_bias, post_gain, post_bias, expand_bias, reduce_bias,
        )
    ]
    counts = [vector.shape[1] for vector in vectors]
    vectors = jnp.pad(jnp.concatenate(vectors, 1), ((0, 0), (0, 128 - sum(counts))))
    first_all = gather_blocks(jnp.concatenate([triple_weight, vectors], 1))
    triple_all, vectors_all = first_all[:, : 3 * width], first_all[:, 3 * width :]
    second_all = gather_blocks(jnp.concatenate([output_weight, expand_weight], 1))
    output_all, expand_all = second_all[:, :width], second_all[:, width:]
    reduce_all = gather_blocks(reduce_weight)

    spread = []
    begin = 0
    for count in counts:
        spread.append(vectors_all[:, begin : begin + count].reshape(-1).astype(F32))
        begin += count
    (
        pre_gain_all, pre_bias_all, triple_bias_all, output_bias_all, post_gain_all, post_bias_all,
        expand_bias_all, reduce_bias_all,
    ) = spread

    far_tokens = to_odd(tokens[WIN:, :REAL])
    far_pulls = to_odd(cotangent[WIN:, :REAL])
    flat = pack(parity, tokens, far_tokens).astype(F32)
    pulls = pack(parity, cotangent, far_pulls).astype(F32)
    band_row, column_of = jnp.asarray(BAND_ROW), jnp.asarray(COLUMN)
    real_row = jnp.where(parity == 0, band_row, band_row + WIN)
    inside = (real_row < sides[0, 0]) & (column_of < sides[0, 1]) & (jnp.asarray(VALID) == 1)
    inside = inside & ((parity == 1) | (band_row < WIN))
    mask = inside.astype(F32)[:, None]

    normed, pre_back = jax.vjp(layer_norm, flat, pre_gain_all, pre_bias_all)
    entry = (mask * normed).astype(BF)
    added = jnp.concatenate([triple_bias_all[:width], jnp.zeros((width,), F32), triple_bias_all[width:]])
    joint = (dot_n(entry, triple_all) + added).astype(BF)
    table = reversed_table(height_table, width_table)
    fill = triple_bias_all[None, width:].astype(BF)
    mixed, lse = attend(joint, fill, table)
    branch = dot_n(mixed, output_all) + output_bias_all
    middle = flat + mask * branch
    normed_two, post_back = jax.vjp(layer_norm, middle, post_gain_all, post_bias_all)
    entry_two = normed_two.astype(BF)
    hidden = dot_n(entry_two, expand_all) + expand_bias_all
    active, gelu_back = jax.vjp(partial(jax.nn.gelu, approximate=False), hidden)
    active_round = active.astype(BF)
    result = dot_n(active_round, reduce_all) + reduce_bias_all
    out_win = (mask * (middle + result)).astype(BF)
    block_output = unpack(parity, out_win, to_even(send_rows(out_win, moved)), tokens.shape)

    incoming = mask * pulls
    incoming_round = incoming.astype(BF)
    reduce_weight_grad = dot_f(active_round, incoming_round)
    reduce_bias_grad = jnp.sum(incoming, axis=0)
    (grad_hidden,) = gelu_back(dot_t(incoming_round, reduce_all))
    grad_hidden = grad_hidden.astype(BF)
    expand_weight_grad = dot_f(entry_two, grad_hidden)
    expand_bias_grad = jnp.sum(grad_hidden, axis=0, dtype=F32)
    grad_middle, post_gain_grad, post_bias_grad = post_back(dot_t(grad_hidden, expand_all))
    grad_middle = incoming + grad_middle
    reduce_shard = scatter_blocks(reduce_weight_grad)
    grad_branch = (mask * grad_middle).astype(BF)
    output_weight_grad = dot_f(mixed, grad_branch)
    output_bias_grad = jnp.sum(grad_branch, axis=0, dtype=F32)
    second_shard = scatter_blocks(jnp.concatenate([output_weight_grad, expand_weight_grad], 1))
    grad_mixed = dot_t(grad_branch, output_all).astype(BF)
    grad_queries, grad_keys, grad_values, found, values_bias_grad = attend_back(
        joint, grad_mixed, lse, fill, table
    )
    tables = sum_all(jnp.stack(table_grads(found, height_table.shape[0])))
    grad_joint = jnp.concatenate([grad_queries, grad_keys, grad_values], axis=1)
    triple_weight_grad = dot_f(entry, grad_joint)
    triple_bias_grad = jnp.concatenate(
        [jnp.sum(grad_queries, axis=0, dtype=F32), values_bias_grad[0]]
    )
    grad_entry = dot_t(grad_joint, triple_all)
    grad_flat, pre_gain_grad, pre_bias_grad = pre_back(mask * grad_entry)
    grad_win = (grad_middle + grad_flat).astype(BF)
    input_grad = unpack(parity, grad_win, to_even(send_rows(grad_win, moved)), tokens.shape)
    vector_grads = jnp.concatenate(
        [
            vector.reshape(width, -1)
            for vector in (
                pre_gain_grad, pre_bias_grad, triple_bias_grad, output_bias_grad, post_gain_grad,
                post_bias_grad, expand_bias_grad, reduce_bias_grad,
            )
        ],
        1,
    )
    vector_grads = jnp.pad(vector_grads, ((0, 0), (0, 128 - sum(counts))))
    first_shard = scatter_blocks(jnp.concatenate([triple_weight_grad, vector_grads], 1))
    shards = []
    begin = 3 * width
    for count in counts:
        shards.append(first_shard[:, begin : begin + count].reshape(-1))
        begin += count
    return (
        block_output,
        input_grad,
        shards[0],
        shards[1],
        first_shard[:, : 3 * width],
        shards[2],
        tables[0],
        tables[1],
        second_shard[:, :width],
        shards[3],
        shards[4],
        shards[5],
        second_shard[:, width:],
        shards[6],
        reduce_shard,
        shards[7],
    )


def solution(mesh):
    split = P(("img", "rows"))
    flat = P(("img", "rows"), None)
    grids = P(("img", "rows"), None, None)
    in_specs = (
        grids, P(), split, split, flat, split, P(), P(), flat, split, split, split, flat, split,
        flat, split, grids,
    )
    out_specs = (
        grids, grids, split, split, flat, split, P(), P(), flat, split, split, split, flat, split,
        flat, split,
    )
    return jax.shard_map(local, mesh=mesh, in_specs=in_specs, out_specs=out_specs, check_vma=False)
```

time: 1150 us -> 468 us (0.41)
  matrix products: 416 us -> 76.8 us
  waiting for transfers between devices: 285 us -> 102 us
  local copies, waits for them, and re-layouts: 167 us -> 59.1 us
  other arithmetic: 167 us -> 69.7 us
  blocking collectives: 85.5 us -> 0 us
  Pallas kernels: 0 us -> 74.5 us
  starting transfers between devices: 4.37 us -> 75.2 us
  between operations: 15.6 us -> 2.25 us
    dot_general x42 -> x12, matrix products: 416 us -> 76.8 us  [the longest x4 33.3 us: dot_n(): lax.dot_general(left, right, (((1,), (0,)), ((), ())), preferred_element_...]
    reduce_scatter x4 -> x0, waiting for transfers between devices: 277 us -> none  [the longest x1 142 us: local(): lax.psum_scatter(reduce_weight_grad, ('img', 'rows'), scatter_dimension=0...]
    reduce_sum x6 -> x5, other arithmetic: 140 us -> 6.72 us  [the longest x1 2.46 us: layer_norm(): return centred * lax.rsqrt(variance + 1e-06) * gain + bias]
    ppermute x4 -> x58, waiting for transfers between devices: 0.01 us -> 102 us  [the longest x26 70.4 us: swap_rows(): lax.ppermute(block, 'rows', [(place, place ^ 1 << bit) for place in range...]
    unnamed x2 -> x0, blocking collectives: 85.5 us -> none
    pallas_call x0 -> x8, Pallas kernels: none -> 74.5 us  [the longest x1 36.3 us: attend_back(): pl.pallas_call(attend_back_kernel, grid=(pairs,), in_specs=[column(0), co...]
    ppermute x4 -> x58, starting transfers between devices: 4.05 us -> 75.2 us  [the longest x26 36.4 us: swap_rows(): lax.ppermute(block, 'rows', [(place, place ^ 1 << bit) for place in range...]
    reshape x21 -> x17, local copies, waits for them, and re-layouts: 51 us -> 10.9 us  [the longest x8 6.05 us: local(): vector.reshape(block, -1)]
  transfers between devices with their start and end apart: 12 -> 58, of which waited for: 3 -> 23; matrix products, arithmetic and copies ran while one was open for 48% -> 25% of each run, Pallas kernels for 0% -> 8%
where the time goes in v1:
time: 468 us; the launch traced here: 460 us
  waiting for transfers between devices  102 us (22%)
  matrix products  76.8 us (16%)
  starting transfers between devices  75.2 us (16%)
  Pallas kernels  74.5 us (16%)
  other arithmetic  69.7 us (15%)
  local copies, waits for them, and re-layouts  59.1 us (13%)
    ppermute x26, waiting for transfers between devices, swap_rows(): lax.ppermute(block, 'rows', [(place, place ^ 1 << bit) for place in range...  70.4 us
    ppermute x26, starting transfers between devices, swap_rows(): lax.ppermute(block, 'rows', [(place, place ^ 1 << bit) for place in range...  36.4 us
    pallas_call x1, Pallas kernels, attend_back(): pl.pallas_call(attend_back_kernel, grid=(pairs,), in_specs=[column(0), co...  36.3 us
    dot_general x4, matrix products, dot_n(): lax.dot_general(left, right, (((1,), (0,)), ((), ())), preferred_element_...  33.3 us
    ppermute x21, waiting for transfers between devices, shift_depth(): lax.ppermute(block, 'rows', [(place, (place + 4 * step) % count) for plac...  31.6 us
    ppermute x21, starting transfers between devices, shift_depth(): lax.ppermute(block, 'rows', [(place, (place + 4 * step) % count) for plac...  30.2 us
    pallas_call x1, Pallas kernels, attend(): pl.pallas_call(attend_kernel, grid=(pairs,), in_specs=[column(0), column(...  22.6 us
    dot_general x4, matrix products, dot_t(): lax.dot_general(left, right, (((1,), (1,)), ((), ())), preferred_element_...  22.2 us
  transfers between devices with their start and end apart: 58, of which 23 were waited for; matrix products, arithmetic and copies ran while one was open for 25% of the time, Pallas kernels for 8%

profile of v1, /device:TPU:0, one launch (start us, length us, event | category | flops | bytes accessed | tf_op | source)
XLA Modules:
  0.0 459.7 jit_solution(2916571953879014902)
XLA Ops:
  39.2 8.9 %collective-permute-done.18 = bf16[96,768]{1,0:T(8,128)(2,1)S(1)} collective-permute-done((bf16[96,768]{1,0:T(8,128)(2,1)S(1)}, bf16[96,768]{1,0:T(8,128)(2,1)S(1)}, u32[]{:S(2)}, u32[]{:S(2)}) %collective-permute-start.18) | collective-permute-done | bytes 147488 | tf_op jit(solution)/shard_map/ppermute | solution.py:391
  62.6 9.6 %collective-permute-done.4 = bf16[4,24,1152]{2,1,0:T(8,128)(2,1)S(1)} collective-permute-done((bf16[4,24,1152]{2,1,0:T(8,128)(2,1)S(1)}, bf16[4,24,1152]{2,1,0:T(8,128)(2,1)S(1)}, u32[]{:S(2)}, u32[]{:S(2)}) %collective-permute-start.4) | collective-permute-done | bytes 221216 | tf_op jit(solution)/shard_map/ppermute | solution.py:382
  96.1 8.8 %collective-permute-done.5 = bf16[4,2,24,1152]{3,2,1,0:T(8,128)(2,1)S(1)} collective-permute-done((bf16[4,2,24,1152]{3,2,1,0:T(8,128)(2,1)}, bf16[4,2,24,1152]{3,2,1,0:T(8,128)(2,1)S(1)}, u32[]{:S(2)}, u32[]{:S(2)}) %collective-permute-start.5) | collective-permute-done | bytes 442400 | tf_op jit(solution)/shard_map/ppermute | solution.py:382
  105.7 9.0 %collective-permute-done.23 = bf16[4,2,96,384]{3,2,0,1:T(8,128)(2,1)S(1)} collective-permute-done((bf16[4,2,96,384]{3,2,0,1:T(8,128)(2,1)S(1)}, bf16[4,2,96,384]{3,2,0,1:T(8,128)(2,1)S(1)}, u32[]{:S(2)}, u32[]{:S(2)}) %collective-permute-start.23) | collective-permute-done | bytes 589856 | tf_op jit(solution)/shard_map/ppermute | solution.py:382
  135.6 6.2 %add_convert_fusion.1.q_ref.k_ref.v_ref = bf16[624,2304]{1,0:T(8,128)(2,1)} fusion(bf16[768,2432]{1,0:T(8,128)(2,1)} %bitcast.280, f32[2304]{0:T(1024)S(1)} %pad_maximum_fusion.12, bf16[624,768]{1,0:T(8,128)(2,1)S(1)} %copy-done.2, f32[768]{0:T(1024)S(1)} %get-tuple-element.35, f32[768]{0:T(1024)S(1)} %get-tuple-element.36, f32[624]{0:T(1024)S(1)} %fusion.92, ...), kind=kOutput, calls=%fused_computation.25 | convolution fusion | flops 2214531072 | bytes 7395648 | tf_op jit(solution)/shard_map/dot_general | solution.py:82
  141.8 22.6 %attend.1 = (bf16[624,768]{1,0:T(8,128)(2,1)}, f32[6,8,1536]{2,1,0:T(8,128)}) custom-call(bf16[624,2304]{1,0:T(8,128)(2,1)} %add_convert_fusion.1.q_ref.k_ref.v_ref, bf16[624,2304]{1,0:T(8,128)(2,1)} %add_convert_fusion.1.q_ref.k_ref.v_ref, bf16[624,2304]{1,0:T(8,128)(2,1)} %add_convert_fusion.1.q_ref.k_ref.v_ref, ...), custom_call_target="tpu_custom_call" | custom-call | tf_op jit(solution)/shard_map/attend/pallas_call | solution.py:234
  164.4 5.5 %maximum_select_fusion.1 = bf16[2,1536,768]{2,1,0:T(8,128)(2,1)S(1)} fusion(bf16[1,1536,768]{2,1,0:T(8,128)(2,1)} %bitcast.69, bf16[1,1536,384]{2,1,0:T(8,128)(2,1)} %bitcast.270, bf16[1,1536,384]{2,1,0:T(8,128)(2,1)} %bitcast.268, pred[]{:T(512)S(6)} %eq.58), kind=kLoop, calls=%fused_computation.26 | loop fusion | flops 30670848 | bytes 9437185 | tf_op jit(solution)/shard_map/jit(_where)/select_n | solution.py:397
  169.9 5.5 %maximum_select_fusion = bf16[2,384,3840]{2,1,0:T(8,128)(2,1)S(1)} fusion(bf16[1,384,3840]{2,1,0:T(8,128)(2,1)} %bitcast.49, bf16[1,384,1920]{2,1,0:T(8,128)(2,1)S(1)} %bitcast.265, bf16[1,384,1920]{2,1,0:T(8,128)(2,1)S(1)} %bitcast.263, pred[]{:T(512)S(6)} %eq.58), kind=kLoop, calls=%fused_computation.21 | loop fusion | flops 38338560 | bytes 11796481 | tf_op jit(solution)/shard_map/jit(_where)/select_n | solution.py:397
  176.9 21.8 %multiply_convert_fusion = (bf16[624,3072]{1,0:T(8,128)(2,1)}, f32[624,3072]{1,0:T(8,128)}, f32[624,3072]{1,0:T(8,128)}) fusion(f32[3072]{0:T(1024)S(1)} %reshape.846, bf16[768,3840]{1,0:T(8,128)(2,1)S(1)} %bitcast.285, f32[624,768]{1,0:T(8,128)S(1)} %get-tuple-element.98, f32[768]{0:T(1024)S(1)} %get-tuple-element.33, f32[768]{0:T(1024)S(1)} %get-tuple-element.32, ...), kind=kOutput, calls=%fused_computation.5 | convolution fusion | flops 3073314816 | bytes 25833472 | tf_op jit(solution)/shard_map/dot_general | solution.py:82
  198.8 10.3 %convert_reduce_fusion = (f32[3072]{0:T(1024)S(1)}, bf16[624,3072]{1,0:T(8,128)(2,1)}) fusion(f32[624,3072]{1,0:T(8,128)} %get-tuple-element.55, bf16[3072,768]{1,0:T(8,128)(2,1)S(1)} %bitcast.290, bf16[624,768]{1,0:T(8,128)(2,1)S(1)} %copy-done.10, f32[624]{0:T(1024)S(1)} %fusion.91, f32[624,3072]{1,0:T(8,128)} %get-tuple-element.99, f32[3072]{0:T(1024)S(1)} %reshape.846), kind=kOutput, calls=%fused_computation.3 | convolution fusion | flops 2978423808 | bytes 24873408 | tf_op jit(solution)/shard_map/dot_general | solution.py:74
  209.1 5.6 %multiply_reduce_fusion = (f32[768]{0:T(1024)S(1)}, f32[624]{0:T(1024)S(1)}, f32[768]{0:T(1024)S(1)}, f32[624,768]{1,0:T(8,128)S(1)}) fusion(f32[624,768]{1,0:T(8,128)S(1)} %get-tuple-element.98, f32[624]{0:T(1024)S(1)} %fusion.93, f32[624]{0:T(1024)S(1)} %broadcast_multiply_fusion, f32[768]{0:T(1024)S(1)} %get-tuple-element.32, ...), kind=kOutput, calls=%fused_computation.62 | convolution fusion | flops 2948233216 | bytes 12407232 | tf_op jit(solution)/shard_map/dot_general | solution.py:74
  221.1 36.3 %attend_back.1 = (bf16[624,768]{1,0:T(8,128)(2,1)}, bf16[624,768]{1,0:T(8,128)(2,1)}, bf16[624,768]{1,0:T(8,128)(2,1)}, f32[6,128,128]{2,1,0:T(8,128)}, f32[1,768]{1,0:T(1,128)}) custom-call(bf16[624,2304]{1,0:T(8,128)(2,1)} %add_convert_fusion.1.q_ref.k_ref.v_ref, bf16[624,2304]{1,0:T(8,128)(2,1)} %add_convert_fusion.1.q_ref.k_ref.v_ref, ...), custom_call_target="tpu_custom_call" | custom-call | tf_op jit(solution)/shard_map/attend_back/pallas_call | solution.py:254
  262.8 4.4 fusion.100
  267.3 5.7 %fusion.97 = f32[768,2304]{1,0:T(8,128)} fusion(bf16[624,2304]{1,0:T(8,128)(2,1)S(1)} %constant_dynamic-update-slice_fusion.2, bf16[624,768]{1,0:T(8,128)(2,1)S(1)} %copy-done.2, f32[768]{0:T(1024)S(1)} %get-tuple-element.35, f32[768]{0:T(1024)S(1)} %get-tuple-element.36, f32[624]{0:T(1024)S(1)} %fusion.92, f32[624]{0:T(1024)S(1)} %broadcast_multiply_fusion.1, ...), kind=kOutput, calls=%fused_computation.297 | convolution fusion | flops 2211655680 | bytes 10925376 | tf_op jit(solution)/shard_map/dot_general | solution.py:78
  273.0 6.8 %fusion.96 = f32[768,3072]{1,0:T(8,128)} fusion(bf16[624,3072]{1,0:T(8,128)(2,1)S(1)} %copy-done.18, f32[624,768]{1,0:T(8,128)S(1)} %copy-done.5, f32[768]{0:T(1024)S(1)} %get-tuple-element.33, f32[768]{0:T(1024)S(1)} %get-tuple-element.32, f32[624]{0:T(1024)S(1)} %fusion.93, f32[624]{0:T(1024)S(1)} %broadcast_multiply_fusion), kind=kOutput, calls=%fused_computation.296 | convolution fusion | flops 2946797568 | bytes 15199104 | tf_op jit(solution)/shard_map/dot_general | solution.py:78
  316.3 8.8 %pad_maximum_fusion = f32[768,3840]{1,0:T(8,128)} fusion(f32[768,3072]{1,0:T(8,128)} %fusion.96, f32[768,768]{1,0:T(8,128)S(1)} %copy-done.19), kind=kLoop, calls=%fused_computation | loop fusion | flops 2949120 | bytes 23592960 | tf_op jit(solution)/shard_map/concatenate | solution.py:575
  329.2 6.2 %fusion.50 = f32[3072,768]{1,0:T(8,128)S(1)} fusion(bf16[624,3072]{1,0:T(8,128)(2,1)} %get-tuple-element.54, bf16[624,768]{1,0:T(8,128)(2,1)S(1)} %copy-done.12, f32[624]{0:T(1024)S(1)} %fusion.91), kind=kOutput, calls=%fused_computation.168 | convolution fusion | flops 2945839104 | bytes 14232000 | tf_op jit(solution)/shard_map/dot_general | solution.py:78
  337.1 6.1 %fusion.16 = bf16[384,3840]{1,0:T(8,128)(2,1)} fusion(f32[2,384,3840]{2,1,0:T(8,128)} %bitcast.256, s32[]{:T(128)S(6)} %select_n.511), kind=kLoop, calls=%fused_computation.41 | loop fusion | bytes 5898244 | tf_op jit(solution)/shard_map/convert_element_type | solution.py:434
  347.2 4.7 %collective-permute-done.40 = f32[2,27,64]{2,0,1:T(2,128)S(1)} collective-permute-done((f32[2,27,64]{2,0,1:T(2,128)S(1)}, f32[2,27,64]{2,0,1:T(2,128)S(1)}, u32[]{:S(2)}, u32[]{:S(2)}) %collective-permute-start.40) | collective-permute-done | bytes 13856 | tf_op jit(solution)/shard_map/ppermute | solution.py:391
  352.0 5.6 %collective-permute-done.41 = f32[2,27,64]{2,0,1:T(2,128)S(1)} collective-permute-done((f32[2,27,64]{2,0,1:T(2,128)S(1)}, f32[2,27,64]{2,0,1:T(2,128)S(1)}, u32[]{:S(2)}, u32[]{:S(2)}) %collective-permute-start.41) | collective-permute-done | bytes 13856 | tf_op jit(solution)/shard_map/ppermute | solution.py:391
  374.4 7.4 %collective-permute-done.31 = bf16[4,2,24,1280]{3,2,1,0:T(8,128)(2,1)S(1)} collective-permute-done((bf16[4,2,24,1280]{3,2,1,0:T(8,128)(2,1)S(1)}, bf16[4,2,24,1280]{3,2,1,0:T(8,128)(2,1)S(1)}, u32[]{:S(2)}, u32[]{:S(2)}) %collective-permute-start.31) | collective-permute-done | bytes 491552 | tf_op jit(solution)/shard_map/ppermute | solution.py:382
  414.1 5.7 %collective-permute-done.54 = bf16[4,96,384]{2,1,0:T(8,128)(2,1)S(1)} collective-permute-done((bf16[4,96,384]{2,1,0:T(8,128)(2,1)S(1)}, bf16[4,96,384]{2,1,0:T(8,128)(2,1)S(1)}, u32[]{:S(2)}, u32[]{:S(2)}) %collective-permute-start.54) | collective-permute-done | bytes 294944 | tf_op jit(solution)/shard_map/ppermute | solution.py:382
  419.9 8.6 %collective-permute-done.52 = bf16[4,96,384]{2,1,0:T(8,128)(2,1)S(1)} collective-permute-done((bf16[4,96,384]{2,1,0:T(8,128)(2,1)S(1)}, bf16[4,96,384]{2,1,0:T(8,128)(2,1)S(1)}, u32[]{:S(2)}, u32[]{:S(2)}) %collective-permute-start.52) | collective-permute-done | bytes 294944 | tf_op jit(solution)/shard_map/ppermute | solution.py:382
  438.5 4.7 %collective-permute-done.46 = bf16[4,24,1920]{2,1,0:T(8,128)(2,1)S(1)} collective-permute-done((bf16[4,24,1920]{2,1,0:T(8,128)(2,1)S(1)}, bf16[4,24,1920]{2,1,0:T(8,128)(2,1)S(1)}, u32[]{:S(2)}, u32[]{:S(2)}) %collective-permute-start.46) | collective-permute-done | bytes 368672 | tf_op jit(solution)/shard_map/ppermute | solution.py:382
  (399 shorter events, 232.4 us)
Async XLA Ops:
  7.8 23.4 %collective-permute-start.2 = (bf16[24,2432]{1,0:T(8,128)(2,1)S(1)}, bf16[24,2432]{1,0:T(8,128)(2,1)S(1)}, u32[]{:S(2)}, u32[]{:S(2)}) collective-permute-start(bf16[24,2432]{1,0:T(8,128)(2,1)S(1)} %fusion.79), channel_id=1, source_target_pairs={{0,8},{1,9},{2,10},{3,11},{4,12},{5,13},{6,14},{7,15},{8,0},{9,1},... | collective-permute-start | bytes 350216 | tf_op jit(solution)/shard_map/ppermute | solution.py:391
  13.2 21.8 %collective-permute-start.3 = (bf16[24,2432]{1,0:T(8,128)(2,1)S(1)}, bf16[24,2432]{1,0:T(8,128)(2,1)S(1)}, u32[]{:S(2)}, u32[]{:S(2)}) collective-permute-start(bf16[24,2432]{1,0:T(8,128)(2,1)S(1)} %fusion.79), channel_id=1, source_target_pairs={{0,4},{1,5},{2,6},{3,7},{4,8},{5,9},{6,10},{7,11},{8,12},{9,13},{1... | collective-permute-start | bytes 350216 | tf_op jit(solution)/shard_map/ppermute | solution.py:391
  13.9 22.3 %collective-permute-start.17 = (bf16[96,768]{1,0:T(8,128)(2,1)}, bf16[96,768]{1,0:T(8,128)(2,1)S(1)}, u32[]{:S(2)}, u32[]{:S(2)}) collective-permute-start(bf16[96,768]{1,0:T(8,128)(2,1)} %param.37), channel_id=1, source_target_pairs={{0,12},{1,13},{2,14},{3,15},{4,0},{5,1},{6,2},{7,3},{8,4},{9,5},{1... | collective-permute-start | bytes 442376 | tf_op jit(solution)/shard_map/ppermute | solution.py:391
  17.0 35.8 %collective-permute-start.19 = (bf16[96,768]{1,0:T(8,128)(2,1)}, bf16[96,768]{1,0:T(8,128)(2,1)S(1)}, u32[]{:S(2)}, u32[]{:S(2)}) collective-permute-start(bf16[96,768]{1,0:T(8,128)(2,1)} %param.37), channel_id=1, source_target_pairs={{0,4},{1,5},{2,6},{3,7},{4,8},{5,9},{6,10},{7,11},{8,12},{9,13},{1... | collective-permute-start | bytes 442376 | tf_op jit(solution)/shard_map/ppermute | solution.py:391
  31.2 29.2 %collective-permute-start.11 = (bf16[24,3840]{1,0:T(8,128)(2,1)S(1)}, bf16[24,3840]{1,0:T(8,128)(2,1)S(1)}, u32[]{:S(2)}, u32[]{:S(2)}) collective-permute-start(bf16[24,3840]{1,0:T(8,128)(2,1)S(1)} %constant_dynamic-update-slice_fusion), channel_id=1, source_target_pairs={{0,4},{1,5},{2,6},{3,7},{4,8},{5,9},{6,10},{7,11},{8,12},{9,13},{1... | collective-permute-start | bytes 552968 | tf_op jit(solution)/shard_map/ppermute | solution.py:391
  35.1 23.7 %collective-permute-start.10 = (bf16[24,3840]{1,0:T(8,128)(2,1)S(1)}, bf16[24,3840]{1,0:T(8,128)(2,1)S(1)}, u32[]{:S(2)}, u32[]{:S(2)}) collective-permute-start(bf16[24,3840]{1,0:T(8,128)(2,1)S(1)} %constant_dynamic-update-slice_fusion), channel_id=1, source_target_pairs={{0,8},{1,9},{2,10},{3,11},{4,12},{5,13},{6,14},{7,15},{8,0},{9,1},... | collective-permute-start | bytes 552968 | tf_op jit(solution)/shard_map/ppermute | solution.py:391
  36.2 22.5 %collective-permute-start.9 = (bf16[24,3840]{1,0:T(8,128)(2,1)S(1)}, bf16[24,3840]{1,0:T(8,128)(2,1)S(1)}, u32[]{:S(2)}, u32[]{:S(2)}) collective-permute-start(bf16[24,3840]{1,0:T(8,128)(2,1)S(1)} %constant_dynamic-update-slice_fusion), channel_id=1, source_target_pairs={{0,12},{1,13},{2,14},{3,15},{4,0},{5,1},{6,2},{7,3},{8,4},{9,5},{1... | collective-permute-start | bytes 552968 | tf_op jit(solution)/shard_map/ppermute | solution.py:391
  48.1 35.8 %collective-permute-start.26 = (bf16[7,32,768]{2,1,0:T(8,128)(2,1)}, bf16[7,32,768]{2,1,0:T(8,128)(2,1)}, u32[]{:S(2)}, u32[]{:S(2)}) collective-permute-start(bf16[7,32,768]{2,1,0:T(8,128)(2,1)} %slice.184), channel_id=1, source_target_pairs={{0,1},{2,3},{4,5},{6,7},{8,9},{10,11},{12,13},{14,15},{16,17},{18,... | collective-permute-start | bytes 1032200 | tf_op jit(solution)/shard_map/ppermute | solution.py:475
  52.9 22.0 %collective-permute-start = (bf16[7,32,768]{2,1,0:T(8,128)(2,1)}, bf16[7,32,768]{2,1,0:T(8,128)(2,1)S(1)}, u32[]{:S(2)}, u32[]{:S(2)}) collective-permute-start(bf16[7,32,768]{2,1,0:T(8,128)(2,1)} %slice.162), channel_id=1, source_target_pairs={{0,1},{2,3},{4,5},{6,7},{8,9},{10,11},{12,13},{14,15},{16,17},{18,... | collective-permute-start | bytes 1032200 | tf_op jit(solution)/shard_map/ppermute | solution.py:475
  58.8 28.4 %collective-permute-start.6 = (bf16[4,24,1280]{2,1,0:T(8,128)(2,1)}, bf16[4,24,1280]{2,1,0:T(8,128)(2,1)S(1)}, u32[]{:S(2)}, u32[]{:S(2)}) collective-permute-start(bf16[4,24,1280]{2,1,0:T(8,128)(2,1)} %constant_dynamic-slice_fusion.11), channel_id=1, source_target_pairs={{0,2},{1,3},{2,0},{3,1},{4,6},{5,7},{6,4},{7,5},{8,10},{9,11},{10,... | collective-permute-start | bytes 737288 | tf_op jit(solution)/shard_map/ppermute | solution.py:382
  60.4 28.5 %collective-permute-start.20 = (bf16[4,96,384]{2,1,0:T(8,128)(2,1)S(1)}, bf16[4,96,384]{2,1,0:T(8,128)(2,1)S(1)}, u32[]{:S(2)}, u32[]{:S(2)}) collective-permute-start(bf16[4,96,384]{2,1,0:T(8,128)(2,1)S(1)} %get-tuple-element.66), channel_id=1, source_target_pairs={{0,1},{1,0},{2,3},{3,2},{4,5},{5,4},{6,7},{7,6},{8,9},{9,8},{10,11... | collective-permute-start | bytes 884744 | tf_op jit(solution)/shard_map/ppermute | solution.py:382
  89.1 27.9 %collective-permute-start.21 = (bf16[4,2,96,384]{3,2,1,0:T(8,128)(2,1)S(1)}, bf16[4,2,96,384]{3,2,1,0:T(8,128)(2,1)S(1)}, u32[]{:S(2)}, u32[]{:S(2)}) collective-permute-start(bf16[4,2,96,384]{3,2,1,0:T(8,128)(2,1)S(1)} %maximum_select_fusion.12), channel_id=1, source_target_pairs={{0,2},{1,3},{2,0},{3,1},{4,6},{5,7},{6,4},{7,5},{8,10},{9,11},{10,... | collective-permute-start | bytes 1769480 | tf_op jit(solution)/shard_map/ppermute | solution.py:382
  90.1 24.5 %collective-permute-start.23 = (bf16[4,2,96,384]{3,2,0,1:T(8,128)(2,1)S(1)}, bf16[4,2,96,384]{3,2,0,1:T(8,128)(2,1)S(1)}, u32[]{:S(2)}, u32[]{:S(2)}) collective-permute-start(bf16[4,2,96,384]{3,2,0,1:T(8,128)(2,1)S(1)} %maximum_select_fusion.14), channel_id=1, source_target_pairs={{0,1},{1,0},{2,3},{3,2},{4,5},{5,4},{6,7},{7,6},{8,9},{9,8},{10,11... | collective-permute-start | bytes 1769480 | tf_op jit(solution)/shard_map/ppermute | solution.py:382
  95.4 29.4 %collective-permute-start.13 = (bf16[4,2,24,1920]{3,2,1,0:T(8,128)(2,1)S(1)}, bf16[4,2,24,1920]{3,2,1,0:T(8,128)(2,1)S(1)}, u32[]{:S(2)}, u32[]{:S(2)}) collective-permute-start(bf16[4,2,24,1920]{3,2,1,0:T(8,128)(2,1)S(1)} %maximum_select_fusion.9), channel_id=1, source_target_pairs={{0,2},{1,3},{2,0},{3,1},{4,6},{5,7},{6,4},{7,5},{8,10},{9,11},{10,... | collective-permute-start | bytes 2211848 | tf_op jit(solution)/shard_map/ppermute | solution.py:382
  119.0 45.5 %collective-permute-start.24 = (bf16[1536,768]{1,0:T(8,128)(2,1)}, bf16[1536,768]{1,0:T(8,128)(2,1)}, u32[]{:S(2)}, u32[]{:S(2)}) collective-permute-start(bf16[1536,768]{1,0:T(8,128)(2,1)} %pad_maximum_fusion.2), channel_id=1, source_target_pairs={{0,16},{16,0},{1,17},{17,1},{2,18},{18,2},{3,19},{19,3},{4,20},{20... | collective-permute-start | bytes 7077896 | tf_op jit(solution)/shard_map/ppermute | solution.py:386
  126.8 43.1 %collective-permute-start.16 = (bf16[384,3840]{1,0:T(8,128)(2,1)}, bf16[384,3840]{1,0:T(8,128)(2,1)}, u32[]{:S(2)}, u32[]{:S(2)}) collective-permute-start(bf16[384,3840]{1,0:T(8,128)(2,1)} %pad_maximum_fusion.1), channel_id=1, source_target_pairs={{0,16},{16,0},{1,17},{17,1},{2,18},{18,2},{3,19},{19,3},{4,20},{20... | collective-permute-start | bytes 8847368 | tf_op jit(solution)/shard_map/ppermute | solution.py:386
  286.0 75.7 %collective-permute-start.25 = (bf16[7,32,768]{2,1,0:T(8,128)(2,1)}, bf16[7,32,768]{2,1,0:T(8,128)(2,1)}, u32[]{:S(2)}, u32[]{:S(2)}) collective-permute-start(bf16[7,32,768]{2,1,0:T(8,128)(2,1)} %send_rows.2), channel_id=1, source_target_pairs={{1,0},{3,2},{5,4},{7,6},{9,8},{11,10},{13,12},{15,14},{17,16},{19,... | collective-permute-start | bytes 1032200 | tf_op jit(solution)/shard_map/ppermute | solution.py:480
  291.4 33.7 %collective-permute-start.36 = (f32[2,27,64]{2,0,1:T(2,128)}, f32[2,27,64]{2,0,1:T(2,128)S(1)}, u32[]{:S(2)}, u32[]{:S(2)}) collective-permute-start(f32[2,27,64]{2,0,1:T(2,128)} %pad_maximum_fusion.11), channel_id=1, source_target_pairs={{0,16},{16,0},{1,17},{17,1},{2,18},{18,2},{3,19},{19,3},{4,20},{20... | collective-permute-start | bytes 41480 | tf_op jit(solution)/shard_map/ppermute | solution.py:386
  304.0 60.7 %collective-permute-start.27 = (bf16[7,32,768]{2,1,0:T(8,128)(2,1)}, bf16[7,32,768]{2,1,0:T(8,128)(2,1)}, u32[]{:S(2)}, u32[]{:S(2)}) collective-permute-start(bf16[7,32,768]{2,1,0:T(8,128)(2,1)} %send_rows.3), channel_id=1, source_target_pairs={{1,0},{3,2},{5,4},{7,6},{9,8},{11,10},{13,12},{15,14},{17,16},{19,... | collective-permute-start | bytes 1032200 | tf_op jit(solution)/shard_map/ppermute | solution.py:480
  316.2 41.5 %collective-permute-start.28 = (bf16[384,2432]{1,0:T(8,128)(2,1)}, bf16[384,2432]{1,0:T(8,128)(2,1)}, u32[]{:S(2)}, u32[]{:S(2)}) collective-permute-start(bf16[384,2432]{1,0:T(8,128)(2,1)} %fusion.32), channel_id=1, source_target_pairs={{0,16},{16,0},{1,17},{17,1},{2,18},{18,2},{3,19},{19,3},{4,20},{20... | collective-permute-start | bytes 5603336 | tf_op jit(solution)/shard_map/ppermute | solution.py:386
  343.2 58.3 %collective-permute-start.42 = (bf16[384,3840]{1,0:T(8,128)(2,1)}, bf16[384,3840]{1,0:T(8,128)(2,1)}, u32[]{:S(2)}, u32[]{:S(2)}) collective-permute-start(bf16[384,3840]{1,0:T(8,128)(2,1)} %fusion.16), channel_id=1, source_target_pairs={{0,16},{16,0},{1,17},{17,1},{2,18},{18,2},{3,19},{19,3},{4,20},{20... | collective-permute-start | bytes 8847368 | tf_op jit(solution)/shard_map/ppermute | solution.py:386
  357.6 26.0 %collective-permute-start.50 = (bf16[1536,768]{1,0:T(8,128)(2,1)}, bf16[1536,768]{1,0:T(8,128)(2,1)}, u32[]{:S(2)}, u32[]{:S(2)}) collective-permute-start(bf16[1536,768]{1,0:T(8,128)(2,1)} %fusion.21), channel_id=1, source_target_pairs={{0,16},{16,0},{1,17},{17,1},{2,18},{18,2},{3,19},{19,3},{4,20},{20... | collective-permute-start | bytes 7077896 | tf_op jit(solution)/shard_map/ppermute | solution.py:386
  405.9 28.7 %collective-permute-start.45 = (bf16[4,2,24,1920]{3,2,1,0:T(8,128)(2,1)S(1)}, bf16[4,2,24,1920]{3,2,1,0:T(8,128)(2,1)S(1)}, u32[]{:S(2)}, u32[]{:S(2)}) collective-permute-start(bf16[4,2,24,1920]{3,2,1,0:T(8,128)(2,1)S(1)} %dynamic-slice_bitcast_fusion), channel_id=1, source_target_pairs={{0,2},{1,3},{2,0},{3,1},{4,6},{5,7},{6,4},{7,5},{8,10},{9,11},{10,... | collective-permute-start | bytes 2211848 | tf_op jit(solution)/shard_map/ppermute | solution.py:382
  413.6 22.9 %collective-permute-start.43 = (bf16[4,2,24,1920]{3,2,0,1:T(8,128)(2,1)S(1)}, bf16[4,2,24,1920]{3,2,0,1:T(8,128)(2,1)S(1)}, u32[]{:S(2)}, u32[]{:S(2)}) collective-permute-start(bf16[4,2,24,1920]{3,2,0,1:T(8,128)(2,1)S(1)} %bitcast.316), channel_id=1, source_target_pairs={{0,1},{1,0},{2,3},{3,2},{4,5},{5,4},{6,7},{7,6},{8,9},{9,8},{10,11... | collective-permute-start | bytes 2211848 | tf_op jit(solution)/shard_map/ppermute | solution.py:382
  (73 other events, 873.2 us)

commit v2 on v1

v2 whole, which is shorter than its diff:
```python
from functools import partial

import jax
import jax.numpy as jnp
import numpy as np
from jax import lax
from jax.experimental import pallas as pl
from jax.experimental.pallas import tpu as pltpu
from jax.sharding import PartitionSpec as P

HEADS = 12
HEAD_DIM = 64
WIN = 14
REAL = 32
KEYS = 208
BF = jnp.bfloat16
F32 = jnp.float32
VMEM_LIMIT = 60 * 2**20


def cost(microseconds):
    return pl.CostEstimate(flops=int(microseconds * 1000000000), bytes_accessed=1, transcendentals=0)


ANY = pl.BlockSpec(memory_space=pl.ANY)

SEGMENTS = []
_offset = 0
for _row, _rows in ((0, WIN), (WIN, REAL - 2 * WIN)):
    for _col, _cols in ((0, WIN), (WIN, WIN), (2 * WIN, REAL - 2 * WIN)):
        _padded = -(-_rows * _cols // 16) * 16
        SEGMENTS.append((_row, _rows, _col, _cols, _padded, _offset))
        _offset += _padded
TOKENS = _offset
BAND = REAL - WIN


def ordered(kernel, count, earlier):
    def body(*refs):
        kernel(*refs[:count], *refs[count + len(earlier) :])

    return body


def window_constants():
    band_row = np.full((TOKENS,), 0, np.int32)
    column = np.full((TOKENS,), 0, np.int32)
    valid = np.zeros((TOKENS,), np.int32)
    along = np.zeros((TOKENS,), np.int32)
    across = np.zeros((TOKENS,), np.int32)
    onehots = np.zeros((len(SEGMENTS), KEYS, 128), np.float32)
    for number, (row, rows, col, cols, padded, offset) in enumerate(SEGMENTS):
        spots = [(a, b) for a in range(rows) for b in range(cols)]
        for place, (a, b) in enumerate(spots):
            band_row[offset + place] = row + a
            column[offset + place] = col + b
            valid[offset + place] = 1
            along[offset + place] = a
            across[offset + place] = b
        rest = [(s, t) for s in range(WIN) for t in range(WIN) if s >= rows or t >= cols]
        slots = spots + [None] * (padded - len(spots)) + rest
        slots = slots + [None] * (KEYS - len(slots))
        for place, spot in enumerate(slots):
            for head in range(2):
                if spot is None:
                    onehots[number, place, 32 * head + 15] = -1e30
                else:
                    for part in range(2):
                        onehots[number, place, 32 * head + 16 * part + spot[0]] = 1
                        onehots[number, place, 64 + 32 * head + 16 * part + spot[1]] = 1
    return band_row, column, valid, along, across, onehots


BAND_ROW, COLUMN, VALID, ALONG, ACROSS, ONEHOTS = window_constants()


def shift_amounts():
    amounts = np.zeros((TOKENS, 128), np.int32)
    amounts[:, :64] = (WIN - 1 - ALONG)[:, None]
    amounts[:, 64:] = (WIN - 1 - ACROSS)[:, None]
    return amounts


SHIFTS = shift_amounts()


def dot_t(left, right):
    return lax.dot_general(left, right, (((1,), (1,)), ((), ())), preferred_element_type=F32)


def dot_f(left, right):
    return lax.dot_general(left, right, (((0,), (0,)), ((), ())), preferred_element_type=F32)


def dot_n(left, right):
    return lax.dot_general(left, right, (((1,), (0,)), ((), ())), preferred_element_type=F32)


def lanes_of(shape):
    return lax.broadcasted_iota(jnp.int32, shape, len(shape) - 1)


def relative_features(queries, table, shifts):
    terms = dot_n(queries, table)
    for bit in range(4):
        rolled = pltpu.roll(terms, 128 - (1 << bit), 1)
        terms = jnp.where((shifts & (1 << bit)) != 0, rolled, terms)
    high = terms.astype(BF).astype(F32)
    low = pltpu.roll(terms - high, 16, 1)
    lane = lanes_of(terms.shape) & 31
    mixed = jnp.where(lane < WIN, high, jnp.where((lane >= 16) & (lane < 16 + WIN), low, 0.0))
    return jnp.where(lane == 15, 1.0, mixed).astype(BF)


def stacked_queries(queries, features, start, count):
    lane = lanes_of((count, 128))
    first = lane < 64
    even = (lane & 32) == 0
    part = queries[start : start + count] * jnp.asarray(0.125, BF)
    extra = features[start : start + count]
    zero = jnp.zeros_like(part)
    top = jnp.concatenate([jnp.where(first, part, zero), jnp.where(even, extra, zero)], 1)
    low = jnp.concatenate([jnp.where(first, zero, part), jnp.where(even, zero, extra)], 1)
    return jnp.concatenate([top, low], 0)


def window_keys(array, start, count, fill):
    if count == KEYS:
        return array[start : start + count]
    rest = jnp.broadcast_to(fill, (KEYS - count, 128)).astype(BF)
    return jnp.concatenate([array[start : start + count], rest], 0)


def tiles_of(total):
    return [(begin, min(128, total - begin)) for begin in range(0, total, 128)]


def lane_spots():
    spots = []
    base = 0
    for _, _, _, _, count, _ in SEGMENTS:
        spots.append((base, 2 * count))
        base += -(-2 * count // 128) * 128
    return spots


def window_sides(number, queries, features, keys, onehots_ref):
    _, _, _, _, count, start = SEGMENTS[number]
    left = stacked_queries(queries, features, start, count)
    none = jnp.zeros((1, 128), BF)
    right = jnp.concatenate([window_keys(keys, start, count, none), onehots_ref[number]], 1)
    return left, right


def attend_kernel(
    q_ref, k_ref, v_ref, fill_ref, table_ref, shifts_ref, onehots_ref,
    mixed_ref, lse_ref, features_ref, scores_ref, weights_ref,
):
    queries = q_ref[...]
    features = relative_features(queries, table_ref[...], shifts_ref[...])
    features_ref[...] = features
    keys, values = k_ref[...], v_ref[...]
    fill = fill_ref[...]
    spots = lane_spots()
    for number, (base, size) in enumerate(spots):
        left, right = window_sides(number, queries, features, keys, onehots_ref)
        scores_ref[:, base : base + size] = dot_t(right, left)
    totals = []
    for base, size in spots:
        scores = scores_ref[:, base : base + size]
        top = jnp.max(scores, axis=0, keepdims=True)
        weights = jnp.exp(scores - top)
        total = jnp.sum(weights, axis=0, keepdims=True)
        lse_ref[0, 0:1, base : base + size] = top + jnp.log(total)
        weights_ref[:, base : base + size] = weights.astype(BF)
        totals.append(1.0 / total)
    for (_, _, _, _, count, start), (base, size), scale in zip(SEGMENTS, spots, totals):
        held = window_keys(values, start, count, fill).T
        both = (dot_n(held, weights_ref[:, base : base + size]) * scale).T
        lane = lanes_of((count, 128))
        mixed = jnp.where(lane < 64, both[:count], both[count:])
        mixed_ref[start : start + count, :] = mixed.astype(BF)


LSE = sum(-(-2 * segment[4] // 128) * 128 for segment in SEGMENTS)


def attend_back_kernel(
    q_ref, k_ref, v_ref, g_ref, lse_ref, features_ref, fill_ref, table_ref, shifts_ref, onehots_ref,
    dqkv_ref, dtable_ref, dbias_ref,
    scores_ref, dprobs_ref, probs_ref, dscores_ref, back_ref, slots_ref,
):
    queries = q_ref[...]
    shifts = shifts_ref[...]
    table = table_ref[...]
    features = features_ref[...]
    keys, values, grads = k_ref[...], v_ref[...], g_ref[...]
    fill = fill_ref[...]
    spots = lane_spots()

    def stacked_pulls(start, count):
        first = lanes_of((count, 128)) < 64
        part = grads[start : start + count]
        zero = jnp.zeros_like(part)
        return jnp.concatenate([jnp.where(first, part, zero), jnp.where(first, zero, part)], 0)

    for number, (base, size) in enumerate(spots):
        _, _, _, _, count, start = SEGMENTS[number]
        left, right = window_sides(number, queries, features, keys, onehots_ref)
        scores_ref[:, base : base + size] = dot_t(right, left)
        held = window_keys(values, start, count, fill)
        dprobs_ref[:, base : base + size] = dot_t(held, stacked_pulls(start, count))
    for base, size in spots:
        lanes = slice(base, base + size)
        probs = jnp.exp(scores_ref[:, lanes] - lse_ref[0, 0:1, lanes])
        product = probs * dprobs_ref[:, lanes]
        delta = jnp.sum(product, axis=0, keepdims=True)
        probs_ref[:, lanes] = probs.astype(BF)
        dscores_ref[:, lanes] = (product - probs * delta).astype(BF)
    bias_sum = jnp.zeros((1, 128), F32)
    for number, (base, size) in enumerate(spots):
        _, _, _, _, count, start = SEGMENTS[number]
        left, right = window_sides(number, queries, features, keys, onehots_ref)
        dscores = dscores_ref[:, base : base + size]
        dvalues = dot_n(probs_ref[:, base : base + size], stacked_pulls(start, count))
        dkeys = dot_n(dscores, left[:, :128])
        dqkv_ref[start : start + count, 256:] = dvalues[:count].astype(BF)
        dqkv_ref[start : start + count, 128:256] = dkeys[:count].astype(BF)
        bias_sum = bias_sum + jnp.sum(dvalues, axis=0, keepdims=True)
        both = dot_f(dscores, right)
        lane = lanes_of((count, 128))
        back_ref[start : start + count, :128] = jnp.where(lane < 64, both[:count, :128], both[count:, :128])
        back_ref[start : start + count, 128:] = jnp.where(
            (lane & 32) == 0, both[:count, 128:], both[count:, 128:]
        )
    lane = lanes_of((TOKENS, 128)) & 31
    slots = jnp.where(lane < WIN, back_ref[:, 128:], 0.0)
    for bit in range(4):
        rolled = pltpu.roll(slots, 1 << bit, 1)
        slots = jnp.where((shifts & (1 << bit)) != 0, rolled, slots)
    high = slots.astype(BF)
    low = (slots - high.astype(F32)).astype(BF)
    slots_ref[:, :128] = high
    slots_ref[:, 128:] = low
    dq = back_ref[:, :128] * 0.125 + dot_t(slots_ref[...], jnp.concatenate([table, table], 1))
    dq = dq.astype(BF)
    dqkv_ref[:, :128] = dq
    found = dot_f(slots_ref[...], queries)
    dtable_ref[0] = found[:128] + found[128:]
    query_sum = jnp.sum(dq.astype(F32), axis=0, keepdims=True)
    dbias_ref[...] = jnp.concatenate([query_sum, bias_sum], 0)


def whole(shape):
    return pl.BlockSpec(shape, lambda step: (0,) * len(shape))


def column(offset, rows=TOKENS):
    return pl.BlockSpec((rows, 128), lambda step: (0, offset + step))


def reversed_table(height_table, width_table):
    slots = height_table.shape[0]
    pad = ((0, 0), (0, 32 - slots))
    height = jnp.pad(height_table[::-1].T, pad)
    width = jnp.pad(width_table[::-1].T, pad)
    none = jnp.zeros_like(height)
    top = jnp.concatenate([height, none, width, none], 1)
    low = jnp.concatenate([none, height, none, width], 1)
    return jnp.concatenate([top, low], 0)


def attend(joint, fill, table, begin, count, given, *earlier):
    pairs = HEADS // 2
    shapes = [
        jax.ShapeDtypeStruct((TOKENS, pairs * 128), BF),
        jax.ShapeDtypeStruct((pairs, 8, LSE), F32),
        jax.ShapeDtypeStruct((TOKENS, pairs * 128), BF),
    ]
    return pl.pallas_call(
        ordered(attend_kernel, 7, tuple(given) + earlier),
        grid=(count,),
        in_specs=[
            column(begin), column(pairs + begin), column(2 * pairs + begin), column(begin, 1),
            whole((128, 128)), whole((TOKENS, 128)), whole((len(SEGMENTS), KEYS, 128)),
        ] + [ANY] * (len(given) + len(earlier)),
        out_specs=[
            column(begin), pl.BlockSpec((1, 8, LSE), lambda step: (begin + step, 0, 0)), column(begin),
        ],
        out_shape=shapes,
        input_output_aliases={7 + place: place for place in range(len(given))},
        scratch_shapes=[pltpu.VMEM((KEYS, LSE), F32), pltpu.VMEM((KEYS, LSE), BF)],
        compiler_params=pltpu.CompilerParams(vmem_limit_bytes=VMEM_LIMIT),
        cost_estimate=cost(5.5),
        name="attend",
    )(joint, joint, joint, fill, table, jnp.asarray(SHIFTS), jnp.asarray(ONEHOTS, BF), *given, *earlier)


def attend_back(joint, grad_mixed, lse, features, fill, table, begin, count, *earlier):
    pairs = HEADS // 2

    def kernel(*refs):
        attend_back_kernel(*refs[:10], *refs[10 + len(earlier) :])

    return pl.pallas_call(
        kernel,
        grid=(count,),
        in_specs=[
            column(begin), column(pairs + begin), column(2 * pairs + begin), column(begin),
            pl.BlockSpec((1, 8, LSE), lambda step: (begin + step, 0, 0)), column(begin), column(begin, 1),
            whole((128, 128)), whole((TOKENS, 128)), whole((len(SEGMENTS), KEYS, 128)),
        ] + [pl.BlockSpec(memory_space=pl.ANY)] * len(earlier),
        out_specs=[
            pl.BlockSpec((TOKENS, 384), lambda step: (0, step)),
            pl.BlockSpec((1, 128, 128), lambda step: (step, 0, 0)), column(0, 2),
        ],
        out_shape=[
            jax.ShapeDtypeStruct((TOKENS, count * 384), BF),
            jax.ShapeDtypeStruct((count, 128, 128), F32),
            jax.ShapeDtypeStruct((2, count * 128), F32),
        ],
        scratch_shapes=[
            pltpu.VMEM((KEYS, LSE), F32), pltpu.VMEM((KEYS, LSE), F32),
            pltpu.VMEM((KEYS, LSE), BF), pltpu.VMEM((KEYS, LSE), BF),
            pltpu.VMEM((TOKENS, 256), F32), pltpu.VMEM((TOKENS, 256), BF),
        ],
        compiler_params=pltpu.CompilerParams(vmem_limit_bytes=VMEM_LIMIT),
        cost_estimate=cost(14.5),
        name="attend_back",
    )(
        joint, joint, joint, grad_mixed, lse, features, fill, table, jnp.asarray(SHIFTS), jnp.asarray(ONEHOTS, BF),
        *earlier,
    )


def tie(value, *earlier):
    def kernel(*refs):
        pass

    return pl.pallas_call(
        kernel,
        in_specs=[pl.BlockSpec(memory_space=pl.ANY)] * (1 + len(earlier)),
        out_specs=pl.BlockSpec(memory_space=pl.ANY),
        out_shape=jax.ShapeDtypeStruct(value.shape, value.dtype),
        input_output_aliases={0: 0},
        name="tie",
    )(value, *earlier)


def table_grads(found, slots):
    total = jnp.sum(found, axis=0)
    height = total[0:32, :64] + total[32:64, 64:]
    width = total[64:96, :64] + total[96:128, 64:]
    return height[:slots][::-1], width[:slots][::-1]


def pack_kernel(masked, moved, parity_ref, own_ref, far_ref, mask_ref, out_ref, stage_ref):
    parity = parity_ref[0]
    stage_ref[...] = jnp.zeros_like(stage_ref)
    for row in range(BAND):
        if row < moved:
            line = jnp.where(parity == 0, own_ref[row, :REAL], far_ref[row]).astype(F32)
        else:
            line = own_ref[row - moved * parity, :REAL].astype(F32)
        for first, rows, col, cols, _, offset in SEGMENTS:
            if first <= row < first + rows:
                place = offset + (row - first) * cols
                stage_ref[place : place + cols, :] = line[col : col + cols]
    if masked:
        out_ref[...] = (stage_ref[...] * mask_ref[...]).astype(out_ref.dtype)
    else:
        out_ref[...] = stage_ref[...].astype(out_ref.dtype)


def pack(parity, own, far, mask, masked, *earlier):
    width = own.shape[2]
    vmem = pl.BlockSpec(memory_space=pltpu.VMEM)
    return pl.pallas_call(
        ordered(partial(pack_kernel, masked, far.shape[0]), 4, earlier),
        in_specs=[pl.BlockSpec(memory_space=pltpu.SMEM), vmem, vmem, vmem] + [ANY] * len(earlier),
        out_specs=vmem,
        out_shape=jax.ShapeDtypeStruct((TOKENS, width), BF),
        scratch_shapes=[pltpu.VMEM((TOKENS, width), F32)],
        compiler_params=pltpu.CompilerParams(vmem_limit_bytes=VMEM_LIMIT),
        cost_estimate=cost(3),
        name="pack",
    )(parity.reshape(1), own, far, mask, *earlier)


def unpack_kernel(moved, parity_ref, win_ref, far_ref, out_ref, wide_ref, stage_ref):
    parity = parity_ref[0]
    wide_ref[...] = win_ref[...].astype(F32)
    for row in range(BAND):
        for first, rows, col, cols, _, offset in SEGMENTS:
            if first <= row < first + rows:
                place = offset + (row - first) * cols
                stage_ref[row, col : col + cols, :] = wide_ref[place : place + cols, :]
    out_ref[...] = jnp.zeros_like(out_ref)
    for row in range(out_ref.shape[0]):
        near = stage_ref[row] if row < WIN else far_ref[row - WIN].astype(F32)
        other = stage_ref[row + moved] if row + moved < BAND else jnp.zeros_like(near)
        out_ref[row, :REAL, :] = jnp.where(parity == 0, near, other).astype(out_ref.dtype)


def unpack(parity, win, far, shape, *earlier):
    width = win.shape[1]
    return pl.pallas_call(
        ordered(partial(unpack_kernel, far.shape[0]), 3, earlier),
        in_specs=[
            pl.BlockSpec(memory_space=pltpu.SMEM),
            pl.BlockSpec(memory_space=pltpu.VMEM),
            pl.BlockSpec(memory_space=pltpu.VMEM),
        ] + [ANY] * len(earlier),
        out_specs=pl.BlockSpec(memory_space=pltpu.VMEM),
        out_shape=jax.ShapeDtypeStruct(shape, BF),
        scratch_shapes=[pltpu.VMEM((TOKENS, width), F32), pltpu.VMEM((BAND, REAL, width), F32)],
        compiler_params=pltpu.CompilerParams(vmem_limit_bytes=VMEM_LIMIT),
        cost_estimate=cost(3),
        name="unpack",
    )(parity.reshape(1), win, far, *earlier)


def send_rows_kernel(win_ref, out_ref, wide_ref, stage_ref):
    wide_ref[...] = win_ref[...].astype(F32)
    for row in range(out_ref.shape[0]):
        for first, rows, col, cols, _, offset in SEGMENTS:
            if first <= row < first + rows:
                place = offset + (row - first) * cols
                stage_ref[row, col : col + cols, :] = wide_ref[place : place + cols, :]
    out_ref[...] = stage_ref[...].astype(out_ref.dtype)


def send_rows(win, moved, *earlier):
    width = win.shape[1]
    vmem = pl.BlockSpec(memory_space=pltpu.VMEM)
    return pl.pallas_call(
        ordered(send_rows_kernel, 1, earlier),
        in_specs=[vmem] + [ANY] * len(earlier),
        out_specs=vmem,
        out_shape=jax.ShapeDtypeStruct((moved, REAL, width), BF),
        scratch_shapes=[pltpu.VMEM((TOKENS, width), F32), pltpu.VMEM((moved, REAL, width), F32)],
        compiler_params=pltpu.CompilerParams(vmem_limit_bytes=VMEM_LIMIT),
        cost_estimate=cost(2.6),
        name="send_rows",
    )(win, *earlier)


def gelu_parts(hidden):
    bell = jnp.exp(hidden * hidden * -0.5)
    size = jnp.abs(hidden)
    turn = pl.reciprocal(1.0 + 0.3275911 * 0.7071067811865476 * size)
    poly = turn * (
        0.5 * 0.254829592
        + turn
        * (
            0.5 * -0.284496736
            + turn * (0.5 * 1.421413741 + turn * (0.5 * -1.453152027 + turn * (0.5 * 1.061405429)))
        )
    )
    tail = poly * bell
    below = jnp.where(hidden >= 0, 1.0 - tail, tail)
    return hidden * below, below + hidden * (0.3989422804014327 * bell)


def mlp_kernel(
    img_ref, entry_ref, pull_ref, expand_ref, expand_far_ref, bias_ref, reduce_ref, reduce_far_ref,
    result_ref, back_ref, dreduce_ref, dexpand_far_ref, dexpand_ref, dbias_ref, turned_ref,
):
    step = pl.program_id(0)
    first_half = step < pl.num_programs(0) // 2
    low = img_ref[0] == 0

    @pl.when(step == 0)
    def _():
        result_ref[...] = jnp.zeros_like(result_ref)
        back_ref[...] = jnp.zeros_like(back_ref)
        turned_ref[...] = entry_ref[...].T

    near, far = expand_ref[...], expand_far_ref[...]
    expand = jnp.concatenate([jnp.where(low, near, far), jnp.where(low, far, near)], 0)
    reduce = jnp.where(first_half, reduce_far_ref[...], reduce_ref[...])
    pull = pull_ref[...]
    hidden = dot_n(entry_ref[...], expand) + bias_ref[...]
    active, slope = gelu_parts(hidden)
    active = active.astype(BF)
    grad = (dot_t(pull, reduce) * slope).astype(BF)
    result_ref[...] += dot_n(active, reduce)
    back_ref[...] += dot_t(grad, expand)
    dexpand = dot_n(turned_ref[...], grad)
    half = dexpand_ref.shape[0]
    dexpand_far_ref[...] = jnp.where(low, dexpand[half:], dexpand[:half]).astype(BF)
    dexpand_ref[...] = jnp.where(low, dexpand[:half], dexpand[half:]).astype(BF)
    dbias_ref[...] = jnp.sum(grad.astype(F32), axis=0, keepdims=True)
    dreduce_ref[...] = dot_f(active, pull).astype(BF)


def mlp(img, entry_two, incoming, expand, expand_far, bias, reduce, reduce_far, *earlier, chunk=768):
    width = entry_two.shape[1]
    hidden = bias.shape[1]
    tokens = entry_two.shape[0]
    steps = hidden // chunk
    half = steps // 2

    def place(step, img):
        return (step + (1 - img[0]) * half) % steps

    def fixed(rows, columns):
        return pl.BlockSpec((rows, columns), lambda step, img: (0, 0))

    def across(rows):
        return pl.BlockSpec((rows, chunk), lambda step, img: (0, place(step, img)))

    return pl.pallas_call(
        ordered(mlp_kernel, 8, earlier),
        grid_spec=pltpu.PrefetchScalarGridSpec(
            num_scalar_prefetch=1,
            grid=(steps,),
            in_specs=[
                fixed(tokens, width), fixed(tokens, width), across(width // 2), across(width // 2), across(1),
                pl.BlockSpec((chunk, width), lambda step, img: (jnp.maximum(step - half, 0), 0)),
                pl.BlockSpec((chunk, width), lambda step, img: (jnp.minimum(step, half - 1), 0)),
            ] + [ANY] * len(earlier),
            out_specs=[
                fixed(tokens, width), fixed(tokens, width),
                pl.BlockSpec((chunk, width), lambda step, img: (place(step, img), 0)),
                across(width // 2), across(width // 2), across(1),
            ],
            scratch_shapes=[pltpu.VMEM((width, tokens), BF)],
        ),
        out_shape=[
            jax.ShapeDtypeStruct((tokens, width), F32),
            jax.ShapeDtypeStruct((tokens, width), F32),
            jax.ShapeDtypeStruct((hidden, width), BF),
            jax.ShapeDtypeStruct((width // 2, hidden), BF),
            jax.ShapeDtypeStruct((width // 2, hidden), BF),
            jax.ShapeDtypeStruct((1, hidden), F32),
        ],
        compiler_params=pltpu.CompilerParams(vmem_limit_bytes=VMEM_LIMIT),
        cost_estimate=cost(29),
        name="mlp",
    )(img.reshape(1), entry_two, incoming, expand, expand_far, bias, reduce, reduce_far, *earlier)


def project_kernel(img_ref, x_ref, mask_ref, rows_ref, near_ref, far_ref, bias_ref, entry_ref, joint_ref):
    @pl.when(pl.program_id(0) == 0)
    def _():
        value = x_ref[...].astype(F32)
        centred = value - jnp.mean(value, axis=1, keepdims=True)
        variance = jnp.mean(centred * centred, axis=1, keepdims=True)
        normed = centred * lax.rsqrt(variance + 1e-06) * rows_ref[0:1] + rows_ref[1:2]
        entry_ref[...] = (mask_ref[...] * normed).astype(BF)

    low = img_ref[0] == 0
    near, far = near_ref[...], far_ref[...]
    weight = jnp.concatenate([jnp.where(low, near, far), jnp.where(low, far, near)], 0)
    joint_ref[...] = (dot_n(entry_ref[...], weight) + bias_ref[...]).astype(BF)


def project(img, x, mask, rows, near, far, bias, *earlier, chunk=768):
    tokens, width = x.shape
    total = bias.shape[1]

    def across(rows):
        return pl.BlockSpec((rows, chunk), lambda step: (0, step))

    return pl.pallas_call(
        ordered(project_kernel, 7, earlier),
        grid=(total // chunk,),
        in_specs=[
            pl.BlockSpec(memory_space=pltpu.SMEM), whole((tokens, width)), whole((tokens, 1)),
            whole((8, width)), across(width // 2), across(width // 2), across(1),
        ] + [ANY] * len(earlier),
        out_specs=[whole((tokens, width)), across(tokens)],
        out_shape=[
            jax.ShapeDtypeStruct((tokens, width), BF), jax.ShapeDtypeStruct((tokens, total), BF),
        ],
        compiler_params=pltpu.CompilerParams(vmem_limit_bytes=VMEM_LIMIT),
        cost_estimate=cost(7),
        name="project",
    )(img.reshape(1), x, mask, rows, near, far, bias, *earlier)


def project_back_kernel(
    img_ref, x_ref, mask_ref, rows_ref, middle_ref, pull_ref,
    nq_ref, nk_ref, nv_ref, fq_ref, fk_ref, fv_ref, *refs,
):
    grad_ref, sums_ref, near_ref, far_ref = refs[-4:]
    step = pl.program_id(0)

    @pl.when(step == 0)
    def _():
        near_ref[...] = jnp.zeros_like(near_ref)
        far_ref[...] = jnp.zeros_like(far_ref)

    pull = pull_ref[...]
    near_ref[...] += dot_t(pull, jnp.concatenate([nq_ref[...], nk_ref[...], nv_ref[...]], 1))
    far_ref[...] += dot_t(pull, jnp.concatenate([fq_ref[...], fk_ref[...], fv_ref[...]], 1))

    @pl.when(step == pl.num_programs(0) - 1)
    def _():
        low = img_ref[0] == 0
        near, far = near_ref[...], far_ref[...]
        grad = jnp.concatenate([jnp.where(low, near, far), jnp.where(low, far, near)], 1) * mask_ref[...]
        value = x_ref[...].astype(F32)
        centred = value - jnp.mean(value, axis=1, keepdims=True)
        variance = jnp.mean(centred * centred, axis=1, keepdims=True)
        rstd = lax.rsqrt(variance + 1e-06)
        xhat = centred * rstd
        product = grad * xhat
        sums_ref[0:1] = jnp.sum(product, axis=0, keepdims=True)
        sums_ref[1:2] = jnp.sum(grad, axis=0, keepdims=True)
        pull = grad * rows_ref[0:1]
        back = pull - jnp.mean(pull, axis=1, keepdims=True)
        back = back - xhat * jnp.mean(pull * xhat, axis=1, keepdims=True)
        grad_ref[...] = (middle_ref[...] + rstd * back).astype(BF)


def project_back(img, x, mask, rows, grad_middle, grad_joint, near, far, *earlier):
    tokens, width = x.shape
    pairs = HEADS // 2
    half = width // 2

    def weight(part):
        return pl.BlockSpec((half, 128), lambda step: (0, part * pairs + step))

    return pl.pallas_call(
        project_back_kernel,
        grid=(pairs,),
        in_specs=[
            pl.BlockSpec(memory_space=pltpu.SMEM), whole((tokens, width)), whole((tokens, 1)),
            whole((8, width)), whole((tokens, width)),
            pl.BlockSpec((tokens, 384), lambda step: (0, step)),
            weight(0), weight(1), weight(2), weight(0), weight(1), weight(2),
        ] + [pl.BlockSpec(memory_space=pl.ANY)] * len(earlier),
        out_specs=[whole((tokens, width)), whole((2, width))],
        out_shape=[jax.ShapeDtypeStruct((tokens, width), BF), jax.ShapeDtypeStruct((2, width), F32)],
        scratch_shapes=[pltpu.VMEM((tokens, half), F32), pltpu.VMEM((tokens, half), F32)],
        compiler_params=pltpu.CompilerParams(vmem_limit_bytes=VMEM_LIMIT),
        cost_estimate=cost(11),
        name="project_back",
    )(
        img.reshape(1), x, mask, rows, grad_middle, grad_joint, near, near, near, far, far, far, *earlier
    )


def mix_kernel(img_ref, mixed_ref, near_ref, far_ref, rows_ref, x_ref, mask_ref, middle_ref, entry_ref):
    low = img_ref[0] == 0
    near, far = near_ref[...], far_ref[...]
    weight = jnp.concatenate([jnp.where(low, near, far), jnp.where(low, far, near)], 0)
    branch = dot_n(mixed_ref[...], weight) + rows_ref[2:3]
    middle = x_ref[...].astype(F32) + mask_ref[...] * branch
    middle_ref[...] = middle
    centred = middle - jnp.mean(middle, axis=1, keepdims=True)
    variance = jnp.mean(centred * centred, axis=1, keepdims=True)
    normed = centred * lax.rsqrt(variance + 1e-06) * rows_ref[4:5] + rows_ref[5:6]
    entry_ref[...] = normed.astype(BF)


def mix(img, mixed, near, far, rows, x, mask, *earlier):
    vmem = pl.BlockSpec(memory_space=pltpu.VMEM)
    return pl.pallas_call(
        ordered(mix_kernel, 7, earlier),
        in_specs=[pl.BlockSpec(memory_space=pltpu.SMEM)] + [vmem] * 6 + [ANY] * len(earlier),
        out_specs=[vmem] * 2,
        out_shape=[jax.ShapeDtypeStruct(x.shape, F32), jax.ShapeDtypeStruct(x.shape, BF)],
        compiler_params=pltpu.CompilerParams(vmem_limit_bytes=VMEM_LIMIT),
        cost_estimate=cost(4.6),
        name="mix",
    )(img.reshape(1), mixed, near, far, rows, x, mask, *earlier)


def mix_back_kernel(
    img_ref, back_ref, result_ref, middle_ref, incoming_ref, mask_ref, rows_ref, near_ref, far_ref, mixed_ref,
    grad_middle_ref, grad_mixed_ref, give_ref, keep_ref, out_ref, sums_ref,
):
    low = img_ref[0] == 0
    mask = mask_ref[...]
    middle = middle_ref[...]
    incoming = incoming_ref[...].astype(F32)
    out_ref[...] = (mask * (middle + (result_ref[...] + rows_ref[3:4]))).astype(BF)
    back = back_ref[...]
    centred = middle - jnp.mean(middle, axis=1, keepdims=True)
    variance = jnp.mean(centred * centred, axis=1, keepdims=True)
    rstd = lax.rsqrt(variance + 1e-06)
    xhat = centred * rstd
    sums_ref[1:2] = jnp.sum(back * xhat, axis=0, keepdims=True)
    sums_ref[2:3] = jnp.sum(back, axis=0, keepdims=True)
    sums_ref[3:4] = jnp.sum(incoming, axis=0, keepdims=True)
    pull = back * rows_ref[4:5]
    inner = pull - jnp.mean(pull, axis=1, keepdims=True)
    inner = inner - xhat * jnp.mean(pull * xhat, axis=1, keepdims=True)
    grad_middle = incoming + rstd * inner
    grad_middle_ref[...] = grad_middle
    branch = (mask * grad_middle).astype(BF)
    sums_ref[0:1] = jnp.sum(branch.astype(F32), axis=0, keepdims=True)
    near, far = near_ref[...], far_ref[...]
    weight = jnp.concatenate([jnp.where(low, near, far), jnp.where(low, far, near)], 0)
    grad_mixed_ref[...] = dot_t(branch, weight).astype(BF)
    half = keep_ref.shape[0]
    total = dot_f(mixed_ref[...], branch)
    give_ref[...] = jnp.where(low, total[half:], total[:half]).astype(BF)
    keep_ref[...] = jnp.where(low, total[:half], total[half:]).astype(BF)


def mix_back(img, back, result, middle, incoming, mask, rows, near, far, mixed, *earlier):
    tokens, width = middle.shape
    vmem = pl.BlockSpec(memory_space=pltpu.VMEM)
    return pl.pallas_call(
        ordered(mix_back_kernel, 10, earlier),
        in_specs=[pl.BlockSpec(memory_space=pltpu.SMEM)] + [vmem] * 9 + [ANY] * len(earlier),
        out_specs=[vmem] * 6,
        out_shape=[
            jax.ShapeDtypeStruct((tokens, width), F32), jax.ShapeDtypeStruct((tokens, width), BF),
            jax.ShapeDtypeStruct((width // 2, width), BF), jax.ShapeDtypeStruct((width // 2, width), BF),
            jax.ShapeDtypeStruct((tokens, width), BF), jax.ShapeDtypeStruct((4, width), F32),
        ],
        compiler_params=pltpu.CompilerParams(vmem_limit_bytes=VMEM_LIMIT),
        cost_estimate=cost(8.8),
        name="mix_back",
    )(img.reshape(1), back, result, middle, incoming, mask, rows, near, far, mixed, *earlier)


def entry_grads_kernel(img_ref, entry_ref, grad_ref, give_ref, keep_ref, turned_ref):
    @pl.when(pl.program_id(0) == 0)
    def _():
        turned_ref[...] = entry_ref[...].T

    low = img_ref[0] == 0
    half = keep_ref.shape[0]
    total = dot_n(turned_ref[...], grad_ref[...])
    give_ref[...] = jnp.where(low, total[half:], total[:half]).astype(BF)
    keep_ref[...] = jnp.where(low, total[:half], total[half:]).astype(BF)


def entry_grads(img, entry, grad, *earlier, chunk=768):
    tokens, width = entry.shape
    total = grad.shape[1]

    def across(rows):
        return pl.BlockSpec((rows, chunk), lambda step: (0, step))

    return pl.pallas_call(
        ordered(entry_grads_kernel, 3, earlier),
        grid=(total // chunk,),
        in_specs=[pl.BlockSpec(memory_space=pltpu.SMEM), whole((tokens, width)), across(tokens)]
        + [ANY] * len(earlier),
        out_specs=[across(width // 2), across(width // 2)],
        out_shape=[
            jax.ShapeDtypeStruct((width // 2, total), BF), jax.ShapeDtypeStruct((width // 2, total), BF),
        ],
        scratch_shapes=[pltpu.VMEM((width, tokens), BF)],
        compiler_params=pltpu.CompilerParams(vmem_limit_bytes=VMEM_LIMIT),
        cost_estimate=cost(7.2),
        name="entry_grads",
    )(img.reshape(1), entry, grad, *earlier)


def sums_kernel(norm_ref, joint_ref, mix_ref, expand_ref, tables_ref, out_ref):
    width = norm_ref.shape[1]
    out_ref[0:2] = norm_ref[...]
    out_ref[2:4] = joint_ref[...]
    out_ref[4:8] = mix_ref[...]
    for part in range(4):
        out_ref[8 + part : 9 + part] = expand_ref[:, part * width : (part + 1) * width]
    out_ref[12:] = jnp.zeros((out_ref.shape[0] - 12, width), F32)
    total = tables_ref[0]
    for pair in range(1, tables_ref.shape[0]):
        total = total + tables_ref[pair]
    height = total[0:32, :64] + total[32:64, 64:]
    across = total[64:96, :64] + total[96:128, 64:]
    both = jnp.concatenate([height, across], 1)
    for part in range(4):
        out_ref[16:24, part * 128 : (part + 1) * 128] = both[part * 8 : (part + 1) * 8]


def sums(norm, joint, mixed, expand, tables, *earlier):
    vmem = pl.BlockSpec(memory_space=pltpu.VMEM)
    return pl.pallas_call(
        ordered(sums_kernel, 5, earlier),
        in_specs=[vmem] * 5 + [ANY] * len(earlier),
        out_specs=vmem,
        out_shape=jax.ShapeDtypeStruct((24, norm.shape[1]), F32),
        cost_estimate=cost(1.9),
        name="sums",
    )(norm, joint, mixed, expand, tables, *earlier)


def add_kernel(one_ref, two_ref, out_ref):
    out_ref[...] = one_ref[...] + two_ref[...]


def add(one, two, *earlier):
    vmem = pl.BlockSpec(memory_space=pltpu.VMEM)
    return pl.pallas_call(
        ordered(add_kernel, 2, earlier),
        in_specs=[vmem] * 2 + [ANY] * len(earlier),
        out_specs=vmem,
        out_shape=jax.ShapeDtypeStruct(one.shape, F32),
        cost_estimate=cost(1),
        name="add",
    )(one, two, *earlier)


def share_kernel(block, slots, place_ref, *refs):
    parts, outs = refs[:-10], refs[-10:]
    depth = len(parts)
    total = None
    for level in range(depth):
        found = parts[0][...]
        for step in range(1, depth):
            found = jnp.where(lax.rem(place_ref[1] - level + depth, depth) == step, parts[step][...], found)
        total = found if total is None else total + found
    width = total.shape[1]
    begin = place_ref[0] * block

    def own(array, size, first):
        return pltpu.roll(array, lax.rem(2 * array.shape[1] - first, array.shape[1]), 1)[:, :size]

    for number, row in enumerate((0, 1, 4, 5, 6, 7)):
        outs[number][...] = own(total[row : row + 1], block, begin)
    joint = jnp.concatenate([total[2:3], total[3:4]], 1)
    outs[6][...] = own(joint, 2 * block, 2 * begin)
    hidden = jnp.concatenate([total[8 + part : 9 + part] for part in range(4)], 1)
    outs[7][...] = own(hidden, 4 * block, 4 * begin)
    for slot in range(slots):
        place = slots - 1 - slot
        line = total[16 + place % 8 : 17 + place % 8, place // 8 * 128 : place // 8 * 128 + 128]
        outs[8][slot : slot + 1] = line[:, :64]
        outs[9][slot : slot + 1] = line[:, 64:]


def share(number, parts, block, slots, *earlier):
    vmem = pl.BlockSpec(memory_space=pltpu.VMEM)
    shapes = [(1, block)] * 6 + [(1, 2 * block), (1, 4 * block)] + [(slots, HEAD_DIM)] * 2
    return pl.pallas_call(
        ordered(partial(share_kernel, block, slots), 1 + len(parts), earlier),
        in_specs=[pl.BlockSpec(memory_space=pltpu.SMEM)] + [vmem] * len(parts) + [ANY] * len(earlier),
        out_specs=[vmem] * len(shapes),
        out_shape=[jax.ShapeDtypeStruct(shape, F32) for shape in shapes],
        cost_estimate=cost(1.8),
        name="share",
    )(number, *parts, *earlier)


def place_kernel(depth, *refs):
    parts, triple_ref = refs[:depth], refs[depth]
    pairs = HEADS // 2
    for pair in range(pairs):
        for part in range(3):
            begin, spot = (pair * 3 + part) * 128, (part * pairs + pair) * 128
            value = parts[0][:, begin : begin + 128]
            for other in parts[1:]:
                value = value + other[:, begin : begin + 128].astype(F32)
            triple_ref[:, spot : spot + 128] = value


def place(parts, *earlier):
    vmem = pl.BlockSpec(memory_space=pltpu.VMEM)
    return pl.pallas_call(
        ordered(partial(place_kernel, len(parts)), len(parts), earlier),
        in_specs=[vmem] * len(parts) + [ANY] * len(earlier),
        out_specs=vmem,
        out_shape=jax.ShapeDtypeStruct(parts[0].shape, F32),
        compiler_params=pltpu.CompilerParams(vmem_limit_bytes=VMEM_LIMIT),
        name="place",
    )(*parts, *earlier)


def settle_kernel(cut, *refs):
    parts, (left_ref, right_ref) = refs[:-2], refs[-2:]
    for out_ref, lanes in ((left_ref, slice(0, cut)), (right_ref, slice(cut, None))):
        value = parts[0][:, lanes]
        for part in parts[1:]:
            value = value + part[:, lanes].astype(F32)
        out_ref[...] = value


def settle(parts, cut, *earlier):
    vmem = pl.BlockSpec(memory_space=pltpu.VMEM)
    rows, columns = parts[0].shape
    return pl.pallas_call(
        ordered(partial(settle_kernel, cut), len(parts), earlier),
        in_specs=[vmem] * len(parts) + [ANY] * len(earlier),
        out_specs=[vmem] * 2,
        out_shape=[
            jax.ShapeDtypeStruct((rows, cut), F32), jax.ShapeDtypeStruct((rows, columns - cut), F32),
        ],
        cost_estimate=cost(2),
        name="settle",
    )(*parts, *earlier)


def rows_place():
    me = lax.axis_index("rows")
    return me % 2, me // 2 % 2, me // 4


def swap_rows(block, bit):
    count = lax.axis_size("rows")
    return lax.ppermute(block, "rows", [(place, place ^ (1 << bit)) for place in range(count)])


def swap_img(block):
    return lax.ppermute(block, "img", [(0, 1), (1, 0)])


def shift_depth(block, step):
    count = lax.axis_size("rows")
    return lax.ppermute(
        block, "rows", [(place, (place + 4 * step) % count) for place in range(count)]
    )


def in_order(bit, mine, other, axis):
    return jnp.where(
        bit == 0, jnp.stack([mine, other], axis), jnp.stack([other, mine], axis)
    )


def gather_depth(block):
    depth = lax.axis_size("rows") // 4
    place = rows_place()[2]
    parts = [block] + [shift_depth(block, step) for step in range(1, depth)]
    turned = [parts[-step % depth] for step in range(depth)]
    twice = jnp.stack(turned + turned)
    return lax.dynamic_slice_in_dim(twice, depth - place, depth, 0)


def halves(block):
    cut = block.shape[-1] // 256 * 128
    return block[..., :cut], block[..., cut:]


def join_one_kernel(depth, count, bits_ref, *refs):
    place = bits_ref[2]
    ins, outs = refs[: depth * count], refs[len(refs) - 2 * count :]
    for number in range(count):
        first, second = outs[2 * number : 2 * number + 2]
        cut = first.shape[-1]
        for step in range(depth):
            spot = lax.rem(place - step + depth, depth)
            part = ins[number * depth + step][...]
            first[spot] = part[:, :cut]
            second[spot] = part[:, cut:]


def join_two_kernel(count, bits_ref, *refs):
    x, y = bits_ref[0], bits_ref[1]
    ins, outs = refs[: 4 * count], refs[len(refs) - 2 * count :]
    for number in range(count):
        first, first_far, second, second_far = ins[4 * number : 4 * number + 4]
        joined, joined_two = outs[2 * number : 2 * number + 2]
        for level in range(first.shape[0]):
            joined[level, x] = first[level]
            joined[level, 1 - x] = first_far[level]
            joined_two[level, y] = second[level]
            joined_two[level, 1 - y] = second_far[level]


def join_three_kernel(splits, bits_ref, first, first_far, second, second_far, *refs):
    x, y = bits_ref[0], bits_ref[1]
    outs = refs[len(refs) - len(splits) :]
    cut = first.shape[-1]
    begin = 0
    for size, joined in zip(splits, outs):
        rows = slice(begin, begin + size)
        for level in range(first.shape[0]):
            for side in range(2):
                joined[level, y, side, :, :cut] = first[level, side, rows]
                joined[level, 1 - y, side, :, :cut] = first_far[level, side, rows]
                joined[level, side, x, :, cut:] = second[level, side, rows]
                joined[level, side, 1 - x, :, cut:] = second_far[level, side, rows]
        begin += size


def carry_kernel(weight_ref, *refs):
    out_ref = refs[-1]
    columns = weight_ref.shape[1]
    out_ref[:, :columns] = weight_ref[...]
    pre_gain, pre_bias, triple_bias, output_bias, post_gain, post_bias, expand_bias, reduce_bias = [
        ref[...].astype(F32) for ref in refs[:8]
    ]
    lines = []
    for parts in ((pre_gain, pre_bias, triple_bias, output_bias), (expand_bias, reduce_bias), (post_gain, post_bias)):
        size = sum(part.shape[1] for part in parts)
        lines.append(jnp.concatenate(parts + (jnp.zeros((1, 128 - size), F32),), 1))
    rest = out_ref.shape[0] - len(lines)
    if rest:
        lines.append(jnp.zeros((rest, 128), F32))
    out_ref[:, columns:] = jnp.concatenate(lines, 0).astype(out_ref.dtype)


def carry(weight, vectors, *earlier):
    vmem = pl.BlockSpec(memory_space=pltpu.VMEM)
    return pl.pallas_call(
        ordered(carry_kernel, 1 + len(vectors), earlier),
        in_specs=[vmem] * (1 + len(vectors)) + [ANY] * len(earlier),
        out_specs=vmem,
        out_shape=jax.ShapeDtypeStruct((weight.shape[0], weight.shape[1] + 128), weight.dtype),
        cost_estimate=cost(2),
        name="carry",
    )(weight, *[vector.reshape(1, -1) for vector in vectors], *earlier)


def spread_kernel(block, img_ref, near_ref, far_ref, rows_ref, offsets_ref, fill_ref, expand_ref):
    low = img_ref[0] == 0
    near, far = near_ref[...].astype(F32), far_ref[...].astype(F32)
    count = near.shape[0] // block
    width = rows_ref.shape[1]
    rows_ref[6:8] = jnp.zeros((2, width), F32)
    offsets_ref[...] = jnp.zeros_like(offsets_ref)
    plan = (
        (0, 0, 1, rows_ref, 0), (0, 1, 1, rows_ref, 1), (0, 4, 1, rows_ref, 2),
        (1, 4, 1, rows_ref, 3), (2, 0, 1, rows_ref, 4), (2, 1, 1, rows_ref, 5),
        (1, 0, 4, expand_ref, 0),
    )
    for half in range(2):
        part = jnp.where(low, near, far) if half == 0 else jnp.where(low, far, near)
        for number in range(count):
            spot = half * count + number
            lines = part[number * block : number * block + 3]
            for line, first, size, out_ref, row in plan:
                size = size * block
                out_ref[row : row + 1, spot * size : (spot + 1) * size] = lines[
                    line : line + 1, first * block : first * block + size
                ]
            size = 2 * block
            begin = spot * size + (width if half else 0)
            offsets_ref[:, begin : begin + size] = lines[0:1, size : 2 * size]
    fill_ref[...] = offsets_ref[:, 2 * width :].astype(BF)


def spread(img, near, far, block, *earlier):
    width = 2 * near.shape[0]
    place = near.shape[1] // 128 - 1
    last = pl.BlockSpec((near.shape[0], 128), lambda step: (0, place))
    shapes = [((8, width), F32), ((1, 3 * width), F32), ((1, width), BF), ((1, 4 * width), F32)]
    return pl.pallas_call(
        ordered(partial(spread_kernel, block), 3, earlier),
        grid=(1,),
        in_specs=[pl.BlockSpec(memory_space=pltpu.SMEM), last, last] + [ANY] * len(earlier),
        out_specs=[whole(shape) for shape, _ in shapes],
        out_shape=[jax.ShapeDtypeStruct(shape, kind) for shape, kind in shapes],
        cost_estimate=cost(2),
        name="spread",
    )(img.reshape(1), near, far, *earlier)


def stack_kernel(*refs):
    refs[-1][...] = jnp.concatenate([ref[...].astype(F32) for ref in refs[:-1]], 0).astype(BF)


def stack(blocks, *earlier):
    vmem = pl.BlockSpec(memory_space=pltpu.VMEM)
    rows = sum(block.shape[0] for block in blocks)
    return pl.pallas_call(
        ordered(stack_kernel, len(blocks), earlier),
        in_specs=[vmem] * len(blocks) + [ANY] * len(earlier),
        out_specs=vmem,
        out_shape=jax.ShapeDtypeStruct((rows,) + blocks[0].shape[1:], BF),
        cost_estimate=cost(1.6),
        name="stack",
    )(*blocks, *earlier)


class Gather:
    def __init__(self, block, splits=None):
        self.depth = lax.axis_size("rows") // 4
        self.bits = jnp.stack(rows_place()).astype(jnp.int32)
        self.rows, self.columns = block.shape
        self.splits = splits or (self.rows,)
        self.cut = self.columns // 256 * 128
        self.held = [block]

    def call(self, kernel, name, values, shapes, earlier):
        vmem = pl.BlockSpec(memory_space=pltpu.VMEM)
        return pl.pallas_call(
            kernel,
            in_specs=[pl.BlockSpec(memory_space=pltpu.SMEM)] + [vmem] * len(values) + [ANY] * len(earlier),
            out_specs=[vmem] * len(shapes),
            out_shape=[jax.ShapeDtypeStruct(shape, BF) for shape in shapes],
            compiler_params=pltpu.CompilerParams(vmem_limit_bytes=VMEM_LIMIT),
            cost_estimate=cost(2.3),
            name=name,
        )(self.bits, *values, *earlier)

    def shapes(self, *lead):
        return [lead + (self.rows, self.cut), lead + (self.rows, self.columns - self.cut)]

    def shift(self):
        self.far = [shift_depth(self.held[0], step) for step in range(1, self.depth)]

    def join_one(self, *earlier):
        kernel = partial(join_one_kernel, self.depth, 1)
        self.held = self.call(kernel, "join_one", self.held + self.far, self.shapes(self.depth), earlier)
        return self.held

    def swap_near(self):
        self.far = [swap_rows(part, number) for number, part in enumerate(self.held)]

    def swap_far(self):
        self.far = [swap_rows(part, 1 - number) for number, part in enumerate(self.held)]

    def pairs(self):
        return [array for pair in zip(self.held, self.far) for array in pair]

    def join_two(self, *earlier):
        kernel = partial(join_two_kernel, 1)
        self.held = self.call(kernel, "join_two", self.pairs(), self.shapes(self.depth, 2), earlier)
        return self.held

    def join_three(self, *earlier):
        shapes = [(self.depth, 2, 2, rows, self.columns) for rows in self.splits]
        kernel = partial(join_three_kernel, self.splits)
        self.held = self.call(kernel, "join_three", self.pairs(), shapes, earlier)
        return self.held

    def swap_cores(self):
        flat = [block.reshape(-1, self.columns) for block in self.held]
        return [(block, swap_img(block)) for block in flat]


def fold_one_kernel(count, bits_ref, *refs):
    ins = refs[: 2 * count]
    a_give, a_keep, b_give, b_keep = refs[-4:]
    x, y = bits_ref[0], bits_ref[1]
    cut = a_keep.shape[-1]
    begin = 0
    for near_ref, far_ref in zip(ins[:count], ins[count:]):
        columns = near_ref.shape[-1]
        pieces = [(max(begin, 0), min(begin + columns, cut), True), (max(begin, cut), begin + columns, False)]
        for low, high, first in pieces:
            if low >= high:
                continue
            here = slice(low - begin, high - begin)
            there = slice(low, high) if first else slice(low - cut, high - cut)
            for level in range(near_ref.shape[0]):
                for side in range(2):
                    if first:
                        kept, given = (level, side, x), (level, side, 1 - x)
                    else:
                        kept, given = (level, y, side), (level, 1 - y, side)
                    keep, give = (a_keep, a_give) if first else (b_keep, b_give)
                    value = near_ref[kept + (slice(None), here)].astype(F32) + far_ref[kept + (slice(None), here)].astype(F32)
                    keep[level, side, :, there] = value
                    value = near_ref[given + (slice(None), here)].astype(F32) + far_ref[given + (slice(None), here)].astype(F32)
                    give[level, side, :, there] = value.astype(BF)
        begin += columns


def fold_two_kernel(bits_ref, a_near, a_far, b_near, b_far, *refs):
    a_give, a_keep, b_give, b_keep = refs[-4:]
    x, y = bits_ref[0], bits_ref[1]
    for level in range(a_near.shape[0]):
        a_keep[level] = a_near[level, y] + a_far[level, y].astype(F32)
        a_give[level] = (a_near[level, 1 - y] + a_far[level, 1 - y].astype(F32)).astype(BF)
        b_keep[level] = b_near[level, x] + b_far[level, x].astype(F32)
        b_give[level] = (b_near[level, 1 - x] + b_far[level, 1 - x].astype(F32)).astype(BF)


def fold_three_kernel(depth, bits_ref, a_near, a_far, b_near, b_far, *refs):
    place = bits_ref[2]
    keep, gives = refs[-depth], refs[len(refs) - depth + 1 :]
    cut = a_near.shape[-1]
    for step, out in enumerate((keep,) + tuple(gives)):
        spot = lax.rem(place + step, depth)
        out[:, :cut] = (a_near[spot] + a_far[spot].astype(F32)).astype(out.dtype)
        out[:, cut:] = (b_near[spot] + b_far[spot].astype(F32)).astype(out.dtype)


def fold_call(kernel, name, bits, values, outs, earlier):
    vmem = pl.BlockSpec(memory_space=pltpu.VMEM)
    return pl.pallas_call(
        kernel,
        in_specs=[pl.BlockSpec(memory_space=pltpu.SMEM)] + [vmem] * len(values)
        + [pl.BlockSpec(memory_space=pl.ANY)] * len(earlier),
        out_specs=[vmem] * len(outs),
        out_shape=[jax.ShapeDtypeStruct(shape, kind) for shape, kind in outs],
        compiler_params=pltpu.CompilerParams(vmem_limit_bytes=VMEM_LIMIT),
        cost_estimate=cost(2.3),
        name=name,
    )(bits, *values, *earlier)


class Scatter:
    def __init__(self, give, keep):
        self.depth = lax.axis_size("rows") // 4
        self.columns = sum(part.shape[-1] for part in keep)
        self.cut = self.columns // 256 * 128
        self.bits = jnp.stack(rows_place()).astype(jnp.int32)
        self.shape = (self.depth, 2, 2, keep[0].shape[0] // lax.axis_size("rows"), -1)
        self.give, self.keep = give, keep

    def swap_near(self):
        self.far = [swap_img(part) for part in self.give]

    def outs(self, *lead):
        rows = self.shape[3]
        first, second = lead + (rows, self.cut), lead + (rows, self.columns - self.cut)
        return [(first, BF), (first, F32), (second, BF), (second, F32)]

    def fold_one(self, *earlier):
        values = [part.reshape(self.shape) for part in list(self.keep) + self.far]
        kernel = partial(fold_one_kernel, len(self.keep))
        self.out = fold_call(kernel, "fold_one", self.bits, values, self.outs(self.depth, 2), earlier)
        return self.out

    def swap_middle(self):
        self.far = swap_rows(self.out[0], 0), swap_rows(self.out[2], 1)
        return self.far

    def fold_two(self, *earlier):
        values = [self.out[1], self.far[0], self.out[3], self.far[1]]
        self.out = fold_call(
            fold_two_kernel, "fold_two", self.bits, values, self.outs(self.depth), earlier
        )
        return self.out

    def swap_far(self):
        self.far = swap_rows(self.out[0], 1), swap_rows(self.out[2], 0)
        return self.far

    def fold_three(self, *earlier):
        depth, rows = self.depth, self.shape[3]
        block = (rows, self.columns)
        vmem = pl.BlockSpec(memory_space=pltpu.VMEM)
        self.out = pl.pallas_call(
            partial(fold_three_kernel, depth),
            in_specs=[pl.BlockSpec(memory_space=pltpu.SMEM)] + [vmem] * 4
            + [pl.BlockSpec(memory_space=pl.ANY)] * len(earlier),
            out_specs=[vmem] * depth,
            out_shape=[jax.ShapeDtypeStruct(block, F32)]
            + [jax.ShapeDtypeStruct(block, BF) for _ in range(depth - 1)],
            compiler_params=pltpu.CompilerParams(vmem_limit_bytes=VMEM_LIMIT),
            cost_estimate=cost(2.5),
            name="fold_three",
        )(self.bits, self.out[1], self.far[0], self.out[3], self.far[1], *earlier)
        return self.out

    def swap_last(self):
        return [self.out[0]] + [shift_depth(self.out[step], step) for step in range(1, self.depth)]

    def last(self):
        parts = self.swap_last()
        return sum((part.astype(F32) for part in parts[1:]), parts[0])


def sum_all(value):
    value = value + swap_img(value)
    value = value + swap_rows(value, 0)
    value = value + swap_rows(value, 1)
    return jnp.sum(gather_depth(value), axis=0)


def layer_norm(value, gain, bias):
    center = jnp.mean(value, axis=-1, keepdims=True)
    centred = value - center
    variance = jnp.mean(centred * centred, axis=-1, keepdims=True)
    return centred * lax.rsqrt(variance + 1e-06) * gain + bias


def to_odd(block):
    count = lax.axis_size("rows")
    return lax.ppermute(block, "rows", [(place, place + 1) for place in range(0, count, 2)])


def to_even(block):
    count = lax.axis_size("rows")
    return lax.ppermute(block, "rows", [(place + 1, place) for place in range(0, count, 2)])


def local(
    tokens,
    extent,
    pre_gain,
    pre_bias,
    triple_weight,
    triple_bias,
    height_table,
    width_table,
    output_weight,
    output_bias,
    post_gain,
    post_bias,
    expand_weight,
    expand_bias,
    reduce_weight,
    reduce_bias,
    cotangent,
):
    rows_dev, _, width = tokens.shape
    moved = rows_dev - WIN
    block = pre_gain.shape[0]
    parity = lax.axis_index("rows") % 2
    image = lax.axis_index("img") * (lax.axis_size("rows") // 2) + lax.axis_index("rows") // 2
    sides = lax.dynamic_slice(extent, (image, 0), (1, 2))

    img = lax.axis_index("img")
    last = []

    def then(result):
        arrays = result if isinstance(result, (list, tuple)) else [result]
        last[:] = [min(arrays, key=lambda array: array.size)]
        return result

    band_row, column_of = jnp.asarray(BAND_ROW), jnp.asarray(COLUMN)
    real_row = jnp.where(parity == 0, band_row, band_row + WIN)
    inside = (real_row < sides[0, 0]) & (column_of < sides[0, 1]) & (jnp.asarray(VALID) == 1)
    inside = inside & ((parity == 1) | (band_row < WIN))
    mask = inside.astype(F32)[:, None]
    table = reversed_table(height_table, width_table)
    vectors = (
        pre_gain, pre_bias, triple_bias, output_bias, post_gain, post_bias, expand_bias, reduce_bias,
    )

    far_tokens = to_odd(tokens[WIN:, :REAL])
    one = Gather(then(carry(triple_weight, vectors)))
    one.shift()
    two = Gather(
        then(stack([reduce_weight, output_weight], *last)), (reduce_weight.shape[0], block)
    )
    then(one.join_one(*last))
    one.swap_near()
    two.shift()
    x = then(pack(parity, tokens, far_tokens, mask, False, *last))
    three = Gather(then(stack([expand_weight], *last)))
    then(one.join_two(*last, *two.far[::2]))
    one.swap_far()
    far_pulls = to_odd(cotangent[WIN:, :REAL])
    then(one.join_three(*last, *two.far[1::2]))
    (triple_pair,) = one.swap_cores()
    then(two.join_one(*last))
    two.swap_near()
    rows, offsets, fill, hidden_bias = then(spread(img, *triple_pair, block, *last))
    three.shift()
    incoming = then(pack(parity, cotangent, far_pulls, mask, True, *last))
    then(two.join_two(*last))
    two.swap_far()
    entry, joint = then(project(img, x, mask, rows, *triple_pair, offsets, *last))
    heads = then(attend(joint, fill, table, 0, 3, (), *last, *three.far[::2]))
    then(three.join_one(*last))
    three.swap_near()
    mixed, lse, features = then(attend(joint, fill, table, 3, 3, heads, *last))
    then(two.join_three(*last))
    reduce_pair, output_pair = two.swap_cores()
    then(three.join_two(*last))
    three.swap_far()
    middle, entry_two = then(mix(img, mixed, *output_pair, rows, x, mask, *last))
    then(three.join_three(*last))
    (expand_pair,) = three.swap_cores()

    result, grad_entry_two, reduce_grad, expand_far, expand_near, hidden_sums = then(
        mlp(img, entry_two, incoming, *expand_pair, hidden_bias, *reduce_pair, *last)
    )
    reduce_shard = lax.psum_scatter(reduce_grad, ("img", "rows"), scatter_dimension=0, tiled=True).astype(F32)
    grad_middle, grad_mixed, output_far, output_near, out_win, mix_sums = then(
        mix_back(img, grad_entry_two, result, middle, incoming, mask, rows, *output_pair, mixed, *last)
    )
    first_sum = Scatter([expand_far, output_far], [expand_near, output_near])
    first_sum.swap_near()
    then(first_sum.fold_one(*last))
    first_sum.swap_middle()
    out_rows = to_even(then(send_rows(out_win, moved, *last)))
    grad_joint, tables, joint_sums = then(
        attend_back(joint, grad_mixed, lse, features, fill, table, 0, HEADS // 2, *last)
    )
    joint_far, joint_near = then(entry_grads(img, entry, grad_joint, *last))
    last_sum = Scatter([joint_far], [joint_near])
    last_sum.swap_near()
    then(first_sum.fold_two(*last))
    first_sum.swap_far()
    grad_win, norm_sums = then(
        project_back(img, x, mask, rows, grad_middle, grad_joint, *triple_pair, *last)
    )
    then(last_sum.fold_one(*last, out_rows))
    last_sum.swap_middle()
    then(first_sum.fold_three(*last))
    first_parts = first_sum.swap_last()
    small = then(sums(norm_sums, joint_sums, mix_sums, hidden_sums, tables, *last))
    grad_rows = to_even(then(send_rows(grad_win, moved, *last)))
    small = then(add(small, swap_img(small), *last))
    block_output = then(unpack(parity, out_win, out_rows, tokens.shape, *last))
    then(last_sum.fold_two(*last))
    last_sum.swap_far()
    small = then(add(small, swap_rows(small, 0), *last))
    expand_shard, output_shard = then(settle(first_parts, expand_far.shape[1], *last))
    then(last_sum.fold_three(*last))
    last_parts = last_sum.swap_last()
    small = then(add(small, swap_rows(small, 1), *last))
    depths = [small] + [shift_depth(small, step) for step in range(1, lax.axis_size("rows") // 4)]
    input_grad = then(unpack(parity, grad_win, grad_rows, tokens.shape, *last))
    triple_shard = then(place(last_parts, *last))
    number = img * lax.axis_size("rows") + lax.axis_index("rows")
    number = jnp.stack([number, rows_place()[2]]).astype(jnp.int32)
    shares = share(number, depths, block, height_table.shape[0], *last)
    pre_gain_grad, pre_bias_grad, output_bias_grad, post_gain_grad, post_bias_grad, reduce_bias_grad = [
        array.reshape(-1) for array in shares[:6]
    ]
    return (
        block_output,
        input_grad,
        pre_gain_grad,
        pre_bias_grad,
        triple_shard,
        shares[6].reshape(-1),
        shares[8],
        shares[9],
        output_shard,
        output_bias_grad,
        post_gain_grad,
        post_bias_grad,
        expand_shard,
        shares[7].reshape(-1),
        reduce_shard,
        reduce_bias_grad,
    )


def solution(mesh):
    split = P(("img", "rows"))
    flat = P(("img", "rows"), None)
    grids = P(("img", "rows"), None, None)
    in_specs = (
        grids, P(), split, split, flat, split, P(), P(), flat, split, split, split, flat, split,
        flat, split, grids,
    )
    out_specs = (
        grids, grids, split, split, flat, split, P(), P(), flat, split, split, split, flat, split,
        flat, split,
    )
    return jax.shard_map(local, mesh=mesh, in_specs=in_specs, out_specs=out_specs, check_vma=False)
```

time: 468 us -> 319 us (0.68); the launches traced: 460 us -> 318 us
  Pallas kernels: 74.5 us -> 173 us
  matrix products: 76.8 us -> 0 us
  waiting for transfers between devices: 102 us -> 33.4 us
  other arithmetic: 69.7 us -> 4.84 us
  local copies, waits for them, and re-layouts: 59.1 us -> 26.4 us
  between operations: 2.25 us -> 14.6 us
  starting transfers between devices: 75.2 us -> 65 us
    pallas_call x8 -> x41, Pallas kernels: 74.5 us -> 173 us  [the longest x1 29.1 us: mlp(): pl.pallas_call(ordered(mlp_kernel, 8, earlier), grid_spec=pltpu.PrefetchS...]
    dot_general x12 -> x0, matrix products: 76.8 us -> none  [the longest x4 33.3 us: dot_n(): lax.dot_general(left, right, (((1,), (0,)), ((), ())), preferred_element_...]
    ppermute x26 -> x22, waiting for transfers between devices: 70.4 us -> 13.8 us  [swap_rows(): lax.ppermute(block, 'rows', [(place, place ^ 1 << bit) for place in range...]
    ppermute x21 -> x18, waiting for transfers between devices: 31.6 us -> 12.9 us  [shift_depth(): lax.ppermute(block, 'rows', [(place, (place + 4 * step) % count) for plac...]
    concatenate x8 -> x0, other arithmetic: 17.2 us -> none  [the longest x1 8.85 us: local(): jnp.concatenate([output_weight_grad, expand_weight_grad], 1)]
    convert_element_type x21 -> x1, other arithmetic: 18.5 us -> 1.64 us  [local(): lax.psum_scatter(reduce_grad, ('img', 'rows'), scatter_dimension=0, tiled...]
    select_n x21 -> x0, other arithmetic: 15.3 us -> none  [in_order(): jnp.where(bit == 0, jnp.stack([mine, other], axis), jnp.stack([other, min...]
    ppermute x26 -> x22, starting transfers between devices: 36.4 us -> 21.8 us  [swap_rows(): lax.ppermute(block, 'rows', [(place, place ^ 1 << bit) for place in range...]
  transfers between devices with their start and end apart: 58 -> 53, of which waited for: 23 -> 11; matrix products, arithmetic and copies ran while one was open for 25% -> 2% of each run, Pallas kernels for 8% -> 43%
where the time goes in v2:
time: 319 us; the launch traced here: 318 us
  Pallas kernels  173 us (54%)
  starting transfers between devices  65 us (20%)
  waiting for transfers between devices  33.4 us (10%)
  local copies, waits for them, and re-layouts  26.4 us (8%)
  between operations  14.6 us (5%)
  other arithmetic  4.84 us (2%)
    ppermute x18, starting transfers between devices, shift_depth(): lax.ppermute(block, 'rows', [(place, (place + 4 * step) % count) for plac...  33.4 us
    pallas_call x1, Pallas kernels, mlp(): pl.pallas_call(ordered(mlp_kernel, 8, earlier), grid_spec=pltpu.PrefetchS...  29.1 us
    pallas_call x9, Pallas kernels, call(): pl.pallas_call(kernel, in_specs=[pl.BlockSpec(memory_space=pltpu.SMEM)] +...  22.9 us
    unnamed x134, local copies, waits for them, and re-layouts  22.8 us
    ppermute x22, starting transfers between devices, swap_rows(): lax.ppermute(block, 'rows', [(place, place ^ 1 << bit) for place in range...  21.8 us
    pallas_call x4, Pallas kernels, fold_call(): pl.pallas_call(kernel, in_specs=[pl.BlockSpec(memory_space=pltpu.SMEM)] +...  15.4 us
    pallas_call x1, Pallas kernels, attend_back(): pl.pallas_call(kernel, grid=(count,), in_specs=[column(begin), column(pai...  14.6 us
    ppermute x22, waiting for transfers between devices, swap_rows(): lax.ppermute(block, 'rows', [(place, place ^ 1 << bit) for place in range...  13.8 us
  transfers between devices with their start and end apart: 53, of which 11 were waited for; matrix products, arithmetic and copies ran while one was open for 2% of the time, Pallas kernels for 43%

profile of v2, /device:TPU:0, one launch (start us, length us, event | category | flops | bytes accessed | tf_op | source)
XLA Modules:
  0.0 317.8 jit_solution(555788788577453921)
XLA Ops:
  9.0 5.1 %collective-permute-start.3 = (bf16[24,2432]{1,0:T(8,128)(2,1)}, bf16[24,2432]{1,0:T(8,128)(2,1)S(1)}, u32[]{:S(2)}, u32[]{:S(2)}) collective-permute-start(bf16[24,2432]{1,0:T(8,128)(2,1)} %carry.1.refs_2_.refs_0_), channel_id=1, source_target_pairs={{0,12},{1,13},{2,14},{3,15},{4,0},{5,1},{6,2},{7,3},{8,4},{9,5},{1... | collective-permute-start | bytes 350216 | tf_op jit(solution)/shard_map/ppermute | solution.py:909
  20.5 3.4 %collective-permute-start = (bf16[7,32,768]{2,1,0:T(8,128)(2,1)S(1)}, bf16[7,32,768]{2,1,0:T(8,128)(2,1)S(1)}, u32[]{:S(2)}, u32[]{:S(2)}) collective-permute-start(bf16[7,32,768]{2,1,0:T(8,128)(2,1)S(1)} %slice.12), channel_id=1, source_target_pairs={{0,1},{2,3},{4,5},{6,7},{8,9},{10,11},{12,13},{14,15},{16,17},{18,... | collective-permute-start | bytes 1032200 | tf_op jit(solution)/shard_map/ppermute | solution.py:1264
  43.7 3.6 %collective-permute-start.10 = (bf16[120,768]{1,0:T(8,128)(2,1)S(1)}, bf16[120,768]{1,0:T(8,128)(2,1)S(1)}, u32[]{:S(2)}, u32[]{:S(2)}) collective-permute-start(bf16[120,768]{1,0:T(8,128)(2,1)S(1)} %copy-done.42), channel_id=1, source_target_pairs={{0,8},{1,9},{2,10},{3,11},{4,12},{5,13},{6,14},{7,15},{8,0},{9,1},... | collective-permute-start | bytes 552968 | tf_op jit(solution)/shard_map/ppermute | solution.py:909
  47.2 6.0 %collective-permute-done.10.refs_1_.refs_2_ = bf16[120,768]{1,0:T(8,128)(2,1)S(1)} collective-permute-done((bf16[120,768]{1,0:T(8,128)(2,1)S(1)}, bf16[120,768]{1,0:T(8,128)(2,1)S(1)}, u32[]{:S(2)}, u32[]{:S(2)}) %collective-permute-start.10) | collective-permute-done | bytes 184352 | tf_op jit(solution)/shard_map/ppermute | solution.py:909
  58.7 3.2 %collective-permute-start.14 = (bf16[7,32,768]{2,1,0:T(8,128)(2,1)S(1)}, bf16[7,32,768]{2,1,0:T(8,128)(2,1)S(1)}, u32[]{:S(2)}, u32[]{:S(2)}) collective-permute-start(bf16[7,32,768]{2,1,0:T(8,128)(2,1)S(1)} %slice.15), channel_id=1, source_target_pairs={{0,1},{2,3},{4,5},{6,7},{8,9},{10,11},{12,13},{14,15},{16,17},{18,... | collective-permute-start | bytes 1032200 | tf_op jit(solution)/shard_map/ppermute | solution.py:1264
  63.1 3.4 %collective-permute-start.17 = (bf16[24,3072]{1,0:T(8,128)(2,1)S(1)}, bf16[24,3072]{1,0:T(8,128)(2,1)}, u32[]{:S(2)}, u32[]{:S(2)}) collective-permute-start(bf16[24,3072]{1,0:T(8,128)(2,1)S(1)} %copy-done.52), channel_id=1, source_target_pairs={{0,8},{1,9},{2,10},{3,11},{4,12},{5,13},{6,14},{7,15},{8,0},{9,1},... | collective-permute-start | bytes 442376 | tf_op jit(solution)/shard_map/ppermute | solution.py:909
  85.2 6.9 %project.1 = (bf16[624,768]{1,0:T(8,128)(2,1)}, bf16[624,2304]{1,0:T(8,128)(2,1)}) custom-call(s32[1]{0:T(128)} %bitcast.1.refs_0_.img_ref, bf16[624,768]{1,0:T(8,128)(2,1)} %pack.2.refs_1_.refs_5_.x_ref, f32[624,1]{1,0:T(8,128)} %reshape.154.refs_3_.refs_2_.refs_6_.refs_5_.mask_ref, f32[8,768]{1,0:T(8,128)} %get-tuple-element.104.refs_3_.refs_4_.refs_6_.rows_ref, ...), custom_call_target="tpu_custom_call" | custom-call | flops 7000000000 | bytes 1 | tf_op jit(solution)/shard_map/project/pallas_call | solution.py:566
  92.8 6.6 %attend.2 = (bf16[624,768]{1,0:T(8,128)(2,1)}, f32[6,8,1536]{2,1,0:T(8,128)}, bf16[624,768]{1,0:T(8,128)(2,1)}) custom-call(bf16[624,2304]{1,0:T(8,128)(2,1)} %get-tuple-element.109.refs_0_.refs_1_.refs_2_, bf16[624,2304]{1,0:T(8,128)(2,1)} %get-tuple-element.109.refs_0_.refs_1_.refs_2_, bf16[624,2304]{1,0:T(8,128)(2,1)} %get-tuple-element.109.refs_0_.refs_1_.refs_2_, ...), custom_call_target="tpu_custom_call" | custom-call | flops 5500000256 | bytes 1 | tf_op jit(solution)/shard_map/attend/pallas_call | solution.py:280
  103.7 6.6 %attend.3 = (bf16[624,768]{1,0:T(8,128)(2,1)}, f32[6,8,1536]{2,1,0:T(8,128)}, bf16[624,768]{1,0:T(8,128)(2,1)}) custom-call(bf16[624,2304]{1,0:T(8,128)(2,1)} %get-tuple-element.109.refs_0_.refs_1_.refs_2_, bf16[624,2304]{1,0:T(8,128)(2,1)} %get-tuple-element.109.refs_0_.refs_1_.refs_2_, ...), custom_call_target="tpu_custom_call", output_to_operand_aliasing={{0}: (7, {}), {1}: (8, {}), {2}: (9, {})} | custom-call | flops 5500000256 | bytes 1 | tf_op jit(solution)/shard_map/attend/pallas_call | solution.py:280
  111.4 3.6 %join_three.4 = (bf16[4,2,2,96,768]{4,3,2,1,0:T(8,128)(2,1)}, bf16[4,2,2,24,768]{4,3,2,1,0:T(8,128)(2,1)}) custom-call(s32[3]{0:T(128)} %pad_add_fusion.bits_ref, bf16[4,2,120,384]{3,2,1,0:T(8,128)(2,1)} %get-tuple-element.108.refs_7_.first, bf16[4,2,120,384]{3,2,1,0:T(8,128)(2,1)} %copy-done.17, bf16[4,2,120,384]{3,2,1,0:T(8,128)(2,1)} %get-tuple-element.116.second, ...), custom_call_target="tpu_custom_call" | custom-call | flops 2300000000 | bytes 1 | tf_op jit(solution)/shard_map/join_three/pallas_call | solution.py:1077
  121.4 4.7 %mix.1 = (f32[624,768]{1,0:T(8,128)}, bf16[624,768]{1,0:T(8,128)(2,1)}) custom-call(s32[1]{0:T(128)} %bitcast.1.refs_0_.img_ref, bf16[624,768]{1,0:T(8,128)(2,1)} %get-tuple-element.115.refs_1_.refs_9_, bf16[384,768]{1,0:T(8,128)(2,1)} %bitcast.50, bf16[384,768]{1,0:T(8,128)(2,1)} %copy-done.20, ...), custom_call_target="tpu_custom_call" | custom-call | flops 4600000000 | bytes 1 | tf_op jit(solution)/shard_map/mix/pallas_call | solution.py:661
  126.0 8.7 %collective-permute-done.24.second_far = bf16[4,2,24,1536]{3,2,1,0:T(8,128)(2,1)S(1)} collective-permute-done((bf16[4,2,24,1536]{3,2,1,0:T(8,128)(2,1)}, bf16[4,2,24,1536]{3,2,1,0:T(8,128)(2,1)S(1)}, u32[]{:S(2)}, u32[]{:S(2)}) %collective-permute-start.24) | collective-permute-done | bytes 589856 | tf_op jit(solution)/shard_map/ppermute | solution.py:900
  135.6 3.2 join_three.5.refs_8_
  138.8 4.9 %collective-permute-done.25.refs_4_ = bf16[384,3072]{1,0:T(8,128)(2,1)} collective-permute-done((bf16[384,3072]{1,0:T(8,128)(2,1)}, bf16[384,3072]{1,0:T(8,128)(2,1)}, u32[]{:S(2)}, u32[]{:S(2)}) %collective-permute-start.25) | collective-permute-done | bytes 2359328 | tf_op jit(solution)/shard_map/ppermute | solution.py:904
  143.6 29.1 %mlp.1 = (f32[624,768]{1,0:T(8,128)}, f32[624,768]{1,0:T(8,128)}, bf16[3072,768]{1,0:T(8,128)(2,1)}, bf16[384,3072]{1,0:T(8,128)(2,1)}, bf16[384,3072]{1,0:T(8,128)(2,1)}, /*index=5*/f32[1,3072]{1,0:T(1,128)}) custom-call(s32[1]{0:T(128)} %bitcast.1.refs_0_.img_ref, bf16[624,768]{1,0:T(8,128)(2,1)} %get-tuple-element.121.refs_1_, ...), custom_call_target="tpu_custom_call" | custom-call | flops 28999999488 | bytes 1 | tf_op jit(solution)/shard_map/mlp/pallas_call | solution.py:513
  173.0 8.5 %mix_back.1 = (f32[624,768]{1,0:T(8,128)}, bf16[624,768]{1,0:T(8,128)(2,1)}, bf16[384,768]{1,0:T(8,128)(2,1)}, bf16[384,768]{1,0:T(8,128)(2,1)}, bf16[624,768]{1,0:T(8,128)(2,1)}, /*index=5*/f32[4,768]{1,0:T(4,128)}) custom-call(s32[1]{0:T(128)} %bitcast.1.refs_0_.img_ref, f32[624,768]{1,0:T(8,128)} %get-tuple-element.126.refs_1_, ...), custom_call_target="tpu_custom_call" | custom-call | flops 8800000000 | bytes 1 | tf_op jit(solution)/shard_map/mix_back/pallas_call | solution.py:708
  185.3 5.0 %fold_one.2 = (bf16[4,2,24,1920]{3,2,1,0:T(8,128)(2,1)}, f32[4,2,24,1920]{3,2,1,0:T(8,128)}, bf16[4,2,24,1920]{3,2,1,0:T(8,128)(2,1)}, f32[4,2,24,1920]{3,2,1,0:T(8,128)}) custom-call(s32[3]{0:T(128)} %pad_add_fusion.bits_ref, bf16[4,2,2,24,3072]{4,3,2,1,0:T(8,128)(2,1)} %bitcast.61, bf16[4,2,2,24,768]{4,3,2,1,0:T(8,128)(2,1)} %bitcast.63, ...), custom_call_target="tpu_custom_call" | custom-call | flops 2300000000 | bytes 1 | tf_op jit(solution)/shard_map/fold_one/pallas_call | solution.py:1173
  194.5 14.6 %attend_back.1 = (bf16[624,2304]{1,0:T(8,128)(2,1)}, f32[6,128,128]{2,1,0:T(8,128)}, f32[2,768]{1,0:T(2,128)}) custom-call(bf16[624,2304]{1,0:T(8,128)(2,1)} %get-tuple-element.109.refs_0_.refs_1_.refs_2_, bf16[624,2304]{1,0:T(8,128)(2,1)} %get-tuple-element.109.refs_0_.refs_1_.refs_2_, bf16[624,2304]{1,0:T(8,128)(2,1)} %get-tuple-element.109.refs_0_.refs_1_.refs_2_, ...), custom_call_target="tpu_custom_call" | custom-call | flops 14499999744 | bytes 1 | tf_op jit(solution)/shard_map/attend_back/pallas_call | solution.py:305
  209.1 7.0 %entry_grads.1 = (bf16[384,2304]{1,0:T(8,128)(2,1)}, bf16[384,2304]{1,0:T(8,128)(2,1)}) custom-call(s32[1]{0:T(128)} %bitcast.1.refs_0_.img_ref, bf16[624,768]{1,0:T(8,128)(2,1)} %get-tuple-element.110.refs_7_.refs_1_, bf16[624,2304]{1,0:T(8,128)(2,1)} %get-tuple-element.139.refs_2_.pull_ref, f32[2,768]{1,0:T(2,128)} %get-tuple-element.143.refs_3_.refs_1_), custom_call_target="tpu_custom_call" | custom-call | flops 7200000000 | bytes 1 | tf_op jit(solution)/shard_map/entry_grads/pallas_call | solution.py:742
  218.3 3.9 %fold_two.2 = (bf16[4,24,1920]{2,1,0:T(8,128)(2,1)}, f32[4,24,1920]{2,1,0:T(8,128)}, bf16[4,24,1920]{2,1,0:T(8,128)(2,1)}, f32[4,24,1920]{2,1,0:T(8,128)}) custom-call(s32[3]{0:T(128)} %pad_add_fusion.bits_ref, f32[4,2,24,1920]{3,2,1,0:T(8,128)} %get-tuple-element.140.a_near, bf16[4,2,24,1920]{3,2,1,0:T(8,128)(2,1)} %copy-done.18, ...), custom_call_target="tpu_custom_call" | custom-call | flops 2300000000 | bytes 1 | tf_op jit(solution)/shard_map/fold_two/pallas_call | solution.py:1173
  222.2 3.4 %collective-permute-start.33 = (bf16[4,24,1920]{2,1,0:T(8,128)(2,1)}, bf16[4,24,1920]{2,1,0:T(8,128)(2,1)S(1)}, u32[]{:S(2)}, u32[]{:S(2)}) collective-permute-start(bf16[4,24,1920]{2,1,0:T(8,128)(2,1)} %get-tuple-element.150), channel_id=1, source_target_pairs={{0,1},{1,0},{2,3},{3,2},{4,5},{5,4},{6,7},{7,6},{8,9},{9,8},{10,11... | collective-permute-start | bytes 1105928 | tf_op jit(solution)/shard_map/ppermute | solution.py:900
  226.7 11.5 %project_back.1 = (bf16[624,768]{1,0:T(8,128)(2,1)}, f32[2,768]{1,0:T(2,128)}) custom-call(s32[1]{0:T(128)} %bitcast.1.refs_0_.img_ref, bf16[624,768]{1,0:T(8,128)(2,1)} %pack.2.refs_1_.refs_5_.x_ref, f32[624,1]{1,0:T(8,128)} %reshape.154.refs_3_.refs_2_.refs_6_.refs_5_.mask_ref, f32[8,768]{1,0:T(8,128)} %get-tuple-element.104.refs_3_.refs_4_.refs_6_.rows_ref, ...), custom_call_target="tpu_custom_call" | custom-call | flops 11000000512 | bytes 1 | tf_op jit(solution)/shard_map/project_back/pallas_call | solution.py:626
  239.4 3.6 %fold_one.3 = (bf16[4,2,24,1152]{3,2,1,0:T(8,128)(2,1)}, f32[4,2,24,1152]{3,2,1,0:T(8,128)}, bf16[4,2,24,1152]{3,2,1,0:T(8,128)(2,1)}, f32[4,2,24,1152]{3,2,1,0:T(8,128)}) custom-call(s32[3]{0:T(128)} %pad_add_fusion.bits_ref, bf16[4,2,2,24,2304]{4,3,2,1,0:T(8,128)(2,1)} %bitcast.62, bf16[4,2,2,24,2304]{4,3,2,1,0:T(8,128)(2,1)} %bitcast.48, ...), custom_call_target="tpu_custom_call" | custom-call | flops 2300000000 | bytes 1 | tf_op jit(solution)/shard_map/fold_one/pallas_call | solution.py:1173
  296.2 6.8 %collective-permute-done.50.refs_2_ = bf16[24,2304]{1,0:T(8,128)(2,1)S(1)} collective-permute-done((bf16[24,2304]{1,0:T(8,128)(2,1)S(1)}, bf16[24,2304]{1,0:T(8,128)(2,1)S(1)}, u32[]{:S(2)}, u32[]{:S(2)}) %collective-permute-start.50) | collective-permute-done | bytes 110624 | tf_op jit(solution)/shard_map/ppermute | solution.py:909
  (273 shorter events, 139.8 us)
Async XLA Ops:
  7.2 302.1 %reduce-scatter.2.cloned.1.call-start = ((), (), s32[]{:S(2)}) async-start(), calls=%async_computation.1 | async-start | bytes 4866048 | tf_op jit(solution)/shard_map/reduce_scatter | solution.py:1355
  9.0 18.4 %collective-permute-start.3 = (bf16[24,2432]{1,0:T(8,128)(2,1)}, bf16[24,2432]{1,0:T(8,128)(2,1)S(1)}, u32[]{:S(2)}, u32[]{:S(2)}) collective-permute-start(bf16[24,2432]{1,0:T(8,128)(2,1)} %carry.1.refs_2_.refs_0_), channel_id=1, source_target_pairs={{0,12},{1,13},{2,14},{3,15},{4,0},{5,1},{6,2},{7,3},{8,4},{9,5},{1... | collective-permute-start | bytes 350216 | tf_op jit(solution)/shard_map/ppermute | solution.py:909
  16.7 20.6 %collective-permute-start.7 = (bf16[120,768]{1,0:T(8,128)(2,1)}, bf16[120,768]{1,0:T(8,128)(2,1)S(1)}, u32[]{:S(2)}, u32[]{:S(2)}) collective-permute-start(bf16[120,768]{1,0:T(8,128)(2,1)} %stack.17.refs_4_.refs_0_), channel_id=1, source_target_pairs={{0,12},{1,13},{2,14},{3,15},{4,0},{5,1},{6,2},{7,3},{8,4},{9,5},{1... | collective-permute-start | bytes 552968 | tf_op jit(solution)/shard_map/ppermute | solution.py:909
  63.1 36.3 %collective-permute-start.17 = (bf16[24,3072]{1,0:T(8,128)(2,1)S(1)}, bf16[24,3072]{1,0:T(8,128)(2,1)}, u32[]{:S(2)}, u32[]{:S(2)}) collective-permute-start(bf16[24,3072]{1,0:T(8,128)(2,1)S(1)} %copy-done.52), channel_id=1, source_target_pairs={{0,8},{1,9},{2,10},{3,11},{4,12},{5,13},{6,14},{7,15},{8,0},{9,1},... | collective-permute-start | bytes 442376 | tf_op jit(solution)/shard_map/ppermute | solution.py:909
  66.5 25.6 %collective-permute-start.16 = (bf16[24,3072]{1,0:T(8,128)(2,1)S(1)}, bf16[24,3072]{1,0:T(8,128)(2,1)}, u32[]{:S(2)}, u32[]{:S(2)}) collective-permute-start(bf16[24,3072]{1,0:T(8,128)(2,1)S(1)} %copy-done.52), channel_id=1, source_target_pairs={{0,12},{1,13},{2,14},{3,15},{4,0},{5,1},{6,2},{7,3},{8,4},{9,5},{1... | collective-permute-start | bytes 442376 | tf_op jit(solution)/shard_map/ppermute | solution.py:909
  72.3 19.8 %collective-permute-start.15 = (bf16[24,3072]{1,0:T(8,128)(2,1)S(1)}, bf16[24,3072]{1,0:T(8,128)(2,1)S(1)}, u32[]{:S(2)}, u32[]{:S(2)}) collective-permute-start(bf16[24,3072]{1,0:T(8,128)(2,1)S(1)} %copy-done.52), channel_id=1, source_target_pairs={{0,4},{1,5},{2,6},{3,7},{4,8},{5,9},{6,10},{7,11},{8,12},{9,13},{1... | collective-permute-start | bytes 442376 | tf_op jit(solution)/shard_map/ppermute | solution.py:909
  83.4 26.9 %collective-permute-start.19 = (bf16[4,2,120,384]{3,2,1,0:T(8,128)(2,1)}, bf16[4,2,120,384]{3,2,1,0:T(8,128)(2,1)S(1)}, u32[]{:S(2)}, u32[]{:S(2)}) collective-permute-start(bf16[4,2,120,384]{3,2,1,0:T(8,128)(2,1)} %get-tuple-element.116.second), channel_id=1, source_target_pairs={{0,1},{1,0},{2,3},{3,2},{4,5},{5,4},{6,7},{7,6},{8,9},{9,8},{10,11... | collective-permute-start | bytes 2211848 | tf_op jit(solution)/shard_map/ppermute | solution.py:900
  83.6 26.7 %collective-permute-start.18 = (bf16[4,2,120,384]{3,2,1,0:T(8,128)(2,1)}, bf16[4,2,120,384]{3,2,1,0:T(8,128)(2,1)S(1)}, u32[]{:S(2)}, u32[]{:S(2)}) collective-permute-start(bf16[4,2,120,384]{3,2,1,0:T(8,128)(2,1)} %get-tuple-element.108.refs_7_.first), channel_id=1, source_target_pairs={{0,2},{1,3},{2,0},{3,1},{4,6},{5,7},{6,4},{7,5},{8,10},{9,11},{10,... | collective-permute-start | bytes 2211848 | tf_op jit(solution)/shard_map/ppermute | solution.py:900
  118.8 15.9 %collective-permute-start.24 = (bf16[4,2,24,1536]{3,2,1,0:T(8,128)(2,1)}, bf16[4,2,24,1536]{3,2,1,0:T(8,128)(2,1)S(1)}, u32[]{:S(2)}, u32[]{:S(2)}) collective-permute-start(bf16[4,2,24,1536]{3,2,1,0:T(8,128)(2,1)} %get-tuple-element.122.second), channel_id=1, source_target_pairs={{0,1},{1,0},{2,3},{3,2},{4,5},{5,4},{6,7},{7,6},{8,9},{9,8},{10,11... | collective-permute-start | bytes 1769480 | tf_op jit(solution)/shard_map/ppermute | solution.py:900
  120.5 18.2 %collective-permute-start.26 = (bf16[1536,768]{1,0:T(8,128)(2,1)S(1)}, bf16[1536,768]{1,0:T(8,128)(2,1)}, u32[]{:S(2)}, u32[]{:S(2)}) collective-permute-start(bf16[1536,768]{1,0:T(8,128)(2,1)S(1)} %bitcast.38), channel_id=1, source_target_pairs={{0,16},{16,0},{1,17},{17,1},{2,18},{18,2},{3,19},{19,3},{4,20},{20... | collective-permute-start | bytes 7077896 | tf_op jit(solution)/shard_map/ppermute | solution.py:904
  190.3 27.1 %collective-permute-start.30 = (bf16[4,2,24,1920]{3,2,1,0:T(8,128)(2,1)}, bf16[4,2,24,1920]{3,2,1,0:T(8,128)(2,1)S(1)}, u32[]{:S(2)}, u32[]{:S(2)}) collective-permute-start(bf16[4,2,24,1920]{3,2,1,0:T(8,128)(2,1)} %get-tuple-element.135.refs_1_), channel_id=1, source_target_pairs={{0,1},{1,0},{2,3},{3,2},{4,5},{5,4},{6,7},{7,6},{8,9},{9,8},{10,11... | collective-permute-start | bytes 2211848 | tf_op jit(solution)/shard_map/ppermute | solution.py:900
  193.5 23.9 %collective-permute-start.31 = (bf16[4,2,24,1920]{3,2,1,0:T(8,128)(2,1)S(1)}, bf16[4,2,24,1920]{3,2,1,0:T(8,128)(2,1)}, u32[]{:S(2)}, u32[]{:S(2)}) collective-permute-start(bf16[4,2,24,1920]{3,2,1,0:T(8,128)(2,1)S(1)} %copy-done.19), channel_id=1, source_target_pairs={{0,2},{1,3},{2,0},{3,1},{4,6},{5,7},{6,4},{7,5},{8,10},{9,11},{10,... | collective-permute-start | bytes 2211848 | tf_op jit(solution)/shard_map/ppermute | solution.py:900
  216.1 22.1 %collective-permute-start.34 = (bf16[384,2304]{1,0:T(8,128)(2,1)}, bf16[384,2304]{1,0:T(8,128)(2,1)S(1)}, u32[]{:S(2)}, u32[]{:S(2)}) collective-permute-start(bf16[384,2304]{1,0:T(8,128)(2,1)} %get-tuple-element.144.refs_0_), channel_id=1, source_target_pairs={{0,16},{16,0},{1,17},{17,1},{2,18},{18,2},{3,19},{19,3},{4,20},{20... | collective-permute-start | bytes 5308424 | tf_op jit(solution)/shard_map/ppermute | solution.py:904
  216.1 22.1 %collective-permute-start.29 = (bf16[7,32,768]{2,1,0:T(8,128)(2,1)}, bf16[7,32,768]{2,1,0:T(8,128)(2,1)}, u32[]{:S(2)}, u32[]{:S(2)}) collective-permute-start(bf16[7,32,768]{2,1,0:T(8,128)(2,1)} %send_rows.2.refs_10_), channel_id=1, source_target_pairs={{1,0},{3,2},{5,4},{7,6},{9,8},{11,10},{13,12},{15,14},{17,16},{19,... | collective-permute-start | bytes 1032200 | tf_op jit(solution)/shard_map/ppermute | solution.py:1269
  222.2 20.8 %collective-permute-start.33 = (bf16[4,24,1920]{2,1,0:T(8,128)(2,1)}, bf16[4,24,1920]{2,1,0:T(8,128)(2,1)S(1)}, u32[]{:S(2)}, u32[]{:S(2)}) collective-permute-start(bf16[4,24,1920]{2,1,0:T(8,128)(2,1)} %get-tuple-element.150), channel_id=1, source_target_pairs={{0,1},{1,0},{2,3},{3,2},{4,5},{5,4},{6,7},{7,6},{8,9},{9,8},{10,11... | collective-permute-start | bytes 1105928 | tf_op jit(solution)/shard_map/ppermute | solution.py:900
  225.6 17.5 %collective-permute-start.32 = (bf16[4,24,1920]{2,1,0:T(8,128)(2,1)}, bf16[4,24,1920]{2,1,0:T(8,128)(2,1)S(1)}, u32[]{:S(2)}, u32[]{:S(2)}) collective-permute-start(bf16[4,24,1920]{2,1,0:T(8,128)(2,1)} %get-tuple-element.145.refs_0_), channel_id=1, source_target_pairs={{0,2},{1,3},{2,0},{3,1},{4,6},{5,7},{6,4},{7,5},{8,10},{9,11},{10,... | collective-permute-start | bytes 1105928 | tf_op jit(solution)/shard_map/ppermute | solution.py:900
  243.1 22.6 %collective-permute-start.38 = (bf16[4,2,24,1152]{3,2,1,0:T(8,128)(2,1)}, bf16[4,2,24,1152]{3,2,1,0:T(8,128)(2,1)S(1)}, u32[]{:S(2)}, u32[]{:S(2)}) collective-permute-start(bf16[4,2,24,1152]{3,2,1,0:T(8,128)(2,1)} %get-tuple-element.152.refs_0_), channel_id=1, source_target_pairs={{0,1},{1,0},{2,3},{3,2},{4,5},{5,4},{6,7},{7,6},{8,9},{9,8},{10,11... | collective-permute-start | bytes 1327112 | tf_op jit(solution)/shard_map/ppermute | solution.py:900
  248.5 23.5 %collective-permute-start.43 = (bf16[24,3840]{1,0:T(8,128)(2,1)S(1)}, bf16[24,3840]{1,0:T(8,128)(2,1)S(1)}, u32[]{:S(2)}, u32[]{:S(2)}) collective-permute-start(bf16[24,3840]{1,0:T(8,128)(2,1)S(1)} %copy-done.48), channel_id=1, source_target_pairs={{0,4},{1,5},{2,6},{3,7},{4,8},{5,9},{6,10},{7,11},{8,12},{9,13},{1... | collective-permute-start | bytes 552968 | tf_op jit(solution)/shard_map/ppermute | solution.py:909
  250.3 23.0 %collective-permute-start.44 = (bf16[24,3840]{1,0:T(8,128)(2,1)S(1)}, bf16[24,3840]{1,0:T(8,128)(2,1)S(1)}, u32[]{:S(2)}, u32[]{:S(2)}) collective-permute-start(bf16[24,3840]{1,0:T(8,128)(2,1)S(1)} %copy-done.46), channel_id=1, source_target_pairs={{0,8},{1,9},{2,10},{3,11},{4,12},{5,13},{6,14},{7,15},{8,0},{9,1},... | collective-permute-start | bytes 552968 | tf_op jit(solution)/shard_map/ppermute | solution.py:909
  253.9 20.9 %collective-permute-start.45 = (bf16[24,3840]{1,0:T(8,128)(2,1)S(1)}, bf16[24,3840]{1,0:T(8,128)(2,1)S(1)}, u32[]{:S(2)}, u32[]{:S(2)}) collective-permute-start(bf16[24,3840]{1,0:T(8,128)(2,1)S(1)} %copy-done.45), channel_id=1, source_target_pairs={{0,12},{1,13},{2,14},{3,15},{4,0},{5,1},{6,2},{7,3},{8,4},{9,5},{1... | collective-permute-start | bytes 552968 | tf_op jit(solution)/shard_map/ppermute | solution.py:909
  272.0 17.3 %collective-permute-start.36 = (bf16[7,32,768]{2,1,0:T(8,128)(2,1)S(1)}, bf16[7,32,768]{2,1,0:T(8,128)(2,1)S(1)}, u32[]{:S(2)}, u32[]{:S(2)}) collective-permute-start(bf16[7,32,768]{2,1,0:T(8,128)(2,1)S(1)} %copy-done.33), channel_id=1, source_target_pairs={{1,0},{3,2},{5,4},{7,6},{9,8},{11,10},{13,12},{15,14},{17,16},{19,... | collective-permute-start | bytes 1032200 | tf_op jit(solution)/shard_map/ppermute | solution.py:1269
  285.0 21.3 %collective-permute-start.48 = (f32[24,768]{1,0:T(8,128)}, f32[24,768]{1,0:T(8,128)S(1)}, u32[]{:S(2)}, u32[]{:S(2)}) collective-permute-start(f32[24,768]{1,0:T(8,128)} %add.55.refs_3_.refs_1_), channel_id=1, source_target_pairs={{0,12},{1,13},{2,14},{3,15},{4,0},{5,1},{6,2},{7,3},{8,4},{9,5},{1... | collective-permute-start | bytes 221192 | tf_op jit(solution)/shard_map/ppermute | solution.py:909
  287.3 18.9 %collective-permute-start.47 = (f32[24,768]{1,0:T(8,128)}, f32[24,768]{1,0:T(8,128)S(1)}, u32[]{:S(2)}, u32[]{:S(2)}) collective-permute-start(f32[24,768]{1,0:T(8,128)} %add.55.refs_3_.refs_1_), channel_id=1, source_target_pairs={{0,8},{1,9},{2,10},{3,11},{4,12},{5,13},{6,14},{7,15},{8,0},{9,1},... | collective-permute-start | bytes 221192 | tf_op jit(solution)/shard_map/ppermute | solution.py:909
  287.8 18.4 %collective-permute-start.46 = (f32[24,768]{1,0:T(8,128)}, f32[24,768]{1,0:T(8,128)S(1)}, u32[]{:S(2)}, u32[]{:S(2)}) collective-permute-start(f32[24,768]{1,0:T(8,128)} %add.55.refs_3_.refs_1_), channel_id=1, source_target_pairs={{0,4},{1,5},{2,6},{3,7},{4,8},{5,9},{6,10},{7,11},{8,12},{9,13},{1... | collective-permute-start | bytes 221192 | tf_op jit(solution)/shard_map/ppermute | solution.py:909
  (95 other events, 554.6 us)
Sparse Core Ops, SparseCore 0:
  182.0 119.4 reduce-scatter.1

commit v3 on v2

--- a/solution.py
+++ b/solution.py
@@ -19,7 +19,7 @@
 
 
 def cost(microseconds):
-    return pl.CostEstimate(flops=int(microseconds * 1000000000), bytes_accessed=1, transcendentals=0)
+    return pl.CostEstimate(flops=int(microseconds * 1e9), bytes_accessed=1, transcendentals=0)
 
 
 ANY = pl.BlockSpec(memory_space=pl.ANY)
@@ -291,7 +291,7 @@
         input_output_aliases={7 + place: place for place in range(len(given))},
         scratch_shapes=[pltpu.VMEM((KEYS, LSE), F32), pltpu.VMEM((KEYS, LSE), BF)],
         compiler_params=pltpu.CompilerParams(vmem_limit_bytes=VMEM_LIMIT),
-        cost_estimate=cost(5.5),
+        cost_estimate=cost(11),
         name="attend",
     )(joint, joint, joint, fill, table, jnp.asarray(SHIFTS), jnp.asarray(ONEHOTS, BF), *given, *earlier)
 
@@ -325,7 +325,7 @@
             pltpu.VMEM((TOKENS, 256), F32), pltpu.VMEM((TOKENS, 256), BF),
         ],
         compiler_params=pltpu.CompilerParams(vmem_limit_bytes=VMEM_LIMIT),
-        cost_estimate=cost(14.5),
+        cost_estimate=cost(9),
         name="attend_back",
     )(
         joint, joint, joint, grad_mixed, lse, features, fill, table, jnp.asarray(SHIFTS), jnp.asarray(ONEHOTS, BF),
@@ -354,29 +354,29 @@
     return height[:slots][::-1], width[:slots][::-1]
 
 
-def pack_kernel(masked, moved, parity_ref, own_ref, far_ref, mask_ref, out_ref, stage_ref):
+def pack_kernel(begin, moved, parity_ref, own_ref, far_ref, mask_ref, out_ref, stage_ref):
     parity = parity_ref[0]
     stage_ref[...] = jnp.zeros_like(stage_ref)
     for row in range(BAND):
         if row < moved:
-            line = jnp.where(parity == 0, own_ref[row, :REAL], far_ref[row]).astype(F32)
+            line = jnp.where(parity == 0, own_ref[row, :REAL], far_ref[begin + row]).astype(F32)
         else:
             line = own_ref[row - moved * parity, :REAL].astype(F32)
         for first, rows, col, cols, _, offset in SEGMENTS:
             if first <= row < first + rows:
                 place = offset + (row - first) * cols
                 stage_ref[place : place + cols, :] = line[col : col + cols]
-    if masked:
+    if begin:
         out_ref[...] = (stage_ref[...] * mask_ref[...]).astype(out_ref.dtype)
     else:
         out_ref[...] = stage_ref[...].astype(out_ref.dtype)
 
 
-def pack(parity, own, far, mask, masked, *earlier):
+def pack(parity, own, far, mask, begin, *earlier):
     width = own.shape[2]
     vmem = pl.BlockSpec(memory_space=pltpu.VMEM)
     return pl.pallas_call(
-        ordered(partial(pack_kernel, masked, far.shape[0]), 4, earlier),
+        ordered(partial(pack_kernel, begin, far.shape[0] // 2), 4, earlier),
         in_specs=[pl.BlockSpec(memory_space=pltpu.SMEM), vmem, vmem, vmem] + [ANY] * len(earlier),
         out_specs=vmem,
         out_shape=jax.ShapeDtypeStruct((TOKENS, width), BF),
@@ -415,7 +415,7 @@
         out_shape=jax.ShapeDtypeStruct(shape, BF),
         scratch_shapes=[pltpu.VMEM((TOKENS, width), F32), pltpu.VMEM((BAND, REAL, width), F32)],
         compiler_params=pltpu.CompilerParams(vmem_limit_bytes=VMEM_LIMIT),
-        cost_estimate=cost(3),
+        cost_estimate=cost(0.5),
         name="unpack",
     )(parity.reshape(1), win, far, *earlier)
 
@@ -440,7 +440,7 @@
         out_shape=jax.ShapeDtypeStruct((moved, REAL, width), BF),
         scratch_shapes=[pltpu.VMEM((TOKENS, width), F32), pltpu.VMEM((moved, REAL, width), F32)],
         compiler_params=pltpu.CompilerParams(vmem_limit_bytes=VMEM_LIMIT),
-        cost_estimate=cost(2.6),
+        cost_estimate=cost(0.5),
         name="send_rows",
     )(win, *earlier)
 
@@ -463,7 +463,7 @@
 
 
 def mlp_kernel(
-    img_ref, entry_ref, pull_ref, expand_ref, expand_far_ref, bias_ref, reduce_ref, reduce_far_ref,
+    img_ref, entry_ref, pull_ref, expand_ref, bias_ref, reduce_ref, reduce_far_ref,
     result_ref, back_ref, dreduce_ref, dexpand_far_ref, dexpand_ref, dbias_ref, turned_ref,
 ):
     step = pl.program_id(0)
@@ -476,8 +476,7 @@
         back_ref[...] = jnp.zeros_like(back_ref)
         turned_ref[...] = entry_ref[...].T
 
-    near, far = expand_ref[...], expand_far_ref[...]
-    expand = jnp.concatenate([jnp.where(low, near, far), jnp.where(low, far, near)], 0)
+    expand = expand_ref[...]
     reduce = jnp.where(first_half, reduce_far_ref[...], reduce_ref[...])
     pull = pull_ref[...]
     hidden = dot_n(entry_ref[...], expand) + bias_ref[...]
@@ -494,7 +493,7 @@
     dreduce_ref[...] = dot_f(active, pull).astype(BF)
 
 
-def mlp(img, entry_two, incoming, expand, expand_far, bias, reduce, reduce_far, *earlier, chunk=768):
+def mlp(img, entry_two, incoming, expand, bias, reduce, reduce_far, *earlier, chunk=768):
     width = entry_two.shape[1]
     hidden = bias.shape[1]
     tokens = entry_two.shape[0]
@@ -511,12 +510,12 @@
         return pl.BlockSpec((rows, chunk), lambda step, img: (0, place(step, img)))
 
     return pl.pallas_call(
-        ordered(mlp_kernel, 8, earlier),
+        ordered(mlp_kernel, 7, earlier),
         grid_spec=pltpu.PrefetchScalarGridSpec(
             num_scalar_prefetch=1,
             grid=(steps,),
             in_specs=[
-                fixed(tokens, width), fixed(tokens, width), across(width // 2), across(width // 2), across(1),
+                fixed(tokens, width), fixed(tokens, width), across(width), across(1),
                 pl.BlockSpec((chunk, width), lambda step, img: (jnp.maximum(step - half, 0), 0)),
                 pl.BlockSpec((chunk, width), lambda step, img: (jnp.minimum(step, half - 1), 0)),
             ] + [ANY] * len(earlier),
@@ -538,7 +537,7 @@
         compiler_params=pltpu.CompilerParams(vmem_limit_bytes=VMEM_LIMIT),
         cost_estimate=cost(29),
         name="mlp",
-    )(img.reshape(1), entry_two, incoming, expand, expand_far, bias, reduce, reduce_far, *earlier)
+    )(img.reshape(1), entry_two, incoming, expand, bias, reduce, reduce_far, *earlier)
 
 
 def project_kernel(img_ref, x_ref, mask_ref, rows_ref, near_ref, far_ref, bias_ref, entry_ref, joint_ref):
@@ -643,11 +642,8 @@
     )
 
 
-def mix_kernel(img_ref, mixed_ref, near_ref, far_ref, rows_ref, x_ref, mask_ref, middle_ref, entry_ref):
-    low = img_ref[0] == 0
-    near, far = near_ref[...], far_ref[...]
-    weight = jnp.concatenate([jnp.where(low, near, far), jnp.where(low, far, near)], 0)
-    branch = dot_n(mixed_ref[...], weight) + rows_ref[2:3]
+def mix_kernel(mixed_ref, weight_ref, rows_ref, x_ref, mask_ref, middle_ref, entry_ref):
+    branch = dot_n(mixed_ref[...], weight_ref[...]) + rows_ref[2:3]
     middle = x_ref[...].astype(F32) + mask_ref[...] * branch
     middle_ref[...] = middle
     centred = middle - jnp.mean(middle, axis=1, keepdims=True)
@@ -656,21 +652,30 @@
     entry_ref[...] = normed.astype(BF)
 
 
-def mix(img, mixed, near, far, rows, x, mask, *earlier):
-    vmem = pl.BlockSpec(memory_space=pltpu.VMEM)
-    return pl.pallas_call(
-        ordered(mix_kernel, 7, earlier),
-        in_specs=[pl.BlockSpec(memory_space=pltpu.SMEM)] + [vmem] * 6 + [ANY] * len(earlier),
-        out_specs=[vmem] * 2,
+def last_columns(array, width):
+    place = array.shape[1] // width - 1
+    return pl.BlockSpec((array.shape[0], width), lambda step: (0, place))
+
+
+def mix(mixed, weights, rows, x, mask, *earlier):
+    tokens, width = x.shape
+    return pl.pallas_call(
+        ordered(mix_kernel, 5, earlier),
+        grid=(1,),
+        in_specs=[
+            whole((tokens, width)), last_columns(weights, width), whole(rows.shape), whole((tokens, width)),
+            whole(mask.shape),
+        ] + [ANY] * len(earlier),
+        out_specs=[whole((tokens, width))] * 2,
         out_shape=[jax.ShapeDtypeStruct(x.shape, F32), jax.ShapeDtypeStruct(x.shape, BF)],
         compiler_params=pltpu.CompilerParams(vmem_limit_bytes=VMEM_LIMIT),
         cost_estimate=cost(4.6),
         name="mix",
-    )(img.reshape(1), mixed, near, far, rows, x, mask, *earlier)
+    )(mixed, weights, rows, x, mask, *earlier)
 
 
 def mix_back_kernel(
-    img_ref, back_ref, result_ref, middle_ref, incoming_ref, mask_ref, rows_ref, near_ref, far_ref, mixed_ref,
+    img_ref, back_ref, result_ref, middle_ref, incoming_ref, mask_ref, rows_ref, weight_ref, mixed_ref,
     grad_middle_ref, grad_mixed_ref, give_ref, keep_ref, out_ref, sums_ref,
 ):
     low = img_ref[0] == 0
@@ -693,31 +698,34 @@
     grad_middle_ref[...] = grad_middle
     branch = (mask * grad_middle).astype(BF)
     sums_ref[0:1] = jnp.sum(branch.astype(F32), axis=0, keepdims=True)
-    near, far = near_ref[...], far_ref[...]
-    weight = jnp.concatenate([jnp.where(low, near, far), jnp.where(low, far, near)], 0)
-    grad_mixed_ref[...] = dot_t(branch, weight).astype(BF)
+    grad_mixed_ref[...] = dot_t(branch, weight_ref[...]).astype(BF)
     half = keep_ref.shape[0]
     total = dot_f(mixed_ref[...], branch)
     give_ref[...] = jnp.where(low, total[half:], total[:half]).astype(BF)
     keep_ref[...] = jnp.where(low, total[:half], total[half:]).astype(BF)
 
 
-def mix_back(img, back, result, middle, incoming, mask, rows, near, far, mixed, *earlier):
+def mix_back(img, back, result, middle, incoming, mask, rows, weights, mixed, *earlier):
     tokens, width = middle.shape
-    vmem = pl.BlockSpec(memory_space=pltpu.VMEM)
-    return pl.pallas_call(
-        ordered(mix_back_kernel, 10, earlier),
-        in_specs=[pl.BlockSpec(memory_space=pltpu.SMEM)] + [vmem] * 9 + [ANY] * len(earlier),
-        out_specs=[vmem] * 6,
+    half = (width // 2, width)
+    full = whole((tokens, width))
+    return pl.pallas_call(
+        ordered(mix_back_kernel, 9, earlier),
+        grid=(1,),
+        in_specs=[
+            pl.BlockSpec(memory_space=pltpu.SMEM), full, full, full, full, whole(mask.shape),
+            whole(rows.shape), last_columns(weights, width), full,
+        ] + [ANY] * len(earlier),
+        out_specs=[full, full, whole(half), whole(half), full, whole((4, width))],
         out_shape=[
             jax.ShapeDtypeStruct((tokens, width), F32), jax.ShapeDtypeStruct((tokens, width), BF),
-            jax.ShapeDtypeStruct((width // 2, width), BF), jax.ShapeDtypeStruct((width // 2, width), BF),
+            jax.ShapeDtypeStruct(half, BF), jax.ShapeDtypeStruct(half, BF),
             jax.ShapeDtypeStruct((tokens, width), BF), jax.ShapeDtypeStruct((4, width), F32),
         ],
         compiler_params=pltpu.CompilerParams(vmem_limit_bytes=VMEM_LIMIT),
-        cost_estimate=cost(8.8),
+        cost_estimate=cost(7),
         name="mix_back",
-    )(img.reshape(1), back, result, middle, incoming, mask, rows, near, far, mixed, *earlier)
+    )(img.reshape(1), back, result, middle, incoming, mask, rows, weights, mixed, *earlier)
 
 
 def entry_grads_kernel(img_ref, entry_ref, grad_ref, give_ref, keep_ref, turned_ref):
@@ -750,7 +758,7 @@
         ],
         scratch_shapes=[pltpu.VMEM((width, tokens), BF)],
         compiler_params=pltpu.CompilerParams(vmem_limit_bytes=VMEM_LIMIT),
-        cost_estimate=cost(7.2),
+        cost_estimate=cost(5),
         name="entry_grads",
     )(img.reshape(1), entry, grad, *earlier)
 
@@ -780,7 +788,7 @@
         in_specs=[vmem] * 5 + [ANY] * len(earlier),
         out_specs=vmem,
         out_shape=jax.ShapeDtypeStruct((24, norm.shape[1]), F32),
-        cost_estimate=cost(1.9),
+        cost_estimate=cost(1.0),
         name="sums",
     )(norm, joint, mixed, expand, tables, *earlier)
 
@@ -796,20 +804,36 @@
         in_specs=[vmem] * 2 + [ANY] * len(earlier),
         out_specs=vmem,
         out_shape=jax.ShapeDtypeStruct(one.shape, F32),
-        cost_estimate=cost(1),
+        cost_estimate=cost(0.5),
         name="add",
     )(one, two, *earlier)
 
 
-def share_kernel(block, slots, place_ref, *refs):
-    parts, outs = refs[:-10], refs[-10:]
-    depth = len(parts)
+def add_depth_kernel(depth, place_ref, *refs):
+    parts, out_ref = refs[:depth], refs[-1]
     total = None
     for level in range(depth):
         found = parts[0][...]
         for step in range(1, depth):
-            found = jnp.where(lax.rem(place_ref[1] - level + depth, depth) == step, parts[step][...], found)
+            found = jnp.where((place_ref[2] ^ step) == level, parts[step][...], found)
         total = found if total is None else total + found
+    out_ref[...] = total
+
+
+def add_depth(bits, parts, *earlier):
+    vmem = pl.BlockSpec(memory_space=pltpu.VMEM)
+    return pl.pallas_call(
+        ordered(partial(add_depth_kernel, len(parts)), 1 + len(parts), earlier),
+        in_specs=[pl.BlockSpec(memory_space=pltpu.SMEM)] + [vmem] * len(parts) + [ANY] * len(earlier),
+        out_specs=vmem,
+        out_shape=jax.ShapeDtypeStruct(parts[0].shape, F32),
+        cost_estimate=cost(0.5),
+        name="add_depth",
+    )(bits, *parts, *earlier)
+
+
+def share_kernel(block, slots, place_ref, one_ref, two_ref, *outs):
+    total = one_ref[...] + two_ref[...]
     width = total.shape[1]
     begin = place_ref[0] * block
 
@@ -829,17 +853,17 @@
         outs[9][slot : slot + 1] = line[:, 64:]
 
 
-def share(number, parts, block, slots, *earlier):
+def share(number, one, two, block, slots, *earlier):
     vmem = pl.BlockSpec(memory_space=pltpu.VMEM)
     shapes = [(1, block)] * 6 + [(1, 2 * block), (1, 4 * block)] + [(slots, HEAD_DIM)] * 2
     return pl.pallas_call(
-        ordered(partial(share_kernel, block, slots), 1 + len(parts), earlier),
-        in_specs=[pl.BlockSpec(memory_space=pltpu.SMEM)] + [vmem] * len(parts) + [ANY] * len(earlier),
+        ordered(partial(share_kernel, block, slots), 3, earlier),
+        in_specs=[pl.BlockSpec(memory_space=pltpu.SMEM)] + [vmem] * 2 + [ANY] * len(earlier),
         out_specs=[vmem] * len(shapes),
         out_shape=[jax.ShapeDtypeStruct(shape, F32) for shape in shapes],
         cost_estimate=cost(1.8),
         name="share",
-    )(number, *parts, *earlier)
+    )(number.reshape(1), one, two, *earlier)
 
 
 def place_kernel(depth, *refs):
@@ -885,7 +909,7 @@
         out_shape=[
             jax.ShapeDtypeStruct((rows, cut), F32), jax.ShapeDtypeStruct((rows, columns - cut), F32),
         ],
-        cost_estimate=cost(2),
+        cost_estimate=cost(1),
         name="settle",
     )(*parts, *earlier)
 
@@ -904,26 +928,9 @@
     return lax.ppermute(block, "img", [(0, 1), (1, 0)])
 
 
-def shift_depth(block, step):
+def swap_depth(block, step):
     count = lax.axis_size("rows")
-    return lax.ppermute(
-        block, "rows", [(place, (place + 4 * step) % count) for place in range(count)]
-    )
-
-
-def in_order(bit, mine, other, axis):
-    return jnp.where(
-        bit == 0, jnp.stack([mine, other], axis), jnp.stack([other, mine], axis)
-    )
-
-
-def gather_depth(block):
-    depth = lax.axis_size("rows") // 4
-    place = rows_place()[2]
-    parts = [block] + [shift_depth(block, step) for step in range(1, depth)]
-    turned = [parts[-step % depth] for step in range(depth)]
-    twice = jnp.stack(turned + turned)
-    return lax.dynamic_slice_in_dim(twice, depth - place, depth, 0)
+    return lax.ppermute(block, "rows", [(place, place ^ (4 * step)) for place in range(count)])
 
 
 def halves(block):
@@ -931,17 +938,14 @@
     return block[..., :cut], block[..., cut:]
 
 
-def join_one_kernel(depth, count, bits_ref, *refs):
+def join_one_kernel(offsets, bits_ref, *refs):
     place = bits_ref[2]
-    ins, outs = refs[: depth * count], refs[len(refs) - 2 * count :]
-    for number in range(count):
-        first, second = outs[2 * number : 2 * number + 2]
-        cut = first.shape[-1]
-        for step in range(depth):
-            spot = lax.rem(place - step + depth, depth)
-            part = ins[number * depth + step][...]
-            first[spot] = part[:, :cut]
-            second[spot] = part[:, cut:]
+    ins, (first, second) = refs[: len(offsets)], refs[-2:]
+    cut = first.shape[-1]
+    for offset, part_ref in zip(offsets, ins):
+        part = part_ref[...]
+        first[place ^ offset] = part[:, :cut]
+        second[place ^ offset] = part[:, cut:]
 
 
 def join_two_kernel(count, bits_ref, *refs):
@@ -957,20 +961,17 @@
             joined_two[level, 1 - y] = second_far[level]
 
 
-def join_three_kernel(splits, bits_ref, first, first_far, second, second_far, *refs):
+def join_three_kernel(begin, bits_ref, first, first_far, second, second_far, *refs):
     x, y = bits_ref[0], bits_ref[1]
-    outs = refs[len(refs) - len(splits) :]
+    joined = refs[-1]
     cut = first.shape[-1]
-    begin = 0
-    for size, joined in zip(splits, outs):
-        rows = slice(begin, begin + size)
-        for level in range(first.shape[0]):
-            for side in range(2):
-                joined[level, y, side, :, :cut] = first[level, side, rows]
-                joined[level, 1 - y, side, :, :cut] = first_far[level, side, rows]
-                joined[level, side, x, :, cut:] = second[level, side, rows]
-                joined[level, side, 1 - x, :, cut:] = second_far[level, side, rows]
-        begin += size
+    rows = slice(begin, begin + joined.shape[3])
+    for level in range(first.shape[0]):
+        for side in range(2):
+            joined[level, y, side, :, :cut] = first[level, side, rows]
+            joined[level, 1 - y, side, :, :cut] = first_far[level, side, rows]
+            joined[level, side, x, :, cut:] = second[level, side, rows]
+            joined[level, side, 1 - x, :, cut:] = second_far[level, side, rows]
 
 
 def carry_kernel(weight_ref, *refs):
@@ -1064,11 +1065,10 @@
 
 
 class Gather:
-    def __init__(self, block, splits=None):
+    def __init__(self, block):
         self.depth = lax.axis_size("rows") // 4
         self.bits = jnp.stack(rows_place()).astype(jnp.int32)
         self.rows, self.columns = block.shape
-        self.splits = splits or (self.rows,)
         self.cut = self.columns // 256 * 128
         self.held = [block]
 
@@ -1088,10 +1088,16 @@
         return [lead + (self.rows, self.cut), lead + (self.rows, self.columns - self.cut)]
 
     def shift(self):
-        self.far = [shift_depth(self.held[0], step) for step in range(1, self.depth)]
+        held = [(0, self.held[0])]
+        bit = self.depth // 2
+        while bit:
+            held += [(offset ^ bit, swap_depth(block, bit)) for offset, block in held]
+            bit //= 2
+        self.offsets = [offset for offset, _ in held]
+        self.far = [block for _, block in held[1:]]
 
     def join_one(self, *earlier):
-        kernel = partial(join_one_kernel, self.depth, 1)
+        kernel = partial(join_one_kernel, self.offsets)
         self.held = self.call(kernel, "join_one", self.held + self.far, self.shapes(self.depth), earlier)
         return self.held
 
@@ -1109,15 +1115,10 @@
         self.held = self.call(kernel, "join_two", self.pairs(), self.shapes(self.depth, 2), earlier)
         return self.held
 
-    def join_three(self, *earlier):
-        shapes = [(self.depth, 2, 2, rows, self.columns) for rows in self.splits]
-        kernel = partial(join_three_kernel, self.splits)
-        self.held = self.call(kernel, "join_three", self.pairs(), shapes, earlier)
-        return self.held
-
-    def swap_cores(self):
-        flat = [block.reshape(-1, self.columns) for block in self.held]
-        return [(block, swap_img(block)) for block in flat]
+    def join_three(self, begin, rows, *earlier):
+        shapes = [(self.depth, 2, 2, rows, self.columns)]
+        kernel = partial(join_three_kernel, begin)
+        return self.call(kernel, "join_three", self.pairs(), shapes, earlier)[0].reshape(-1, self.columns)
 
 
 def fold_one_kernel(count, bits_ref, *refs):
@@ -1163,12 +1164,12 @@
     keep, gives = refs[-depth], refs[len(refs) - depth + 1 :]
     cut = a_near.shape[-1]
     for step, out in enumerate((keep,) + tuple(gives)):
-        spot = lax.rem(place + step, depth)
+        spot = place ^ step
         out[:, :cut] = (a_near[spot] + a_far[spot].astype(F32)).astype(out.dtype)
         out[:, cut:] = (b_near[spot] + b_far[spot].astype(F32)).astype(out.dtype)
 
 
-def fold_call(kernel, name, bits, values, outs, earlier):
+def fold_call(kernel, name, bits, values, outs, earlier, estimate):
     vmem = pl.BlockSpec(memory_space=pltpu.VMEM)
     return pl.pallas_call(
         kernel,
@@ -1177,13 +1178,14 @@
         out_specs=[vmem] * len(outs),
         out_shape=[jax.ShapeDtypeStruct(shape, kind) for shape, kind in outs],
         compiler_params=pltpu.CompilerParams(vmem_limit_bytes=VMEM_LIMIT),
-        cost_estimate=cost(2.3),
+        cost_estimate=cost(estimate),
         name=name,
     )(bits, *values, *earlier)
 
 
 class Scatter:
-    def __init__(self, give, keep):
+    def __init__(self, give, keep, costs):
+        self.costs = costs
         self.depth = lax.axis_size("rows") // 4
         self.columns = sum(part.shape[-1] for part in keep)
         self.cut = self.columns // 256 * 128
@@ -1202,7 +1204,7 @@
     def fold_one(self, *earlier):
         values = [part.reshape(self.shape) for part in list(self.keep) + self.far]
         kernel = partial(fold_one_kernel, len(self.keep))
-        self.out = fold_call(kernel, "fold_one", self.bits, values, self.outs(self.depth, 2), earlier)
+        self.out = fold_call(kernel, "fold_one", self.bits, values, self.outs(self.depth, 2), earlier, self.costs[0])
         return self.out
 
     def swap_middle(self):
@@ -1212,7 +1214,7 @@
     def fold_two(self, *earlier):
         values = [self.out[1], self.far[0], self.out[3], self.far[1]]
         self.out = fold_call(
-            fold_two_kernel, "fold_two", self.bits, values, self.outs(self.depth), earlier
+            fold_two_kernel, "fold_two", self.bits, values, self.outs(self.depth), earlier, self.costs[1]
         )
         return self.out
 
@@ -1232,13 +1234,13 @@
             out_shape=[jax.ShapeDtypeStruct(block, F32)]
             + [jax.ShapeDtypeStruct(block, BF) for _ in range(depth - 1)],
             compiler_params=pltpu.CompilerParams(vmem_limit_bytes=VMEM_LIMIT),
-            cost_estimate=cost(2.5),
+            cost_estimate=cost(self.costs[2]),
             name="fold_three",
         )(self.bits, self.out[1], self.far[0], self.out[3], self.far[1], *earlier)
         return self.out
 
     def swap_last(self):
-        return [self.out[0]] + [shift_depth(self.out[step], step) for step in range(1, self.depth)]
+        return [self.out[0]] + [swap_depth(self.out[step], step) for step in range(1, self.depth)]
 
     def last(self):
         parts = self.swap_last()
@@ -1313,50 +1315,41 @@
         pre_gain, pre_bias, triple_bias, output_bias, post_gain, post_bias, expand_bias, reduce_bias,
     )
 
-    far_tokens = to_odd(tokens[WIN:, :REAL])
+    far_rows = to_odd(jnp.concatenate([tokens[WIN:, :REAL], cotangent[WIN:, :REAL]]))
+    later_all = lax.all_gather(
+        jnp.concatenate([expand_weight, output_weight], 1), ("img", "rows"), axis=0, tiled=True
+    )
     one = Gather(then(carry(triple_weight, vectors)))
     one.shift()
-    two = Gather(
-        then(stack([reduce_weight, output_weight], *last)), (reduce_weight.shape[0], block)
-    )
+    two = Gather(then(stack([reduce_weight], *last)))
     then(one.join_one(*last))
     one.swap_near()
     two.shift()
-    x = then(pack(parity, tokens, far_tokens, mask, False, *last))
-    three = Gather(then(stack([expand_weight], *last)))
-    then(one.join_two(*last, *two.far[::2]))
+    x = then(pack(parity, tokens, far_rows, mask, 0, *last))
+    then(one.join_two(*last, *two.far[:-1]))
     one.swap_far()
-    far_pulls = to_odd(cotangent[WIN:, :REAL])
-    then(one.join_three(*last, *two.far[1::2]))
-    (triple_pair,) = one.swap_cores()
+    incoming = then(pack(parity, cotangent, far_rows, mask, moved, *last))
+    triple_near = then(one.join_three(0, block, *last, two.far[-1]))
+    triple_pair = triple_near, swap_img(triple_near)
     then(two.join_one(*last))
     two.swap_near()
     rows, offsets, fill, hidden_bias = then(spread(img, *triple_pair, block, *last))
-    three.shift()
-    incoming = then(pack(parity, cotangent, far_pulls, mask, True, *last))
+    entry, joint = then(project(img, x, mask, rows, *triple_pair, offsets, *last))
     then(two.join_two(*last))
     two.swap_far()
-    entry, joint = then(project(img, x, mask, rows, *triple_pair, offsets, *last))
-    heads = then(attend(joint, fill, table, 0, 3, (), *last, *three.far[::2]))
-    then(three.join_one(*last))
-    three.swap_near()
-    mixed, lse, features = then(attend(joint, fill, table, 3, 3, heads, *last))
-    then(two.join_three(*last))
-    reduce_pair, output_pair = two.swap_cores()
-    then(three.join_two(*last))
-    three.swap_far()
-    middle, entry_two = then(mix(img, mixed, *output_pair, rows, x, mask, *last))
-    then(three.join_three(*last))
-    (expand_pair,) = three.swap_cores()
+    mixed, lse, features = then(attend(joint, fill, table, 0, HEADS // 2, (), *last))
+    reduce_near = then(two.join_three(0, reduce_weight.shape[0], *last))
+    reduce_pair = reduce_near, swap_img(reduce_near)
+    middle, entry_two = then(mix(mixed, later_all, rows, x, mask, *last))
 
     result, grad_entry_two, reduce_grad, expand_far, expand_near, hidden_sums = then(
-        mlp(img, entry_two, incoming, *expand_pair, hidden_bias, *reduce_pair, *last)
+        mlp(img, entry_two, incoming, later_all, hidden_bias, *reduce_pair, *last)
     )
     reduce_shard = lax.psum_scatter(reduce_grad, ("img", "rows"), scatter_dimension=0, tiled=True).astype(F32)
     grad_middle, grad_mixed, output_far, output_near, out_win, mix_sums = then(
-        mix_back(img, grad_entry_two, result, middle, incoming, mask, rows, *output_pair, mixed, *last)
+        mix_back(img, grad_entry_two, result, middle, incoming, mask, rows, later_all, mixed, *last)
     )
-    first_sum = Scatter([expand_far, output_far], [expand_near, output_near])
+    first_sum = Scatter([expand_far, output_far], [expand_near, output_near], (2.3, 2.3, 1.5))
     first_sum.swap_near()
     then(first_sum.fold_one(*last))
     first_sum.swap_middle()
@@ -1365,7 +1358,7 @@
         attend_back(joint, grad_mixed, lse, features, fill, table, 0, HEADS // 2, *last)
     )
     joint_far, joint_near = then(entry_grads(img, entry, grad_joint, *last))
-    last_sum = Scatter([joint_far], [joint_near])
+    last_sum = Scatter([joint_far], [joint_near], (2.3, 2.3, 1.5))
     last_sum.swap_near()
     then(first_sum.fold_two(*last))
     first_sum.swap_far()
@@ -1377,22 +1370,21 @@
     then(first_sum.fold_three(*last))
     first_parts = first_sum.swap_last()
     small = then(sums(norm_sums, joint_sums, mix_sums, hidden_sums, tables, *last))
+    depths = [small] + [swap_depth(small, step) for step in range(1, lax.axis_size("rows") // 4)]
     grad_rows = to_even(then(send_rows(grad_win, moved, *last)))
-    small = then(add(small, swap_img(small), *last))
-    block_output = then(unpack(parity, out_win, out_rows, tokens.shape, *last))
+    block_output = then(unpack(parity, out_win, out_rows, tokens.shape, *last, *first_parts[1:2]))
     then(last_sum.fold_two(*last))
     last_sum.swap_far()
+    small = then(add_depth(last_sum.bits, depths, *last))
+    expand_shard, output_shard = then(settle(first_parts, expand_far.shape[1], *last))
     small = then(add(small, swap_rows(small, 0), *last))
-    expand_shard, output_shard = then(settle(first_parts, expand_far.shape[1], *last))
     then(last_sum.fold_three(*last))
     last_parts = last_sum.swap_last()
     small = then(add(small, swap_rows(small, 1), *last))
-    depths = [small] + [shift_depth(small, step) for step in range(1, lax.axis_size("rows") // 4)]
     input_grad = then(unpack(parity, grad_win, grad_rows, tokens.shape, *last))
     triple_shard = then(place(last_parts, *last))
-    number = img * lax.axis_size("rows") + lax.axis_index("rows")
-    number = jnp.stack([number, rows_place()[2]]).astype(jnp.int32)
-    shares = share(number, depths, block, height_table.shape[0], *last)
+    number = (img * lax.axis_size("rows") + lax.axis_index("rows")).astype(jnp.int32)
+    shares = share(number, small, swap_img(small), block, height_table.shape[0], *last)
     pre_gain_grad, pre_bias_grad, output_bias_grad, post_gain_grad, post_bias_grad, reduce_bias_grad = [
         array.reshape(-1) for array in shares[:6]
     ]

time: 319 us -> 287 us (0.90)
  starting transfers between devices: 65 us -> 51.2 us
  Pallas kernels: 173 us -> 161 us
  local copies, waits for them, and re-layouts: 26.4 us -> 22.9 us
    ppermute x18 -> x15, starting transfers between devices: 33.4 us -> 23.2 us  [swap_depth(): lax.ppermute(block, 'rows', [(place, place ^ 4 * step) for place in range...]
    pallas_call x9 -> x6, Pallas kernels: 22.9 us -> 14.8 us  [call(): pl.pallas_call(kernel, in_specs=[pl.BlockSpec(memory_space=pltpu.SMEM)] +...]
    ppermute x8 -> x6, waiting for transfers between devices: 6.71 us -> 2.14 us  [swap_img(): return lax.ppermute(block, 'img', [(0, 1), (1, 0)])]
    unnamed x134 -> x112, local copies, waits for them, and re-layouts: 22.8 us -> 19.2 us
    ppermute x2 -> x1, starting transfers between devices: 6.66 us -> 3.77 us  [to_odd(): lax.ppermute(block, 'rows', [(place, place + 1) for place in range(0, cou...]
    pallas_call x2 -> x1, Pallas kernels: 13.2 us -> 11.2 us  [attend(): pl.pallas_call(ordered(attend_kernel, 7, tuple(given) + earlier), grid=(c...]
    ppermute x22 -> x18, waiting for transfers between devices: 13.8 us -> 11.8 us  [swap_rows(): lax.ppermute(block, 'rows', [(place, place ^ 1 << bit) for place in range...]
    ppermute x18 -> x15, waiting for transfers between devices: 12.9 us -> 14 us  [swap_depth(): lax.ppermute(block, 'rows', [(place, place ^ 4 * step) for place in range...]
  transfers between devices with their start and end apart: 53 -> 44, of which waited for: 11 -> 12; matrix products, arithmetic and copies ran while one was open for 2% -> 2% of each run, Pallas kernels for 43% -> 46%
where the time goes in v3:
time: 287 us; the launch traced here: 286 us
  Pallas kernels  161 us (56%)
  starting transfers between devices  51.2 us (18%)
  waiting for transfers between devices  30.7 us (11%)
  local copies, waits for them, and re-layouts  22.9 us (8%)
  between operations  14.5 us (5%)
  other arithmetic  5.93 us (2%)
    pallas_call x1, Pallas kernels, mlp(): pl.pallas_call(ordered(mlp_kernel, 7, earlier), grid_spec=pltpu.PrefetchS...  28.5 us
    ppermute x15, starting transfers between devices, swap_depth(): lax.ppermute(block, 'rows', [(place, place ^ 4 * step) for place in range...  23.2 us
    ppermute x18, starting transfers between devices, swap_rows(): lax.ppermute(block, 'rows', [(place, place ^ 1 << bit) for place in range...  21.1 us
    unnamed x112, local copies, waits for them, and re-layouts  19.2 us
    pallas_call x4, Pallas kernels, fold_call(): pl.pallas_call(kernel, in_specs=[pl.BlockSpec(memory_space=pltpu.SMEM)] +...  15.5 us
    pallas_call x6, Pallas kernels, call(): pl.pallas_call(kernel, in_specs=[pl.BlockSpec(memory_space=pltpu.SMEM)] +...  14.8 us
    pallas_call x1, Pallas kernels, attend_back(): pl.pallas_call(kernel, grid=(count,), in_specs=[column(begin), column(pai...  14.6 us
    ppermute x15, waiting for transfers between devices, swap_depth(): lax.ppermute(block, 'rows', [(place, place ^ 4 * step) for place in range...  14 us
  transfers between devices with their start and end apart: 44, of which 12 were waited for; matrix products, arithmetic and copies ran while one was open for 2% of the time, Pallas kernels for 46%

profile of v3, /device:TPU:0, one launch (start us, length us, event | category | flops | bytes accessed | tf_op | source)
XLA Modules:
  0.0 286.0 jit_solution(13092657926414980928)
XLA Ops:
  10.6 3.0 %collective-permute-start.2 = (bf16[24,2432]{1,0:T(8,128)(2,1)}, bf16[24,2432]{1,0:T(8,128)(2,1)S(1)}, u32[]{:S(2)}, u32[]{:S(2)}) collective-permute-start(bf16[24,2432]{1,0:T(8,128)(2,1)} %carry.1.refs_1_.refs_0_), channel_id=1, source_target_pairs={{0,4},{1,5},{2,6},{3,7},{4,0},{5,1},{6,2},{7,3},{8,12},{9,13},{10,... | collective-permute-start | bytes 350216 | tf_op jit(solution)/shard_map/ppermute | solution.py:933
  20.5 3.8 %collective-permute-start = (bf16[14,32,768]{2,1,0:T(8,128)(2,1)S(1)}, bf16[14,32,768]{2,1,0:T(8,128)(2,1)S(1)}, u32[]{:S(2)}, u32[]{:S(2)}) collective-permute-start(bf16[14,32,768]{2,1,0:T(8,128)(2,1)S(1)} %pad_maximum_fusion), channel_id=1, source_target_pairs={{0,1},{2,3},{4,5},{6,7},{8,9},{10,11},{12,13},{14,15},{16,17},{18,... | collective-permute-start | bytes 2064392 | tf_op jit(solution)/shard_map/ppermute | solution.py:1266
  40.9 2.9 %pack.2.refs_4_.refs_1_.refs_3_.x_ref = bf16[624,768]{1,0:T(8,128)(2,1)} custom-call(s32[1]{0:T(128)} %bitcast.refs_0_, bf16[21,42,768]{2,1,0:T(8,128)(2,1)} %refs_1_.2, bf16[14,32,768]{2,1,0:T(8,128)(2,1)} %copy-done.23, f32[624,1]{1,0:T(8,128)} %reshape.149.refs_3_.refs_2_.refs_4_.refs_5_.mask_ref, bf16[4,24,1152]{2,1,0:T(8,128)(2,1)} %get-tuple-element.90.refs_4_.refs_0_), custom_call_target="tpu_custom_call" | custom-call | flops 3000000000 | bytes 1 | tf_op jit(solution)/shard_map/pack/pallas_call | solution.py:378
  43.8 3.7 %collective-permute-done.4.refs_1_ = bf16[4,24,1152]{2,1,0:T(8,128)(2,1)S(1)} collective-permute-done((bf16[4,24,1152]{2,1,0:T(8,128)(2,1)}, bf16[4,24,1152]{2,1,0:T(8,128)(2,1)S(1)}, u32[]{:S(2)}, u32[]{:S(2)}) %collective-permute-start.4) | collective-permute-done | bytes 221216 | tf_op jit(solution)/shard_map/ppermute | solution.py:924
  56.7 3.0 %pack.3.refs_0_.refs_2_.refs_4_ = bf16[624,768]{1,0:T(8,128)(2,1)} custom-call(s32[1]{0:T(128)} %bitcast.refs_0_, bf16[21,42,768]{2,1,0:T(8,128)(2,1)} %refs_1_.3, bf16[14,32,768]{2,1,0:T(8,128)(2,1)} %copy-done.23, f32[624,1]{1,0:T(8,128)} %reshape.149.refs_3_.refs_2_.refs_4_.refs_5_.mask_ref, bf16[4,2,24,1152]{3,2,1,0:T(8,128)(2,1)} %get-tuple-element.92.refs_4_.first), custom_call_target="tpu_custom_call" | custom-call | flops 3000000000 | bytes 1 | tf_op jit(solution)/shard_map/pack/pallas_call | solution.py:378
  63.7 2.8 join_three.2
  75.3 7.2 %project.1 = (bf16[624,768]{1,0:T(8,128)(2,1)}, bf16[624,2304]{1,0:T(8,128)(2,1)}) custom-call(s32[1]{0:T(128)} %bitcast.1.refs_0_.img_ref, bf16[624,768]{1,0:T(8,128)(2,1)} %pack.2.refs_4_.refs_1_.refs_3_.x_ref, f32[624,1]{1,0:T(8,128)} %reshape.149.refs_3_.refs_2_.refs_4_.refs_5_.mask_ref, f32[8,768]{1,0:T(8,128)} %get-tuple-element.95.refs_3_.refs_2_.refs_6_.rows_ref, ...), custom_call_target="tpu_custom_call" | custom-call | flops 7000000000 | bytes 1 | tf_op jit(solution)/shard_map/project/pallas_call | solution.py:565
  87.2 11.2 %attend.1 = (bf16[624,768]{1,0:T(8,128)(2,1)}, f32[6,8,1536]{2,1,0:T(8,128)}, bf16[624,768]{1,0:T(8,128)(2,1)}) custom-call(bf16[624,2304]{1,0:T(8,128)(2,1)} %get-tuple-element.98.refs_0_.refs_1_.refs_2_, bf16[624,2304]{1,0:T(8,128)(2,1)} %get-tuple-element.98.refs_0_.refs_1_.refs_2_, bf16[624,2304]{1,0:T(8,128)(2,1)} %get-tuple-element.98.refs_0_.refs_1_.refs_2_, ...), custom_call_target="tpu_custom_call" | custom-call | flops 11000000512 | bytes 1 | tf_op jit(solution)/shard_map/attend/pallas_call | solution.py:280
  98.4 2.8 collective-permute-done.15.second_far
  102.8 3.3 %join_three.3 = bf16[4,2,2,96,768]{4,3,2,1,0:T(8,128)(2,1)} custom-call(s32[3]{0:T(128)} %pad_add_fusion.bits_ref.refs_0_, bf16[4,2,96,384]{3,2,1,0:T(8,128)(2,1)} %get-tuple-element.101.refs_7_.first, bf16[4,2,96,384]{3,2,1,0:T(8,128)(2,1)} %copy-done.26, bf16[4,2,96,384]{3,2,1,0:T(8,128)(2,1)} %get-tuple-element.103.second, ...), custom_call_target="tpu_custom_call" | custom-call | flops 2300000000 | bytes 1 | tf_op jit(solution)/shard_map/join_three/pallas_call | solution.py:1077
  106.1 4.7 %mix.1 = (f32[624,768]{1,0:T(8,128)}, bf16[624,768]{1,0:T(8,128)(2,1)}) custom-call(bf16[624,768]{1,0:T(8,128)(2,1)} %get-tuple-element.102.refs_0_.refs_8_, bf16[768,3840]{1,0:T(8,128)(2,1)} %all-gather.2.cloned.1.call-done.refs_1_.refs_3_.refs_7_, f32[8,768]{1,0:T(8,128)} %get-tuple-element.95.refs_3_.refs_2_.refs_6_.rows_ref, ...), custom_call_target="tpu_custom_call" | custom-call | flops 4600000000 | bytes 1 | tf_op jit(solution)/shard_map/mix/pallas_call | solution.py:662
  112.2 28.5 %mlp.1 = (f32[624,768]{1,0:T(8,128)}, f32[624,768]{1,0:T(8,128)}, bf16[3072,768]{1,0:T(8,128)(2,1)}, bf16[384,3072]{1,0:T(8,128)(2,1)}, bf16[384,3072]{1,0:T(8,128)(2,1)}, /*index=5*/f32[1,3072]{1,0:T(1,128)}) custom-call(s32[1]{0:T(128)} %bitcast.1.refs_0_.img_ref, bf16[624,768]{1,0:T(8,128)(2,1)} %get-tuple-element.105.refs_1_, ...), custom_call_target="tpu_custom_call" | custom-call | flops 28999999488 | bytes 1 | tf_op jit(solution)/shard_map/mlp/pallas_call | solution.py:512
  141.2 8.5 %mix_back.1 = (f32[624,768]{1,0:T(8,128)}, bf16[624,768]{1,0:T(8,128)(2,1)}, bf16[384,768]{1,0:T(8,128)(2,1)}, bf16[384,768]{1,0:T(8,128)(2,1)}, bf16[624,768]{1,0:T(8,128)(2,1)}, /*index=5*/f32[4,768]{1,0:T(4,128)}) custom-call(s32[1]{0:T(128)} %bitcast.1.refs_0_.img_ref, f32[624,768]{1,0:T(8,128)} %get-tuple-element.108.refs_1_, ...), custom_call_target="tpu_custom_call" | custom-call | flops 7000000000 | bytes 1 | tf_op jit(solution)/shard_map/mix_back/pallas_call | solution.py:712
  153.5 5.1 %fold_one.2 = (bf16[4,2,24,1920]{3,2,1,0:T(8,128)(2,1)}, f32[4,2,24,1920]{3,2,1,0:T(8,128)}, bf16[4,2,24,1920]{3,2,1,0:T(8,128)(2,1)}, f32[4,2,24,1920]{3,2,1,0:T(8,128)}) custom-call(s32[3]{0:T(128)} %pad_add_fusion.bits_ref.refs_0_, bf16[4,2,2,24,3072]{4,3,2,1,0:T(8,128)(2,1)} %bitcast.56, bf16[4,2,2,24,768]{4,3,2,1,0:T(8,128)(2,1)} %bitcast.58, ...), custom_call_target="tpu_custom_call" | custom-call | flops 2300000000 | bytes 1 | tf_op jit(solution)/shard_map/fold_one/pallas_call | solution.py:1174
  162.3 14.6 %attend_back.1 = (bf16[624,2304]{1,0:T(8,128)(2,1)}, f32[6,128,128]{2,1,0:T(8,128)}, f32[2,768]{1,0:T(2,128)}) custom-call(bf16[624,2304]{1,0:T(8,128)(2,1)} %get-tuple-element.98.refs_0_.refs_1_.refs_2_, bf16[624,2304]{1,0:T(8,128)(2,1)} %get-tuple-element.98.refs_0_.refs_1_.refs_2_, bf16[624,2304]{1,0:T(8,128)(2,1)} %get-tuple-element.98.refs_0_.refs_1_.refs_2_, ...), custom_call_target="tpu_custom_call" | custom-call | flops 8999999488 | bytes 1 | tf_op jit(solution)/shard_map/attend_back/pallas_call | solution.py:305
  176.9 6.8 %entry_grads.1 = (bf16[384,2304]{1,0:T(8,128)(2,1)}, bf16[384,2304]{1,0:T(8,128)(2,1)}) custom-call(s32[1]{0:T(128)} %bitcast.1.refs_0_.img_ref, bf16[624,768]{1,0:T(8,128)(2,1)} %get-tuple-element.100.refs_4_.refs_1_, bf16[624,2304]{1,0:T(8,128)(2,1)} %get-tuple-element.121.refs_2_.pull_ref, f32[2,768]{1,0:T(2,128)} %get-tuple-element.125.refs_3_.refs_1_), custom_call_target="tpu_custom_call" | custom-call | flops 5000000000 | bytes 1 | tf_op jit(solution)/shard_map/entry_grads/pallas_call | solution.py:750
  186.2 3.8 %fold_two.2 = (bf16[4,24,1920]{2,1,0:T(8,128)(2,1)}, f32[4,24,1920]{2,1,0:T(8,128)}, bf16[4,24,1920]{2,1,0:T(8,128)(2,1)}, f32[4,24,1920]{2,1,0:T(8,128)}) custom-call(s32[3]{0:T(128)} %pad_add_fusion.bits_ref.refs_0_, f32[4,2,24,1920]{3,2,1,0:T(8,128)} %get-tuple-element.122.a_near, bf16[4,2,24,1920]{3,2,1,0:T(8,128)(2,1)} %copy-done.22, ...), custom_call_target="tpu_custom_call" | custom-call | flops 2300000000 | bytes 1 | tf_op jit(solution)/shard_map/fold_two/pallas_call | solution.py:1174
  194.2 11.2 %project_back.1 = (bf16[624,768]{1,0:T(8,128)(2,1)}, f32[2,768]{1,0:T(2,128)}) custom-call(s32[1]{0:T(128)} %bitcast.1.refs_0_.img_ref, bf16[624,768]{1,0:T(8,128)(2,1)} %pack.2.refs_4_.refs_1_.refs_3_.x_ref, f32[624,1]{1,0:T(8,128)} %reshape.149.refs_3_.refs_2_.refs_4_.refs_5_.mask_ref, f32[8,768]{1,0:T(8,128)} %get-tuple-element.95.refs_3_.refs_2_.refs_6_.rows_ref, ...), custom_call_target="tpu_custom_call" | custom-call | flops 11000000512 | bytes 1 | tf_op jit(solution)/shard_map/project_back/pallas_call | solution.py:625
  206.7 3.7 %fold_one.3 = (bf16[4,2,24,1152]{3,2,1,0:T(8,128)(2,1)}, f32[4,2,24,1152]{3,2,1,0:T(8,128)}, bf16[4,2,24,1152]{3,2,1,0:T(8,128)(2,1)}, f32[4,2,24,1152]{3,2,1,0:T(8,128)}) custom-call(s32[3]{0:T(128)} %pad_add_fusion.bits_ref.refs_0_, bf16[4,2,2,24,2304]{4,3,2,1,0:T(8,128)(2,1)} %bitcast.57, bf16[4,2,2,24,2304]{4,3,2,1,0:T(8,128)(2,1)} %bitcast.46, ...), custom_call_target="tpu_custom_call" | custom-call | flops 2300000000 | bytes 1 | tf_op jit(solution)/shard_map/fold_one/pallas_call | solution.py:1174
  225.9 2.9 %unpack.2.refs_0_ = bf16[21,42,768]{2,1,0:T(8,128)(2,1)} custom-call(s32[1]{0:T(128)} %bitcast.refs_0_, bf16[624,768]{1,0:T(8,128)(2,1)} %get-tuple-element.111.refs_0_.refs_1_, bf16[7,32,768]{2,1,0:T(8,128)(2,1)} %copy-done.4, bf16[7,32,768]{2,1,0:T(8,128)(2,1)} %send_rows.3.refs_3_, bf16[24,3840]{1,0:T(8,128)(2,1)} %copy-done.6), custom_call_target="tpu_custom_call" | custom-call | flops 500000000 | bytes 1 | tf_op jit(solution)/shard_map/unpack/pallas_call | solution.py:407
  231.9 2.9 %fold_two.3 = (bf16[4,24,1152]{2,1,0:T(8,128)(2,1)}, f32[4,24,1152]{2,1,0:T(8,128)}, bf16[4,24,1152]{2,1,0:T(8,128)(2,1)}, f32[4,24,1152]{2,1,0:T(8,128)}) custom-call(s32[3]{0:T(128)} %pad_add_fusion.bits_ref.refs_0_, f32[4,2,24,1152]{3,2,1,0:T(8,128)} %get-tuple-element.138.a_near, bf16[4,2,24,1152]{3,2,1,0:T(8,128)(2,1)} %copy-done.29, ...), custom_call_target="tpu_custom_call" | custom-call | flops 2300000000 | bytes 1 | tf_op jit(solution)/shard_map/fold_two/pallas_call | solution.py:1174
  239.8 7.9 %collective-permute-done.33.refs_2_ = bf16[24,3840]{1,0:T(8,128)(2,1)S(1)} collective-permute-done((bf16[24,3840]{1,0:T(8,128)(2,1)S(1)}, bf16[24,3840]{1,0:T(8,128)(2,1)S(1)}, u32[]{:S(2)}, u32[]{:S(2)}) %collective-permute-start.33) | collective-permute-done | bytes 184352 | tf_op jit(solution)/shard_map/ppermute | solution.py:933
  266.2 2.9 %unpack.3.refs_4_ = bf16[21,42,768]{2,1,0:T(8,128)(2,1)} custom-call(s32[1]{0:T(128)} %bitcast.refs_0_, bf16[624,768]{1,0:T(8,128)(2,1)} %get-tuple-element.128.refs_0_.refs_1_, bf16[7,32,768]{2,1,0:T(8,128)(2,1)} %copy-done.2, f32[24,768]{1,0:T(8,128)} %add.49.refs_3_.refs_1_), custom_call_target="tpu_custom_call" | custom-call | flops 500000000 | bytes 1 | tf_op jit(solution)/shard_map/unpack/pallas_call | solution.py:407
  269.1 2.9 %collective-permute-done.40.refs_2_ = bf16[24,2304]{1,0:T(8,128)(2,1)S(1)} collective-permute-done((bf16[24,2304]{1,0:T(8,128)(2,1)}, bf16[24,2304]{1,0:T(8,128)(2,1)S(1)}, u32[]{:S(2)}, u32[]{:S(2)}) %collective-permute-start.40) | collective-permute-done | bytes 110624 | tf_op jit(solution)/shard_map/ppermute | solution.py:933
  (230 shorter events, 121.5 us)
Async XLA Ops:
  7.2 98.9 %all-gather.2.cloned.1.call-start = ((), (), s32[]{:S(2)}) async-start(), calls=%async_computation.1 | async-start | bytes 6082560 | tf_op jit(solution)/shard_map/all_gather | solution.py:1319
  8.9 268.6 %reduce-scatter.2.cloned.1.call-start = ((), (), s32[]{:S(2)}) async-start(), calls=%async_computation.2 | async-start | bytes 4866048 | tf_op jit(solution)/shard_map/reduce_scatter | solution.py:1348
  10.6 18.6 %collective-permute-start.2 = (bf16[24,2432]{1,0:T(8,128)(2,1)}, bf16[24,2432]{1,0:T(8,128)(2,1)S(1)}, u32[]{:S(2)}, u32[]{:S(2)}) collective-permute-start(bf16[24,2432]{1,0:T(8,128)(2,1)} %carry.1.refs_1_.refs_0_), channel_id=1, source_target_pairs={{0,4},{1,5},{2,6},{3,7},{4,0},{5,1},{6,2},{7,3},{8,12},{9,13},{10,... | collective-permute-start | bytes 350216 | tf_op jit(solution)/shard_map/ppermute | solution.py:933
  17.8 26.0 %collective-permute-start.7 = (bf16[96,768]{1,0:T(8,128)(2,1)}, bf16[96,768]{1,0:T(8,128)(2,1)S(1)}, u32[]{:S(2)}, u32[]{:S(2)}) collective-permute-start(bf16[96,768]{1,0:T(8,128)(2,1)} %stack.10.refs_4_.refs_0_), channel_id=1, source_target_pairs={{0,4},{1,5},{2,6},{3,7},{4,0},{5,1},{6,2},{7,3},{8,12},{9,13},{10,... | collective-permute-start | bytes 442376 | tf_op jit(solution)/shard_map/ppermute | solution.py:933
  18.4 25.5 %collective-permute-start.6 = (bf16[96,768]{1,0:T(8,128)(2,1)}, bf16[96,768]{1,0:T(8,128)(2,1)S(1)}, u32[]{:S(2)}, u32[]{:S(2)}) collective-permute-start(bf16[96,768]{1,0:T(8,128)(2,1)} %stack.10.refs_4_.refs_0_), channel_id=1, source_target_pairs={{0,8},{1,9},{2,10},{3,11},{4,12},{5,13},{6,14},{7,15},{8,0},{9,1},... | collective-permute-start | bytes 442376 | tf_op jit(solution)/shard_map/ppermute | solution.py:933
  20.5 19.6 %collective-permute-start = (bf16[14,32,768]{2,1,0:T(8,128)(2,1)S(1)}, bf16[14,32,768]{2,1,0:T(8,128)(2,1)S(1)}, u32[]{:S(2)}, u32[]{:S(2)}) collective-permute-start(bf16[14,32,768]{2,1,0:T(8,128)(2,1)S(1)} %pad_maximum_fusion), channel_id=1, source_target_pairs={{0,1},{2,3},{4,5},{6,7},{8,9},{10,11},{12,13},{14,15},{16,17},{18,... | collective-permute-start | bytes 2064392 | tf_op jit(solution)/shard_map/ppermute | solution.py:1266
  34.3 13.2 %collective-permute-start.4 = (bf16[4,24,1152]{2,1,0:T(8,128)(2,1)}, bf16[4,24,1152]{2,1,0:T(8,128)(2,1)S(1)}, u32[]{:S(2)}, u32[]{:S(2)}) collective-permute-start(bf16[4,24,1152]{2,1,0:T(8,128)(2,1)} %get-tuple-element.90.refs_4_.refs_0_), channel_id=1, source_target_pairs={{0,1},{1,0},{2,3},{3,2},{4,5},{5,4},{6,7},{7,6},{8,9},{9,8},{10,11... | collective-permute-start | bytes 663560 | tf_op jit(solution)/shard_map/ppermute | solution.py:924
  85.8 15.4 %collective-permute-start.15 = (bf16[4,2,96,384]{3,2,1,0:T(8,128)(2,1)}, bf16[4,2,96,384]{3,2,1,0:T(8,128)(2,1)S(1)}, u32[]{:S(2)}, u32[]{:S(2)}) collective-permute-start(bf16[4,2,96,384]{3,2,1,0:T(8,128)(2,1)} %get-tuple-element.103.second), channel_id=1, source_target_pairs={{0,1},{1,0},{2,3},{3,2},{4,5},{5,4},{6,7},{7,6},{8,9},{9,8},{10,11... | collective-permute-start | bytes 1769480 | tf_op jit(solution)/shard_map/ppermute | solution.py:924
  86.8 15.2 %collective-permute-start.14 = (bf16[4,2,96,384]{3,2,1,0:T(8,128)(2,1)}, bf16[4,2,96,384]{3,2,1,0:T(8,128)(2,1)S(1)}, u32[]{:S(2)}, u32[]{:S(2)}) collective-permute-start(bf16[4,2,96,384]{3,2,1,0:T(8,128)(2,1)} %get-tuple-element.101.refs_7_.first), channel_id=1, source_target_pairs={{0,2},{1,3},{2,0},{3,1},{4,6},{5,7},{6,4},{7,5},{8,10},{9,11},{10,... | collective-permute-start | bytes 1769480 | tf_op jit(solution)/shard_map/ppermute | solution.py:924
  158.6 26.4 %collective-permute-start.21 = (bf16[4,2,24,1920]{3,2,1,0:T(8,128)(2,1)}, bf16[4,2,24,1920]{3,2,1,0:T(8,128)(2,1)S(1)}, u32[]{:S(2)}, u32[]{:S(2)}) collective-permute-start(bf16[4,2,24,1920]{3,2,1,0:T(8,128)(2,1)} %get-tuple-element.124), channel_id=1, source_target_pairs={{0,2},{1,3},{2,0},{3,1},{4,6},{5,7},{6,4},{7,5},{8,10},{9,11},{10,... | collective-permute-start | bytes 2211848 | tf_op jit(solution)/shard_map/ppermute | solution.py:924
  159.1 25.9 %collective-permute-start.20 = (bf16[4,2,24,1920]{3,2,1,0:T(8,128)(2,1)}, bf16[4,2,24,1920]{3,2,1,0:T(8,128)(2,1)S(1)}, u32[]{:S(2)}, u32[]{:S(2)}) collective-permute-start(bf16[4,2,24,1920]{3,2,1,0:T(8,128)(2,1)} %get-tuple-element.117.refs_1_), channel_id=1, source_target_pairs={{0,1},{1,0},{2,3},{3,2},{4,5},{5,4},{6,7},{7,6},{8,9},{9,8},{10,11... | collective-permute-start | bytes 2211848 | tf_op jit(solution)/shard_map/ppermute | solution.py:924
  183.7 21.6 %collective-permute-start.24 = (bf16[384,2304]{1,0:T(8,128)(2,1)}, bf16[384,2304]{1,0:T(8,128)(2,1)S(1)}, u32[]{:S(2)}, u32[]{:S(2)}) collective-permute-start(bf16[384,2304]{1,0:T(8,128)(2,1)} %get-tuple-element.126.refs_0_), channel_id=1, source_target_pairs={{0,16},{16,0},{1,17},{17,1},{2,18},{18,2},{3,19},{19,3},{4,20},{20... | collective-permute-start | bytes 5308424 | tf_op jit(solution)/shard_map/ppermute | solution.py:928
  183.7 21.6 %collective-permute-start.19 = (bf16[7,32,768]{2,1,0:T(8,128)(2,1)S(1)}, bf16[7,32,768]{2,1,0:T(8,128)(2,1)S(1)}, u32[]{:S(2)}, u32[]{:S(2)}) collective-permute-start(bf16[7,32,768]{2,1,0:T(8,128)(2,1)S(1)} %copy-done.5), channel_id=1, source_target_pairs={{1,0},{3,2},{5,4},{7,6},{9,8},{11,10},{13,12},{15,14},{17,16},{19,... | collective-permute-start | bytes 1032200 | tf_op jit(solution)/shard_map/ppermute | solution.py:1271
  190.0 22.4 %collective-permute-start.23 = (bf16[4,24,1920]{2,1,0:T(8,128)(2,1)}, bf16[4,24,1920]{2,1,0:T(8,128)(2,1)S(1)}, u32[]{:S(2)}, u32[]{:S(2)}) collective-permute-start(bf16[4,24,1920]{2,1,0:T(8,128)(2,1)} %get-tuple-element.133), channel_id=1, source_target_pairs={{0,1},{1,0},{2,3},{3,2},{4,5},{5,4},{6,7},{7,6},{8,9},{9,8},{10,11... | collective-permute-start | bytes 1105928 | tf_op jit(solution)/shard_map/ppermute | solution.py:924
  192.7 19.7 %collective-permute-start.22 = (bf16[4,24,1920]{2,1,0:T(8,128)(2,1)}, bf16[4,24,1920]{2,1,0:T(8,128)(2,1)S(1)}, u32[]{:S(2)}, u32[]{:S(2)}) collective-permute-start(bf16[4,24,1920]{2,1,0:T(8,128)(2,1)} %get-tuple-element.127.refs_0_), channel_id=1, source_target_pairs={{0,2},{1,3},{2,0},{3,1},{4,6},{5,7},{6,4},{7,5},{8,10},{9,11},{10,... | collective-permute-start | bytes 1105928 | tf_op jit(solution)/shard_map/ppermute | solution.py:924
  210.3 18.5 %collective-permute-start.31 = (bf16[4,2,24,1152]{3,2,1,0:T(8,128)(2,1)}, bf16[4,2,24,1152]{3,2,1,0:T(8,128)(2,1)S(1)}, u32[]{:S(2)}, u32[]{:S(2)}) collective-permute-start(bf16[4,2,24,1152]{3,2,1,0:T(8,128)(2,1)} %get-tuple-element.140), channel_id=1, source_target_pairs={{0,2},{1,3},{2,0},{3,1},{4,6},{5,7},{6,4},{7,5},{8,10},{9,11},{10,... | collective-permute-start | bytes 1327112 | tf_op jit(solution)/shard_map/ppermute | solution.py:924
  210.9 19.6 %collective-permute-start.30 = (bf16[4,2,24,1152]{3,2,1,0:T(8,128)(2,1)}, bf16[4,2,24,1152]{3,2,1,0:T(8,128)(2,1)S(1)}, u32[]{:S(2)}, u32[]{:S(2)}) collective-permute-start(bf16[4,2,24,1152]{3,2,1,0:T(8,128)(2,1)} %get-tuple-element.135.refs_0_), channel_id=1, source_target_pairs={{0,1},{1,0},{2,3},{3,2},{4,5},{5,4},{6,7},{7,6},{8,9},{9,8},{10,11... | collective-permute-start | bytes 1327112 | tf_op jit(solution)/shard_map/ppermute | solution.py:924
  219.3 15.5 %collective-permute-start.29 = (f32[24,768]{1,0:T(8,128)}, f32[24,768]{1,0:T(8,128)S(1)}, u32[]{:S(2)}, u32[]{:S(2)}) collective-permute-start(f32[24,768]{1,0:T(8,128)} %sums.1.refs_1_), channel_id=1, source_target_pairs={{0,12},{1,13},{2,14},{3,15},{4,8},{5,9},{6,10},{7,11},{8,4},{9,5},... | collective-permute-start | bytes 221192 | tf_op jit(solution)/shard_map/ppermute | solution.py:933
  221.6 13.9 %collective-permute-start.28 = (f32[24,768]{1,0:T(8,128)}, f32[24,768]{1,0:T(8,128)S(1)}, u32[]{:S(2)}, u32[]{:S(2)}) collective-permute-start(f32[24,768]{1,0:T(8,128)} %sums.1.refs_1_), channel_id=1, source_target_pairs={{0,8},{1,9},{2,10},{3,11},{4,12},{5,13},{6,14},{7,15},{8,0},{9,1},... | collective-permute-start | bytes 221192 | tf_op jit(solution)/shard_map/ppermute | solution.py:933
  228.8 18.9 %collective-permute-start.33 = (bf16[24,3840]{1,0:T(8,128)(2,1)S(1)}, bf16[24,3840]{1,0:T(8,128)(2,1)S(1)}, u32[]{:S(2)}, u32[]{:S(2)}) collective-permute-start(bf16[24,3840]{1,0:T(8,128)(2,1)S(1)} %copy-done.40), channel_id=1, source_target_pairs={{0,8},{1,9},{2,10},{3,11},{4,12},{5,13},{6,14},{7,15},{8,0},{9,1},... | collective-permute-start | bytes 552968 | tf_op jit(solution)/shard_map/ppermute | solution.py:933
  230.5 17.8 %collective-permute-start.34 = (bf16[24,3840]{1,0:T(8,128)(2,1)S(1)}, bf16[24,3840]{1,0:T(8,128)(2,1)S(1)}, u32[]{:S(2)}, u32[]{:S(2)}) collective-permute-start(bf16[24,3840]{1,0:T(8,128)(2,1)S(1)} %copy-done.39), channel_id=1, source_target_pairs={{0,12},{1,13},{2,14},{3,15},{4,8},{5,9},{6,10},{7,11},{8,4},{9,5},... | collective-permute-start | bytes 552968 | tf_op jit(solution)/shard_map/ppermute | solution.py:933
  234.9 20.8 %collective-permute-start.37 = (bf16[4,24,1152]{2,1,0:T(8,128)(2,1)}, bf16[4,24,1152]{2,1,0:T(8,128)(2,1)S(1)}, u32[]{:S(2)}, u32[]{:S(2)}) collective-permute-start(bf16[4,24,1152]{2,1,0:T(8,128)(2,1)} %get-tuple-element.147), channel_id=1, source_target_pairs={{0,1},{1,0},{2,3},{3,2},{4,5},{5,4},{6,7},{7,6},{8,9},{9,8},{10,11... | collective-permute-start | bytes 663560 | tf_op jit(solution)/shard_map/ppermute | solution.py:924
  235.5 20.1 %collective-permute-start.36 = (bf16[4,24,1152]{2,1,0:T(8,128)(2,1)}, bf16[4,24,1152]{2,1,0:T(8,128)(2,1)S(1)}, u32[]{:S(2)}, u32[]{:S(2)}) collective-permute-start(bf16[4,24,1152]{2,1,0:T(8,128)(2,1)} %get-tuple-element.141.refs_5_), channel_id=1, source_target_pairs={{0,2},{1,3},{2,0},{3,1},{4,6},{5,7},{6,4},{7,5},{8,10},{9,11},{10,... | collective-permute-start | bytes 663560 | tf_op jit(solution)/shard_map/ppermute | solution.py:924
  236.8 28.6 %collective-permute-start.26 = (bf16[7,32,768]{2,1,0:T(8,128)(2,1)S(1)}, bf16[7,32,768]{2,1,0:T(8,128)(2,1)S(1)}, u32[]{:S(2)}, u32[]{:S(2)}) collective-permute-start(bf16[7,32,768]{2,1,0:T(8,128)(2,1)S(1)} %copy-done.3), channel_id=1, source_target_pairs={{1,0},{3,2},{5,4},{7,6},{9,8},{11,10},{13,12},{15,14},{17,16},{19,... | collective-permute-start | bytes 1032200 | tf_op jit(solution)/shard_map/ppermute | solution.py:1271
  (75 other events, 340.2 us)
Sparse Core Ops, SparseCore 0:
  10.9 76.6 all-gather.1
  141.3 123.0 reduce-scatter.1

commit v4 on v3

--- a/solution.py
+++ b/solution.py
@@ -468,7 +468,6 @@
 ):
     step = pl.program_id(0)
     first_half = step < pl.num_programs(0) // 2
-    low = img_ref[0] == 0
 
     @pl.when(step == 0)
     def _():
@@ -485,10 +484,11 @@
     grad = (dot_t(pull, reduce) * slope).astype(BF)
     result_ref[...] += dot_n(active, reduce)
     back_ref[...] += dot_t(grad, expand)
-    dexpand = dot_n(turned_ref[...], grad)
     half = dexpand_ref.shape[0]
-    dexpand_far_ref[...] = jnp.where(low, dexpand[half:], dexpand[:half]).astype(BF)
-    dexpand_ref[...] = jnp.where(low, dexpand[:half], dexpand[half:]).astype(BF)
+    here = pl.ds(pl.multiple_of(img_ref[0] * half, half), half)
+    there = pl.ds(pl.multiple_of((1 - img_ref[0]) * half, half), half)
+    dexpand_far_ref[...] = dot_n(turned_ref[there, :], grad).astype(BF)
+    dexpand_ref[...] = dot_n(turned_ref[here, :], grad).astype(BF)
     dbias_ref[...] = jnp.sum(grad.astype(F32), axis=0, keepdims=True)
     dreduce_ref[...] = dot_f(active, pull).astype(BF)
 
@@ -580,66 +580,68 @@
 
 
 def project_back_kernel(
-    img_ref, x_ref, mask_ref, rows_ref, middle_ref, pull_ref,
-    nq_ref, nk_ref, nv_ref, fq_ref, fk_ref, fv_ref, *refs,
+    img_ref, x_ref, mask_ref, rows_ref, middle_ref, pull_ref, near_ref, far_ref,
+    grad_ref, sums_ref, weight_ref, entry_ref,
 ):
-    grad_ref, sums_ref, near_ref, far_ref = refs[-4:]
-    step = pl.program_id(0)
-
-    @pl.when(step == 0)
-    def _():
-        near_ref[...] = jnp.zeros_like(near_ref)
-        far_ref[...] = jnp.zeros_like(far_ref)
-
-    pull = pull_ref[...]
-    near_ref[...] += dot_t(pull, jnp.concatenate([nq_ref[...], nk_ref[...], nv_ref[...]], 1))
-    far_ref[...] += dot_t(pull, jnp.concatenate([fq_ref[...], fk_ref[...], fv_ref[...]], 1))
-
-    @pl.when(step == pl.num_programs(0) - 1)
-    def _():
-        low = img_ref[0] == 0
-        near, far = near_ref[...], far_ref[...]
-        grad = jnp.concatenate([jnp.where(low, near, far), jnp.where(low, far, near)], 1) * mask_ref[...]
-        value = x_ref[...].astype(F32)
+    img = img_ref[0]
+    half = near_ref.shape[0]
+    pairs = HEADS // 2
+    here = pl.ds(pl.multiple_of(img * half, half), half)
+    there = pl.ds(pl.multiple_of((1 - img) * half, half), half)
+    for pair in range(pairs):
+        for part in range(3):
+            source = slice((part * pairs + pair) * 128, (part * pairs + pair + 1) * 128)
+            target = slice((pair * 3 + part) * 128, (pair * 3 + part + 1) * 128)
+            weight_ref[here, target] = near_ref[:, source]
+            weight_ref[there, target] = far_ref[:, source]
+    entry_ref[...] = dot_t(pull_ref[...], weight_ref[...])
+    gain = rows_ref[0:1]
+    width = x_ref.shape[1]
+
+    def step(number, carry):
+        spot = pl.ds(number * 48, 48)
+        first, second = carry
+        grad = entry_ref[spot, :] * mask_ref[spot, :]
+        value = x_ref[spot, :].astype(F32)
         centred = value - jnp.mean(value, axis=1, keepdims=True)
         variance = jnp.mean(centred * centred, axis=1, keepdims=True)
         rstd = lax.rsqrt(variance + 1e-06)
         xhat = centred * rstd
         product = grad * xhat
-        sums_ref[0:1] = jnp.sum(product, axis=0, keepdims=True)
-        sums_ref[1:2] = jnp.sum(grad, axis=0, keepdims=True)
-        pull = grad * rows_ref[0:1]
+        pull = grad * gain
         back = pull - jnp.mean(pull, axis=1, keepdims=True)
         back = back - xhat * jnp.mean(pull * xhat, axis=1, keepdims=True)
-        grad_ref[...] = (middle_ref[...] + rstd * back).astype(BF)
+        grad_ref[spot, :] = (middle_ref[spot, :] + rstd * back).astype(BF)
+        return first + jnp.sum(product.reshape(-1, 8, width), axis=0), second + jnp.sum(grad.reshape(-1, 8, width), axis=0)
+
+    none = jnp.zeros((8, width), F32)
+    carry = (none, none)
+    for number in range(TOKENS // 48):
+        carry = step(number, carry)
+    first, second = carry
+    sums_ref[0:1] = jnp.sum(first, axis=0, keepdims=True)
+    sums_ref[1:2] = jnp.sum(second, axis=0, keepdims=True)
 
 
 def project_back(img, x, mask, rows, grad_middle, grad_joint, near, far, *earlier):
     tokens, width = x.shape
-    pairs = HEADS // 2
-    half = width // 2
-
-    def weight(part):
-        return pl.BlockSpec((half, 128), lambda step: (0, part * pairs + step))
-
-    return pl.pallas_call(
-        project_back_kernel,
-        grid=(pairs,),
+    total = grad_joint.shape[1]
+    full = whole((tokens, width))
+    weight = whole((width // 2, total))
+    return pl.pallas_call(
+        ordered(project_back_kernel, 8, earlier),
+        grid=(1,),
         in_specs=[
-            pl.BlockSpec(memory_space=pltpu.SMEM), whole((tokens, width)), whole((tokens, 1)),
-            whole((8, width)), whole((tokens, width)),
-            pl.BlockSpec((tokens, 384), lambda step: (0, step)),
-            weight(0), weight(1), weight(2), weight(0), weight(1), weight(2),
-        ] + [pl.BlockSpec(memory_space=pl.ANY)] * len(earlier),
-        out_specs=[whole((tokens, width)), whole((2, width))],
+            pl.BlockSpec(memory_space=pltpu.SMEM), full, whole((tokens, 1)), whole((8, width)), full,
+            whole((tokens, total)), weight, weight,
+        ] + [ANY] * len(earlier),
+        out_specs=[full, whole((2, width))],
         out_shape=[jax.ShapeDtypeStruct((tokens, width), BF), jax.ShapeDtypeStruct((2, width), F32)],
-        scratch_shapes=[pltpu.VMEM((tokens, half), F32), pltpu.VMEM((tokens, half), F32)],
+        scratch_shapes=[pltpu.VMEM((width, total), BF), pltpu.VMEM((tokens, width), F32)],
         compiler_params=pltpu.CompilerParams(vmem_limit_bytes=VMEM_LIMIT),
         cost_estimate=cost(11),
         name="project_back",
-    )(
-        img.reshape(1), x, mask, rows, grad_middle, grad_joint, near, near, near, far, far, far, *earlier
-    )
+    )(img.reshape(1), x, mask, rows, grad_middle, grad_joint, near, far, *earlier)
 
 
 def mix_kernel(mixed_ref, weight_ref, rows_ref, x_ref, mask_ref, middle_ref, entry_ref):
@@ -733,11 +735,13 @@
     def _():
         turned_ref[...] = entry_ref[...].T
 
-    low = img_ref[0] == 0
     half = keep_ref.shape[0]
-    total = dot_n(turned_ref[...], grad_ref[...])
-    give_ref[...] = jnp.where(low, total[half:], total[:half]).astype(BF)
-    keep_ref[...] = jnp.where(low, total[:half], total[half:]).astype(BF)
+    img = img_ref[0]
+    grad = grad_ref[...]
+    here = pl.ds(pl.multiple_of(img * half, half), half)
+    there = pl.ds(pl.multiple_of((1 - img) * half, half), half)
+    give_ref[...] = dot_n(turned_ref[there, :], grad).astype(BF)
+    keep_ref[...] = dot_n(turned_ref[here, :], grad).astype(BF)
 
 
 def entry_grads(img, entry, grad, *earlier, chunk=768):
@@ -763,131 +767,118 @@
     )(img.reshape(1), entry, grad, *earlier)
 
 
-def sums_kernel(norm_ref, joint_ref, mix_ref, expand_ref, tables_ref, out_ref):
+def sums_kernel(
+    block, img_ref, norm_ref, joint_ref, mix_ref, expand_ref, tables_ref, give_ref, keep_ref, table_ref, turned_ref,
+):
     width = norm_ref.shape[1]
-    out_ref[0:2] = norm_ref[...]
-    out_ref[2:4] = joint_ref[...]
-    out_ref[4:8] = mix_ref[...]
-    for part in range(4):
-        out_ref[8 + part : 9 + part] = expand_ref[:, part * width : (part + 1) * width]
-    out_ref[12:] = jnp.zeros((out_ref.shape[0] - 12, width), F32)
+    number = width // block
+    joint = jnp.concatenate([joint_ref[0:1], joint_ref[1:2]], 1)
+
+    def picked(line, count):
+        return [
+            jnp.concatenate(
+                [
+                    line[:, (count * owner + place) * block : (count * owner + place + 1) * block]
+                    for owner in range(number)
+                ],
+                1,
+            )
+            for place in range(count)
+        ]
+
+    rows = [norm_ref[...], mix_ref[...]] + picked(joint, 2) + picked(expand_ref[...], 4)
+    rows.append(jnp.zeros((128 - 12, width), F32))
+    turned_ref[...] = jnp.concatenate(rows, 0).T
+    half = give_ref.shape[0]
+    img = img_ref[0]
+    give_ref[...] = turned_ref[pl.ds(pl.multiple_of((1 - img) * half, half), half), :].astype(BF)
+    keep_ref[...] = turned_ref[pl.ds(pl.multiple_of(img * half, half), half), :].astype(BF)
     total = tables_ref[0]
     for pair in range(1, tables_ref.shape[0]):
         total = total + tables_ref[pair]
     height = total[0:32, :64] + total[32:64, 64:]
     across = total[64:96, :64] + total[96:128, 64:]
     both = jnp.concatenate([height, across], 1)
-    for part in range(4):
-        out_ref[16:24, part * 128 : (part + 1) * 128] = both[part * 8 : (part + 1) * 8]
-
-
-def sums(norm, joint, mixed, expand, tables, *earlier):
+    table_ref[...] = jnp.zeros_like(table_ref)
+    for place in range(table_ref.shape[1] // 128):
+        part = both[place * block : min((place + 1) * block, 32)]
+        table_ref[: part.shape[0], place * 128 : (place + 1) * 128] = part.astype(BF)
+
+
+def sums(img, norm, joint, mixed, expand, tables, block, *earlier):
     vmem = pl.BlockSpec(memory_space=pltpu.VMEM)
-    return pl.pallas_call(
-        ordered(sums_kernel, 5, earlier),
-        in_specs=[vmem] * 5 + [ANY] * len(earlier),
-        out_specs=vmem,
-        out_shape=jax.ShapeDtypeStruct((24, norm.shape[1]), F32),
-        cost_estimate=cost(1.0),
+    width = norm.shape[1]
+    shapes = [(width // 2, 128), (width // 2, 128), (block, -(-32 // block) * 128)]
+    return pl.pallas_call(
+        ordered(partial(sums_kernel, block), 6, earlier),
+        in_specs=[pl.BlockSpec(memory_space=pltpu.SMEM)] + [vmem] * 5 + [ANY] * len(earlier),
+        out_specs=[vmem] * 3,
+        out_shape=[jax.ShapeDtypeStruct(shape, BF) for shape in shapes],
+        scratch_shapes=[pltpu.VMEM((width, 128), F32)],
+        compiler_params=pltpu.CompilerParams(vmem_limit_bytes=VMEM_LIMIT),
+        cost_estimate=cost(0.3),
         name="sums",
-    )(norm, joint, mixed, expand, tables, *earlier)
-
-
-def add_kernel(one_ref, two_ref, out_ref):
-    out_ref[...] = one_ref[...] + two_ref[...]
-
-
-def add(one, two, *earlier):
-    vmem = pl.BlockSpec(memory_space=pltpu.VMEM)
-    return pl.pallas_call(
-        ordered(add_kernel, 2, earlier),
-        in_specs=[vmem] * 2 + [ANY] * len(earlier),
-        out_specs=vmem,
-        out_shape=jax.ShapeDtypeStruct(one.shape, F32),
-        cost_estimate=cost(0.5),
-        name="add",
-    )(one, two, *earlier)
-
-
-def add_depth_kernel(depth, place_ref, *refs):
-    parts, out_ref = refs[:depth], refs[-1]
-    total = None
-    for level in range(depth):
-        found = parts[0][...]
-        for step in range(1, depth):
-            found = jnp.where((place_ref[2] ^ step) == level, parts[step][...], found)
-        total = found if total is None else total + found
-    out_ref[...] = total
-
-
-def add_depth(bits, parts, *earlier):
-    vmem = pl.BlockSpec(memory_space=pltpu.VMEM)
-    return pl.pallas_call(
-        ordered(partial(add_depth_kernel, len(parts)), 1 + len(parts), earlier),
-        in_specs=[pl.BlockSpec(memory_space=pltpu.SMEM)] + [vmem] * len(parts) + [ANY] * len(earlier),
-        out_specs=vmem,
-        out_shape=jax.ShapeDtypeStruct(parts[0].shape, F32),
-        cost_estimate=cost(0.5),
-        name="add_depth",
-    )(bits, *parts, *earlier)
-
-
-def share_kernel(block, slots, place_ref, one_ref, two_ref, *outs):
-    total = one_ref[...] + two_ref[...]
-    width = total.shape[1]
-    begin = place_ref[0] * block
-
-    def own(array, size, first):
-        return pltpu.roll(array, lax.rem(2 * array.shape[1] - first, array.shape[1]), 1)[:, :size]
-
-    for number, row in enumerate((0, 1, 4, 5, 6, 7)):
-        outs[number][...] = own(total[row : row + 1], block, begin)
-    joint = jnp.concatenate([total[2:3], total[3:4]], 1)
-    outs[6][...] = own(joint, 2 * block, 2 * begin)
-    hidden = jnp.concatenate([total[8 + part : 9 + part] for part in range(4)], 1)
-    outs[7][...] = own(hidden, 4 * block, 4 * begin)
-    for slot in range(slots):
-        place = slots - 1 - slot
-        line = total[16 + place % 8 : 17 + place % 8, place // 8 * 128 : place // 8 * 128 + 128]
-        outs[8][slot : slot + 1] = line[:, :64]
-        outs[9][slot : slot + 1] = line[:, 64:]
-
-
-def share(number, one, two, block, slots, *earlier):
-    vmem = pl.BlockSpec(memory_space=pltpu.VMEM)
-    shapes = [(1, block)] * 6 + [(1, 2 * block), (1, 4 * block)] + [(slots, HEAD_DIM)] * 2
-    return pl.pallas_call(
-        ordered(partial(share_kernel, block, slots), 3, earlier),
-        in_specs=[pl.BlockSpec(memory_space=pltpu.SMEM)] + [vmem] * 2 + [ANY] * len(earlier),
-        out_specs=[vmem] * len(shapes),
-        out_shape=[jax.ShapeDtypeStruct(shape, F32) for shape in shapes],
-        cost_estimate=cost(1.8),
-        name="share",
-    )(number.reshape(1), one, two, *earlier)
-
-
-def place_kernel(depth, *refs):
-    parts, triple_ref = refs[:depth], refs[depth]
+    )(img.reshape(1), norm, joint, mixed, expand, tables, *earlier)
+
+
+def place_kernel(depth, slots, place_ref, ready_ref, *refs):
+    parts = refs[:depth]
+    wide_ref, triple_ref, height_ref, width_ref = refs[depth : depth + 4]
+    vector_refs = refs[depth + 4 :]
+    wide_ref[...] = ready_ref[...].astype(F32)
+    block = triple_ref.shape[0]
     pairs = HEADS // 2
+    width = pairs * 128
+
+    def total(lanes):
+        value = parts[0][:, lanes]
+        for part in parts[1:]:
+            value = value + part[:, lanes].astype(F32)
+        return value
+
     for pair in range(pairs):
         for part in range(3):
             begin, spot = (pair * 3 + part) * 128, (part * pairs + pair) * 128
-            value = parts[0][:, begin : begin + 128]
-            for other in parts[1:]:
-                value = value + other[:, begin : begin + 128].astype(F32)
-            triple_ref[:, spot : spot + 128] = value
-
-
-def place(parts, *earlier):
+            triple_ref[:, spot : spot + 128] = total(slice(begin, begin + 128))
+    columns = total(slice(3 * width, 3 * width + 128))
+    columns = jnp.concatenate([columns, jnp.zeros((128 - block, 128), F32)], 0).T
+    begin = 0
+    for out_ref in vector_refs:
+        count = out_ref.shape[1] // block
+        out_ref[...] = jnp.concatenate(
+            [columns[begin + row : begin + row + 1, :block] for row in range(count)], 1
+        )
+        begin += count
+    lanes = slice(3 * width + 128, None)
+    tables = None
+    for level in range(depth):
+        found = parts[0][:, lanes]
+        for step in range(1, depth):
+            found = jnp.where((place_ref[2] ^ step) == level, parts[step][:, lanes].astype(F32), found)
+        tables = found if tables is None else tables + found
+    for slot in range(slots):
+        spot = slots - 1 - slot
+        first = spot // block * 128
+        line = tables[spot % block : spot % block + 1, first : first + 128]
+        height_ref[slot : slot + 1] = line[:, :64]
+        width_ref[slot : slot + 1] = line[:, 64:]
+
+
+def place(bits, ready, parts, slots, *earlier):
     vmem = pl.BlockSpec(memory_space=pltpu.VMEM)
-    return pl.pallas_call(
-        ordered(partial(place_kernel, len(parts)), len(parts), earlier),
-        in_specs=[vmem] * len(parts) + [ANY] * len(earlier),
-        out_specs=vmem,
-        out_shape=jax.ShapeDtypeStruct(parts[0].shape, F32),
+    block = parts[0].shape[0]
+    width = HEADS * HEAD_DIM
+    shapes = [ready.shape, (block, 3 * width)] + [(slots, HEAD_DIM)] * 2
+    shapes += [(1, block)] * 6 + [(1, 2 * block), (1, 4 * block)]
+    return pl.pallas_call(
+        ordered(partial(place_kernel, len(parts), slots), 2 + len(parts), earlier),
+        in_specs=[pl.BlockSpec(memory_space=pltpu.SMEM)] + [vmem] * (1 + len(parts)) + [ANY] * len(earlier),
+        out_specs=[vmem] * len(shapes),
+        out_shape=[jax.ShapeDtypeStruct(shape, F32) for shape in shapes],
         compiler_params=pltpu.CompilerParams(vmem_limit_bytes=VMEM_LIMIT),
+        cost_estimate=cost(1.9),
         name="place",
-    )(*parts, *earlier)
+    )(bits, ready, *parts, *earlier)
 
 
 def settle_kernel(cut, *refs):
@@ -1121,9 +1112,9 @@
         return self.call(kernel, "join_three", self.pairs(), shapes, earlier)[0].reshape(-1, self.columns)
 
 
-def fold_one_kernel(count, bits_ref, *refs):
+def fold_one_kernel(count, ride, bits_ref, *refs):
     ins = refs[: 2 * count]
-    a_give, a_keep, b_give, b_keep = refs[-4:]
+    a_give, a_keep, b_give, b_keep = refs[-4 - bool(ride) :][:4]
     x, y = bits_ref[0], bits_ref[1]
     cut = a_keep.shape[-1]
     begin = 0
@@ -1147,26 +1138,42 @@
                     value = near_ref[given + (slice(None), here)].astype(F32) + far_ref[given + (slice(None), here)].astype(F32)
                     give[level, side, :, there] = value.astype(BF)
         begin += columns
-
-
-def fold_two_kernel(bits_ref, a_near, a_far, b_near, b_far, *refs):
-    a_give, a_keep, b_give, b_keep = refs[-4:]
+    if ride:
+        near, far = refs[2 * count : 2 * count + 2]
+        table = (near[...].astype(F32) + far[...].astype(F32)).astype(BF)
+        refs[-1][...] = table
+        a_give[:, :, :, cut:] = jnp.zeros(a_give.shape[:3] + (ride,), BF)
+        a_give[0, 0, :, cut:] = table
+
+
+def fold_two_kernel(ride, bits_ref, a_near, a_far, b_near, b_far, *refs):
+    a_give, a_keep, b_give, b_keep = refs[-4 - bool(ride) :][:4]
     x, y = bits_ref[0], bits_ref[1]
+    cut = a_keep.shape[-1]
     for level in range(a_near.shape[0]):
-        a_keep[level] = a_near[level, y] + a_far[level, y].astype(F32)
-        a_give[level] = (a_near[level, 1 - y] + a_far[level, 1 - y].astype(F32)).astype(BF)
+        a_keep[level] = a_near[level, y] + a_far[level, y, :, :cut].astype(F32)
+        a_give[level, :, :cut] = (a_near[level, 1 - y] + a_far[level, 1 - y, :, :cut].astype(F32)).astype(BF)
         b_keep[level] = b_near[level, x] + b_far[level, x].astype(F32)
         b_give[level] = (b_near[level, 1 - x] + b_far[level, 1 - x].astype(F32)).astype(BF)
-
-
-def fold_three_kernel(depth, bits_ref, a_near, a_far, b_near, b_far, *refs):
+    if ride:
+        table = (refs[0][...].astype(F32) + a_far[0, 0, :, cut:].astype(F32)).astype(BF)
+        refs[-1][...] = table
+        a_give[:, :, cut:] = jnp.zeros(a_give.shape[:2] + (ride,), BF)
+        a_give[0, :, cut:] = table
+
+
+def fold_three_kernel(depth, ride, bits_ref, a_near, a_far, b_near, b_far, *refs):
     place = bits_ref[2]
     keep, gives = refs[-depth], refs[len(refs) - depth + 1 :]
     cut = a_near.shape[-1]
+    columns = cut + b_near.shape[-1]
     for step, out in enumerate((keep,) + tuple(gives)):
         spot = place ^ step
-        out[:, :cut] = (a_near[spot] + a_far[spot].astype(F32)).astype(out.dtype)
-        out[:, cut:] = (b_near[spot] + b_far[spot].astype(F32)).astype(out.dtype)
+        out[:, :cut] = (a_near[spot] + a_far[spot, :, :cut].astype(F32)).astype(out.dtype)
+        out[:, cut:columns] = (b_near[spot] + b_far[spot].astype(F32)).astype(out.dtype)
+        if ride:
+            table = (refs[0][...].astype(F32) + a_far[0, :, cut:].astype(F32)).astype(BF)
+            out[:, columns:] = table.astype(out.dtype)
 
 
 def fold_call(kernel, name, bits, values, outs, earlier, estimate):
@@ -1184,27 +1191,36 @@
 
 
 class Scatter:
-    def __init__(self, give, keep, costs):
+    def __init__(self, give, keep, costs, table=None):
         self.costs = costs
         self.depth = lax.axis_size("rows") // 4
         self.columns = sum(part.shape[-1] for part in keep)
         self.cut = self.columns // 256 * 128
         self.bits = jnp.stack(rows_place()).astype(jnp.int32)
-        self.shape = (self.depth, 2, 2, keep[0].shape[0] // lax.axis_size("rows"), -1)
-        self.give, self.keep = give, keep
+        self.rows = keep[0].shape[0] // lax.axis_size("rows")
+        self.give, self.keep = list(give), list(keep)
+        self.table = table
+        self.ride = table.shape[1] if table is not None else 0
 
     def swap_near(self):
         self.far = [swap_img(part) for part in self.give]
 
     def outs(self, *lead):
-        rows = self.shape[3]
-        first, second = lead + (rows, self.cut), lead + (rows, self.columns - self.cut)
-        return [(first, BF), (first, F32), (second, BF), (second, F32)]
+        first, second = lead + (self.rows, self.cut), lead + (self.rows, self.columns - self.cut)
+        shapes = [(lead + (self.rows, self.cut + self.ride), BF), (first, F32), (second, BF), (second, F32)]
+        if self.ride:
+            shapes.append(((self.rows, self.ride), BF))
+        return shapes
 
     def fold_one(self, *earlier):
-        values = [part.reshape(self.shape) for part in list(self.keep) + self.far]
-        kernel = partial(fold_one_kernel, len(self.keep))
-        self.out = fold_call(kernel, "fold_one", self.bits, values, self.outs(self.depth, 2), earlier, self.costs[0])
+        shape = (self.depth, 2, 2, self.rows, -1)
+        values = [part.reshape(shape) for part in self.keep + self.far]
+        if self.ride:
+            values += [self.table, swap_img(self.table)]
+        kernel = partial(fold_one_kernel, len(self.keep), self.ride)
+        self.out = fold_call(
+            kernel, "fold_one", self.bits, values, self.outs(self.depth, 2), earlier, self.costs[0]
+        )
         return self.out
 
     def swap_middle(self):
@@ -1212,9 +1228,10 @@
         return self.far
 
     def fold_two(self, *earlier):
-        values = [self.out[1], self.far[0], self.out[3], self.far[1]]
+        values = [self.out[1], self.far[0], self.out[3], self.far[1]] + list(self.out[4:])
+        kernel = partial(fold_two_kernel, self.ride)
         self.out = fold_call(
-            fold_two_kernel, "fold_two", self.bits, values, self.outs(self.depth), earlier, self.costs[1]
+            kernel, "fold_two", self.bits, values, self.outs(self.depth), earlier, self.costs[1]
         )
         return self.out
 
@@ -1223,20 +1240,11 @@
         return self.far
 
     def fold_three(self, *earlier):
-        depth, rows = self.depth, self.shape[3]
-        block = (rows, self.columns)
-        vmem = pl.BlockSpec(memory_space=pltpu.VMEM)
-        self.out = pl.pallas_call(
-            partial(fold_three_kernel, depth),
-            in_specs=[pl.BlockSpec(memory_space=pltpu.SMEM)] + [vmem] * 4
-            + [pl.BlockSpec(memory_space=pl.ANY)] * len(earlier),
-            out_specs=[vmem] * depth,
-            out_shape=[jax.ShapeDtypeStruct(block, F32)]
-            + [jax.ShapeDtypeStruct(block, BF) for _ in range(depth - 1)],
-            compiler_params=pltpu.CompilerParams(vmem_limit_bytes=VMEM_LIMIT),
-            cost_estimate=cost(self.costs[2]),
-            name="fold_three",
-        )(self.bits, self.out[1], self.far[0], self.out[3], self.far[1], *earlier)
+        block = (self.rows, self.columns + self.ride)
+        values = [self.out[1], self.far[0], self.out[3], self.far[1]] + list(self.out[4:])
+        outs = [(block, F32)] + [(block, BF)] * (self.depth - 1)
+        kernel = partial(fold_three_kernel, self.depth, self.ride)
+        self.out = fold_call(kernel, "fold_three", self.bits, values, outs, earlier, self.costs[2])
         return self.out
 
     def swap_last(self):
@@ -1245,20 +1253,6 @@
     def last(self):
         parts = self.swap_last()
         return sum((part.astype(F32) for part in parts[1:]), parts[0])
-
-
-def sum_all(value):
-    value = value + swap_img(value)
-    value = value + swap_rows(value, 0)
-    value = value + swap_rows(value, 1)
-    return jnp.sum(gather_depth(value), axis=0)
-
-
-def layer_norm(value, gain, bias):
-    center = jnp.mean(value, axis=-1, keepdims=True)
-    centred = value - center
-    variance = jnp.mean(centred * centred, axis=-1, keepdims=True)
-    return centred * lax.rsqrt(variance + 1e-06) * gain + bias
 
 
 def to_odd(block):
@@ -1345,7 +1339,7 @@
     result, grad_entry_two, reduce_grad, expand_far, expand_near, hidden_sums = then(
         mlp(img, entry_two, incoming, later_all, hidden_bias, *reduce_pair, *last)
     )
-    reduce_shard = lax.psum_scatter(reduce_grad, ("img", "rows"), scatter_dimension=0, tiled=True).astype(F32)
+    reduce_part = lax.psum_scatter(reduce_grad, ("img", "rows"), scatter_dimension=0, tiled=True)
     grad_middle, grad_mixed, output_far, output_near, out_win, mix_sums = then(
         mix_back(img, grad_entry_two, result, middle, incoming, mask, rows, later_all, mixed, *last)
     )
@@ -1358,53 +1352,49 @@
         attend_back(joint, grad_mixed, lse, features, fill, table, 0, HEADS // 2, *last)
     )
     joint_far, joint_near = then(entry_grads(img, entry, grad_joint, *last))
-    last_sum = Scatter([joint_far], [joint_near], (2.3, 2.3, 1.5))
-    last_sum.swap_near()
     then(first_sum.fold_two(*last))
     first_sum.swap_far()
     grad_win, norm_sums = then(
         project_back(img, x, mask, rows, grad_middle, grad_joint, *triple_pair, *last)
     )
+    vectors_far, vectors_near, table_sums = then(
+        sums(img, norm_sums, joint_sums, mix_sums, hidden_sums, tables, block, *last)
+    )
+    last_sum = Scatter([joint_far, vectors_far], [joint_near, vectors_near], (0.3, 2.3, 1.5), table_sums)
+    last_sum.swap_near()
     then(last_sum.fold_one(*last, out_rows))
     last_sum.swap_middle()
     then(first_sum.fold_three(*last))
     first_parts = first_sum.swap_last()
-    small = then(sums(norm_sums, joint_sums, mix_sums, hidden_sums, tables, *last))
-    depths = [small] + [swap_depth(small, step) for step in range(1, lax.axis_size("rows") // 4)]
-    grad_rows = to_even(then(send_rows(grad_win, moved, *last)))
-    block_output = then(unpack(parity, out_win, out_rows, tokens.shape, *last, *first_parts[1:2]))
+    block_output = then(unpack(parity, out_win, out_rows, tokens.shape, *last))
+    grad_rows = to_even(then(send_rows(grad_win, moved, *last, *first_parts[1:2])))
     then(last_sum.fold_two(*last))
     last_sum.swap_far()
-    small = then(add_depth(last_sum.bits, depths, *last))
     expand_shard, output_shard = then(settle(first_parts, expand_far.shape[1], *last))
-    small = then(add(small, swap_rows(small, 0), *last))
     then(last_sum.fold_three(*last))
     last_parts = last_sum.swap_last()
-    small = then(add(small, swap_rows(small, 1), *last))
     input_grad = then(unpack(parity, grad_win, grad_rows, tokens.shape, *last))
-    triple_shard = then(place(last_parts, *last))
-    number = (img * lax.axis_size("rows") + lax.axis_index("rows")).astype(jnp.int32)
-    shares = share(number, small, swap_img(small), block, height_table.shape[0], *last)
-    pre_gain_grad, pre_bias_grad, output_bias_grad, post_gain_grad, post_bias_grad, reduce_bias_grad = [
-        array.reshape(-1) for array in shares[:6]
-    ]
+    (
+        reduce_shard, triple_shard, height_grad, width_grad, pre_gain_grad, pre_bias_grad, output_bias_grad,
+        post_gain_grad, post_bias_grad, reduce_bias_grad, triple_bias_grad, expand_bias_grad,
+    ) = place(last_sum.bits, reduce_part, last_parts, height_table.shape[0], *last)
     return (
         block_output,
         input_grad,
-        pre_gain_grad,
-        pre_bias_grad,
+        pre_gain_grad.reshape(-1),
+        pre_bias_grad.reshape(-1),
         triple_shard,
-        shares[6].reshape(-1),
-        shares[8],
-        shares[9],
+        triple_bias_grad.reshape(-1),
+        height_grad,
+        width_grad,
         output_shard,
-        output_bias_grad,
-        post_gain_grad,
-        post_bias_grad,
+        output_bias_grad.reshape(-1),
+        post_gain_grad.reshape(-1),
+        post_bias_grad.reshape(-1),
         expand_shard,
-        shares[7].reshape(-1),
+        expand_bias_grad.reshape(-1),
         reduce_shard,
-        reduce_bias_grad,
+        reduce_bias_grad.reshape(-1),
     )
 
 

time: 287 us -> 274 us (0.955)
  Pallas kernels: 161 us -> 152 us
  starting transfers between devices: 51.2 us -> 46.4 us
  waiting for transfers between devices: 30.7 us -> 34.5 us
    pallas_call x9 -> x3, Pallas kernels: 26.1 us -> 12.9 us  [the longest x1 8.59 us: project_back(): pl.pallas_call(ordered(project_back_kernel, 8, earlier), grid=(1,), in_sp...]
    pallas_call x4 -> x6, Pallas kernels: 15.5 us -> 20.7 us  [fold_call(): pl.pallas_call(kernel, in_specs=[pl.BlockSpec(memory_space=pltpu.SMEM)] +...]
    ppermute x15 -> x12, starting transfers between devices: 23.2 us -> 18.7 us  [swap_depth(): lax.ppermute(block, 'rows', [(place, place ^ 4 * step) for place in range...]
    unnamed x112 -> x100, local copies, waits for them, and re-layouts: 19.2 us -> 17.6 us
    ppermute x18 -> x16, waiting for transfers between devices: 11.8 us -> 13.1 us  [swap_rows(): lax.ppermute(block, 'rows', [(place, place ^ 1 << bit) for place in range...]
    ppermute x18 -> x16, starting transfers between devices: 21.1 us -> 19.9 us  [swap_rows(): lax.ppermute(block, 'rows', [(place, place ^ 1 << bit) for place in range...]
    ppermute x15 -> x12, waiting for transfers between devices: 14 us -> 13.4 us  [swap_depth(): lax.ppermute(block, 'rows', [(place, place ^ 4 * step) for place in range...]
  transfers between devices with their start and end apart: 44 -> 40, of which waited for: 12 -> 13; matrix products, arithmetic and copies ran while one was open for 2% -> 2% of each run, Pallas kernels for 46% -> 45%
where the time goes in v4:
time: 274 us; the launch traced here: 273 us
  Pallas kernels  152 us (55%)
  starting transfers between devices  46.4 us (17%)
  waiting for transfers between devices  34.5 us (13%)
  local copies, waits for them, and re-layouts  21.3 us (8%)
  between operations  14.5 us (5%)
  other arithmetic  4.29 us (2%)
    pallas_call x1, Pallas kernels, mlp(): pl.pallas_call(ordered(mlp_kernel, 7, earlier), grid_spec=pltpu.PrefetchS...  28.3 us
    pallas_call x6, Pallas kernels, fold_call(): pl.pallas_call(kernel, in_specs=[pl.BlockSpec(memory_space=pltpu.SMEM)] +...  20.7 us
    ppermute x16, starting transfers between devices, swap_rows(): lax.ppermute(block, 'rows', [(place, place ^ 1 << bit) for place in range...  19.9 us
    ppermute x12, starting transfers between devices, swap_depth(): lax.ppermute(block, 'rows', [(place, place ^ 4 * step) for place in range...  18.7 us
    unnamed x100, local copies, waits for them, and re-layouts  17.6 us
    pallas_call x6, Pallas kernels, call(): pl.pallas_call(kernel, in_specs=[pl.BlockSpec(memory_space=pltpu.SMEM)] +...  14.8 us
    pallas_call x1, Pallas kernels, attend_back(): pl.pallas_call(kernel, grid=(count,), in_specs=[column(begin), column(pai...  14.6 us
    ppermute x12, waiting for transfers between devices, swap_depth(): lax.ppermute(block, 'rows', [(place, place ^ 4 * step) for place in range...  13.4 us
  transfers between devices with their start and end apart: 40, of which 13 were waited for; matrix products, arithmetic and copies ran while one was open for 2% of the time, Pallas kernels for 45%

profile of v4, /device:TPU:0, one launch (start us, length us, event | category | flops | bytes accessed | tf_op | source)
XLA Modules:
  0.0 273.2 jit_solution(4908693946211794749)
XLA Ops:
  10.6 3.0 %collective-permute-start.2 = (bf16[24,2432]{1,0:T(8,128)(2,1)}, bf16[24,2432]{1,0:T(8,128)(2,1)S(1)}, u32[]{:S(2)}, u32[]{:S(2)}) collective-permute-start(bf16[24,2432]{1,0:T(8,128)(2,1)} %carry.1.refs_1_.refs_0_), channel_id=1, source_target_pairs={{0,4},{1,5},{2,6},{3,7},{4,0},{5,1},{6,2},{7,3},{8,12},{9,13},{10,... | collective-permute-start | bytes 350216 | tf_op jit(solution)/shard_map/ppermute | solution.py:924
  20.4 3.8 %collective-permute-start = (bf16[14,32,768]{2,1,0:T(8,128)(2,1)S(1)}, bf16[14,32,768]{2,1,0:T(8,128)(2,1)S(1)}, u32[]{:S(2)}, u32[]{:S(2)}) collective-permute-start(bf16[14,32,768]{2,1,0:T(8,128)(2,1)S(1)} %pad_maximum_fusion), channel_id=1, source_target_pairs={{0,1},{2,3},{4,5},{6,7},{8,9},{10,11},{12,13},{14,15},{16,17},{18,... | collective-permute-start | bytes 2064392 | tf_op jit(solution)/shard_map/ppermute | solution.py:1260
  40.9 2.9 %pack.2.refs_4_.refs_1_.refs_3_ = bf16[624,768]{1,0:T(8,128)(2,1)} custom-call(s32[1]{0:T(128)} %bitcast.refs_0_, bf16[21,42,768]{2,1,0:T(8,128)(2,1)} %refs_1_.2, bf16[14,32,768]{2,1,0:T(8,128)(2,1)} %copy-done.22, f32[624,1]{1,0:T(8,128)} %reshape.154.refs_3_.refs_2_.refs_4_.refs_5_, bf16[4,24,1152]{2,1,0:T(8,128)(2,1)} %get-tuple-element.97.refs_4_.refs_0_), custom_call_target="tpu_custom_call" | custom-call | flops 3000000000 | bytes 1 | tf_op jit(solution)/shard_map/pack/pallas_call | solution.py:378
  43.8 3.7 %collective-permute-done.4.refs_1_ = bf16[4,24,1152]{2,1,0:T(8,128)(2,1)S(1)} collective-permute-done((bf16[4,24,1152]{2,1,0:T(8,128)(2,1)}, bf16[4,24,1152]{2,1,0:T(8,128)(2,1)S(1)}, u32[]{:S(2)}, u32[]{:S(2)}) %collective-permute-start.4) | collective-permute-done | bytes 221216 | tf_op jit(solution)/shard_map/ppermute | solution.py:915
  56.7 3.0 %pack.3.refs_0_.refs_2_.refs_4_ = bf16[624,768]{1,0:T(8,128)(2,1)} custom-call(s32[1]{0:T(128)} %bitcast.refs_0_, bf16[21,42,768]{2,1,0:T(8,128)(2,1)} %refs_1_.3, bf16[14,32,768]{2,1,0:T(8,128)(2,1)} %copy-done.22, f32[624,1]{1,0:T(8,128)} %reshape.154.refs_3_.refs_2_.refs_4_.refs_5_, bf16[4,2,24,1152]{3,2,1,0:T(8,128)(2,1)} %get-tuple-element.99.refs_4_.first), custom_call_target="tpu_custom_call" | custom-call | flops 3000000000 | bytes 1 | tf_op jit(solution)/shard_map/pack/pallas_call | solution.py:378
  63.7 2.8 %join_three.2 = bf16[4,2,2,24,2432]{4,3,2,1,0:T(8,128)(2,1)} custom-call(s32[3]{0:T(128)} %pad_add_fusion.bits_ref.refs_0_, bf16[4,2,24,1152]{3,2,1,0:T(8,128)(2,1)} %get-tuple-element.99.refs_4_.first, bf16[4,2,24,1152]{3,2,1,0:T(8,128)(2,1)} %copy-done.29, bf16[4,2,24,1280]{3,2,1,0:T(8,128)(2,1)} %get-tuple-element.100.second, ...), custom_call_target="tpu_custom_call" | custom-call | flops 2300000000 | bytes 1 | tf_op jit(solution)/shard_map/join_three/pallas_call | solution.py:1068
  75.3 7.2 %project.1 = (bf16[624,768]{1,0:T(8,128)(2,1)}, bf16[624,2304]{1,0:T(8,128)(2,1)}) custom-call(s32[1]{0:T(128)} %bitcast.1.refs_0_, bf16[624,768]{1,0:T(8,128)(2,1)} %pack.2.refs_4_.refs_1_.refs_3_, f32[624,1]{1,0:T(8,128)} %reshape.154.refs_3_.refs_2_.refs_4_.refs_5_, f32[8,768]{1,0:T(8,128)} %get-tuple-element.102.refs_3_.refs_2_.refs_6_, ...), custom_call_target="tpu_custom_call" | custom-call | flops 7000000000 | bytes 1 | tf_op jit(solution)/shard_map/project/pallas_call | solution.py:565
  87.2 11.2 %attend.1 = (bf16[624,768]{1,0:T(8,128)(2,1)}, f32[6,8,1536]{2,1,0:T(8,128)}, bf16[624,768]{1,0:T(8,128)(2,1)}) custom-call(bf16[624,2304]{1,0:T(8,128)(2,1)} %get-tuple-element.105.refs_0_.refs_1_.refs_2_, bf16[624,2304]{1,0:T(8,128)(2,1)} %get-tuple-element.105.refs_0_.refs_1_.refs_2_, bf16[624,2304]{1,0:T(8,128)(2,1)} %get-tuple-element.105.refs_0_.refs_1_.refs_2_, ...), custom_call_target="tpu_custom_call" | custom-call | flops 11000000512 | bytes 1 | tf_op jit(solution)/shard_map/attend/pallas_call | solution.py:280
  102.9 3.3 %join_three.3 = bf16[4,2,2,96,768]{4,3,2,1,0:T(8,128)(2,1)} custom-call(s32[3]{0:T(128)} %pad_add_fusion.bits_ref.refs_0_, bf16[4,2,96,384]{3,2,1,0:T(8,128)(2,1)} %get-tuple-element.108.refs_7_.first, bf16[4,2,96,384]{3,2,1,0:T(8,128)(2,1)} %copy-done.25, bf16[4,2,96,384]{3,2,1,0:T(8,128)(2,1)} %get-tuple-element.110.second, ...), custom_call_target="tpu_custom_call" | custom-call | flops 2300000000 | bytes 1 | tf_op jit(solution)/shard_map/join_three/pallas_call | solution.py:1068
  106.2 4.8 %mix.1 = (f32[624,768]{1,0:T(8,128)}, bf16[624,768]{1,0:T(8,128)(2,1)}) custom-call(bf16[624,768]{1,0:T(8,128)(2,1)} %get-tuple-element.109.refs_0_.refs_8_, bf16[768,3840]{1,0:T(8,128)(2,1)} %all-gather.2.cloned.1.call-done.refs_1_.refs_3_.refs_7_, f32[8,768]{1,0:T(8,128)} %get-tuple-element.102.refs_3_.refs_2_.refs_6_, ...), custom_call_target="tpu_custom_call" | custom-call | flops 4600000000 | bytes 1 | tf_op jit(solution)/shard_map/mix/pallas_call | solution.py:664
  112.3 28.3 %mlp.1 = (f32[624,768]{1,0:T(8,128)}, f32[624,768]{1,0:T(8,128)}, bf16[3072,768]{1,0:T(8,128)(2,1)}, bf16[384,3072]{1,0:T(8,128)(2,1)}, bf16[384,3072]{1,0:T(8,128)(2,1)}, /*index=5*/f32[1,3072]{1,0:T(1,128)}) custom-call(s32[1]{0:T(128)} %bitcast.1.refs_0_, bf16[624,768]{1,0:T(8,128)(2,1)} %get-tuple-element.112.refs_1_, ...), custom_call_target="tpu_custom_call" | custom-call | flops 28999999488 | bytes 1 | tf_op jit(solution)/shard_map/mlp/pallas_call | solution.py:512
  141.2 8.6 %mix_back.1 = (f32[624,768]{1,0:T(8,128)}, bf16[624,768]{1,0:T(8,128)(2,1)}, bf16[384,768]{1,0:T(8,128)(2,1)}, bf16[384,768]{1,0:T(8,128)(2,1)}, bf16[624,768]{1,0:T(8,128)(2,1)}, /*index=5*/f32[4,768]{1,0:T(4,128)}) custom-call(s32[1]{0:T(128)} %bitcast.1.refs_0_, f32[624,768]{1,0:T(8,128)} %get-tuple-element.115.refs_1_, ...), custom_call_target="tpu_custom_call" | custom-call | flops 7000000000 | bytes 1 | tf_op jit(solution)/shard_map/mix_back/pallas_call | solution.py:714
  153.5 5.0 %fold_one.2 = (bf16[4,2,24,1920]{3,2,1,0:T(8,128)(2,1)}, f32[4,2,24,1920]{3,2,1,0:T(8,128)}, bf16[4,2,24,1920]{3,2,1,0:T(8,128)(2,1)}, f32[4,2,24,1920]{3,2,1,0:T(8,128)}) custom-call(s32[3]{0:T(128)} %pad_add_fusion.bits_ref.refs_0_, bf16[4,2,2,24,3072]{4,3,2,1,0:T(8,128)(2,1)} %bitcast.58, bf16[4,2,2,24,768]{4,3,2,1,0:T(8,128)(2,1)} %bitcast.59, ...), custom_call_target="tpu_custom_call" | custom-call | flops 2300000000 | bytes 1 | tf_op jit(solution)/shard_map/fold_one/pallas_call | solution.py:1181
  162.3 14.6 %attend_back.1 = (bf16[624,2304]{1,0:T(8,128)(2,1)}, f32[6,128,128]{2,1,0:T(8,128)}, f32[2,768]{1,0:T(2,128)}) custom-call(bf16[624,2304]{1,0:T(8,128)(2,1)} %get-tuple-element.105.refs_0_.refs_1_.refs_2_, bf16[624,2304]{1,0:T(8,128)(2,1)} %get-tuple-element.105.refs_0_.refs_1_.refs_2_, bf16[624,2304]{1,0:T(8,128)(2,1)} %get-tuple-element.105.refs_0_.refs_1_.refs_2_, ...), custom_call_target="tpu_custom_call" | custom-call | flops 8999999488 | bytes 1 | tf_op jit(solution)/shard_map/attend_back/pallas_call | solution.py:305
  176.9 6.4 %entry_grads.1 = (bf16[384,2304]{1,0:T(8,128)(2,1)}, bf16[384,2304]{1,0:T(8,128)(2,1)}) custom-call(s32[1]{0:T(128)} %bitcast.1.refs_0_, bf16[624,768]{1,0:T(8,128)(2,1)} %get-tuple-element.107.refs_4_.refs_1_, bf16[624,2304]{1,0:T(8,128)(2,1)} %get-tuple-element.130.refs_2_.refs_5_, f32[2,768]{1,0:T(2,128)} %get-tuple-element.131.refs_3_.refs_2_), custom_call_target="tpu_custom_call" | custom-call | flops 5000000000 | bytes 1 | tf_op jit(solution)/shard_map/entry_grads/pallas_call | solution.py:754
  186.0 3.8 %fold_two.2 = (bf16[4,24,1920]{2,1,0:T(8,128)(2,1)}, f32[4,24,1920]{2,1,0:T(8,128)}, bf16[4,24,1920]{2,1,0:T(8,128)(2,1)}, f32[4,24,1920]{2,1,0:T(8,128)}) custom-call(s32[3]{0:T(128)} %pad_add_fusion.bits_ref.refs_0_, f32[4,2,24,1920]{3,2,1,0:T(8,128)} %get-tuple-element.125.a_near, bf16[4,2,24,1920]{3,2,1,0:T(8,128)(2,1)} %copy-done.21, ...), custom_call_target="tpu_custom_call" | custom-call | flops 2300000000 | bytes 1 | tf_op jit(solution)/shard_map/fold_two/pallas_call | solution.py:1181
  193.9 8.6 %project_back.1 = (bf16[624,768]{1,0:T(8,128)(2,1)}, f32[2,768]{1,0:T(2,128)}) custom-call(s32[1]{0:T(128)} %bitcast.1.refs_0_, bf16[624,768]{1,0:T(8,128)(2,1)} %pack.2.refs_4_.refs_1_.refs_3_, f32[624,1]{1,0:T(8,128)} %reshape.154.refs_3_.refs_2_.refs_4_.refs_5_, f32[8,768]{1,0:T(8,128)} %get-tuple-element.102.refs_3_.refs_2_.refs_6_, ...), custom_call_target="tpu_custom_call" | custom-call | flops 11000000512 | bytes 1 | tf_op jit(solution)/shard_map/project_back/pallas_call | solution.py:631
  207.4 3.8 %fold_one.3 = (bf16[4,2,24,1408]{3,2,1,0:T(8,128)(2,1)}, f32[4,2,24,1152]{3,2,1,0:T(8,128)}, bf16[4,2,24,1280]{3,2,1,0:T(8,128)(2,1)}, f32[4,2,24,1280]{3,2,1,0:T(8,128)}, bf16[24,256]{1,0:T(8,128)(2,1)}) custom-call(s32[3]{0:T(128)} %pad_add_fusion.bits_ref.refs_0_, bf16[4,2,2,24,2304]{4,3,2,1,0:T(8,128)(2,1)} %bitcast.34, ...), custom_call_target="tpu_custom_call" | custom-call | flops 300000000 | bytes 1 | tf_op jit(solution)/shard_map/fold_one/pallas_call | solution.py:1181
  219.8 2.9 %unpack.2.refs_1_ = bf16[21,42,768]{2,1,0:T(8,128)(2,1)} custom-call(s32[1]{0:T(128)} %bitcast.refs_0_, bf16[624,768]{1,0:T(8,128)(2,1)} %get-tuple-element.118.refs_0_.refs_1_, bf16[7,32,768]{2,1,0:T(8,128)(2,1)} %copy-done.3, f32[24,3840]{1,0:T(8,128)} %get-tuple-element.145.refs_3_.refs_0_), custom_call_target="tpu_custom_call" | custom-call | flops 500000000 | bytes 1 | tf_op jit(solution)/shard_map/unpack/pallas_call | solution.py:407
  222.7 3.0 %collective-permute-done.27.refs_2_.refs_1_ = bf16[24,3840]{1,0:T(8,128)(2,1)S(1)} collective-permute-done((bf16[24,3840]{1,0:T(8,128)(2,1)}, bf16[24,3840]{1,0:T(8,128)(2,1)S(1)}, u32[]{:S(2)}, u32[]{:S(2)}) %collective-permute-start.27) | collective-permute-done | bytes 184352 | tf_op jit(solution)/shard_map/ppermute | solution.py:924
  229.5 3.1 %fold_two.3 = (bf16[4,24,1408]{2,1,0:T(8,128)(2,1)}, f32[4,24,1152]{2,1,0:T(8,128)}, bf16[4,24,1280]{2,1,0:T(8,128)(2,1)}, f32[4,24,1280]{2,1,0:T(8,128)}, bf16[24,256]{1,0:T(8,128)(2,1)}) custom-call(s32[3]{0:T(128)} %pad_add_fusion.bits_ref.refs_0_, f32[4,2,24,1152]{3,2,1,0:T(8,128)} %get-tuple-element.148.a_near, bf16[4,2,24,1408]{3,2,1,0:T(8,128)(2,1)} %copy-done.26, ...), custom_call_target="tpu_custom_call" | custom-call | flops 2300000000 | bytes 1 | tf_op jit(solution)/shard_map/fold_two/pallas_call | solution.py:1181
  239.3 4.0 %collective-permute-done.32.b_far = bf16[4,24,1280]{2,1,0:T(8,128)(2,1)S(1)} collective-permute-done((bf16[4,24,1280]{2,1,0:T(8,128)(2,1)}, bf16[4,24,1280]{2,1,0:T(8,128)(2,1)S(1)}, u32[]{:S(2)}, u32[]{:S(2)}) %collective-permute-start.32) | collective-permute-done | bytes 245792 | tf_op jit(solution)/shard_map/ppermute | solution.py:915
  252.0 2.9 %unpack.3.refs_6_ = bf16[21,42,768]{2,1,0:T(8,128)(2,1)} custom-call(s32[1]{0:T(128)} %bitcast.refs_0_, bf16[624,768]{1,0:T(8,128)(2,1)} %get-tuple-element.146.refs_0_.refs_1_, bf16[7,32,768]{2,1,0:T(8,128)(2,1)} %copy-done.5, f32[24,2688]{1,0:T(8,128)} %get-tuple-element.160.refs_3_.refs_2_), custom_call_target="tpu_custom_call" | custom-call | flops 500000000 | bytes 1 | tf_op jit(solution)/shard_map/unpack/pallas_call | solution.py:407
  254.9 7.1 %collective-permute-done.36.refs_4_ = bf16[24,2688]{1,0:T(8,128)(2,1)S(1)} collective-permute-done((bf16[24,2688]{1,0:T(8,128)(2,1)}, bf16[24,2688]{1,0:T(8,128)(2,1)S(1)}, u32[]{:S(2)}, u32[]{:S(2)}) %collective-permute-start.36) | collective-permute-done | bytes 129056 | tf_op jit(solution)/shard_map/ppermute | solution.py:924
  (205 shorter events, 111.0 us)
Async XLA Ops:
  7.2 99.0 %all-gather.2.cloned.1.call-start = ((), (), s32[]{:S(2)}) async-start(), calls=%async_computation.1 | async-start | bytes 6082560 | tf_op jit(solution)/shard_map/all_gather | solution.py:1313
  8.9 255.3 %reduce-scatter.2.cloned.1.call-start = ((), (), s32[]{:S(2)}) async-start(), calls=%async_computation.2 | async-start | bytes 4866048 | tf_op jit(solution)/shard_map/reduce_scatter | solution.py:1342
  10.6 18.6 %collective-permute-start.2 = (bf16[24,2432]{1,0:T(8,128)(2,1)}, bf16[24,2432]{1,0:T(8,128)(2,1)S(1)}, u32[]{:S(2)}, u32[]{:S(2)}) collective-permute-start(bf16[24,2432]{1,0:T(8,128)(2,1)} %carry.1.refs_1_.refs_0_), channel_id=1, source_target_pairs={{0,4},{1,5},{2,6},{3,7},{4,0},{5,1},{6,2},{7,3},{8,12},{9,13},{10,... | collective-permute-start | bytes 350216 | tf_op jit(solution)/shard_map/ppermute | solution.py:924
  17.8 26.0 %collective-permute-start.7 = (bf16[96,768]{1,0:T(8,128)(2,1)}, bf16[96,768]{1,0:T(8,128)(2,1)S(1)}, u32[]{:S(2)}, u32[]{:S(2)}) collective-permute-start(bf16[96,768]{1,0:T(8,128)(2,1)} %stack.10.refs_4_.refs_0_), channel_id=1, source_target_pairs={{0,4},{1,5},{2,6},{3,7},{4,0},{5,1},{6,2},{7,3},{8,12},{9,13},{10,... | collective-permute-start | bytes 442376 | tf_op jit(solution)/shard_map/ppermute | solution.py:924
  18.4 25.5 %collective-permute-start.6 = (bf16[96,768]{1,0:T(8,128)(2,1)}, bf16[96,768]{1,0:T(8,128)(2,1)S(1)}, u32[]{:S(2)}, u32[]{:S(2)}) collective-permute-start(bf16[96,768]{1,0:T(8,128)(2,1)} %stack.10.refs_4_.refs_0_), channel_id=1, source_target_pairs={{0,8},{1,9},{2,10},{3,11},{4,12},{5,13},{6,14},{7,15},{8,0},{9,1},... | collective-permute-start | bytes 442376 | tf_op jit(solution)/shard_map/ppermute | solution.py:924
  20.4 19.6 %collective-permute-start = (bf16[14,32,768]{2,1,0:T(8,128)(2,1)S(1)}, bf16[14,32,768]{2,1,0:T(8,128)(2,1)S(1)}, u32[]{:S(2)}, u32[]{:S(2)}) collective-permute-start(bf16[14,32,768]{2,1,0:T(8,128)(2,1)S(1)} %pad_maximum_fusion), channel_id=1, source_target_pairs={{0,1},{2,3},{4,5},{6,7},{8,9},{10,11},{12,13},{14,15},{16,17},{18,... | collective-permute-start | bytes 2064392 | tf_op jit(solution)/shard_map/ppermute | solution.py:1260
  34.3 13.2 %collective-permute-start.4 = (bf16[4,24,1152]{2,1,0:T(8,128)(2,1)}, bf16[4,24,1152]{2,1,0:T(8,128)(2,1)S(1)}, u32[]{:S(2)}, u32[]{:S(2)}) collective-permute-start(bf16[4,24,1152]{2,1,0:T(8,128)(2,1)} %get-tuple-element.97.refs_4_.refs_0_), channel_id=1, source_target_pairs={{0,1},{1,0},{2,3},{3,2},{4,5},{5,4},{6,7},{7,6},{8,9},{9,8},{10,11... | collective-permute-start | bytes 663560 | tf_op jit(solution)/shard_map/ppermute | solution.py:915
  35.7 11.8 %collective-permute-start.5 = (bf16[4,24,1280]{2,1,0:T(8,128)(2,1)}, bf16[4,24,1280]{2,1,0:T(8,128)(2,1)S(1)}, u32[]{:S(2)}, u32[]{:S(2)}) collective-permute-start(bf16[4,24,1280]{2,1,0:T(8,128)(2,1)} %get-tuple-element.98.refs_2_), channel_id=1, source_target_pairs={{0,2},{1,3},{2,0},{3,1},{4,6},{5,7},{6,4},{7,5},{8,10},{9,11},{10,... | collective-permute-start | bytes 737288 | tf_op jit(solution)/shard_map/ppermute | solution.py:915
  69.7 12.8 %collective-permute-start.13 = (bf16[4,96,384]{2,1,0:T(8,128)(2,1)}, bf16[4,96,384]{2,1,0:T(8,128)(2,1)S(1)}, u32[]{:S(2)}, u32[]{:S(2)}) collective-permute-start(bf16[4,96,384]{2,1,0:T(8,128)(2,1)} %get-tuple-element.106.refs_2_), channel_id=1, source_target_pairs={{0,2},{1,3},{2,0},{3,1},{4,6},{5,7},{6,4},{7,5},{8,10},{9,11},{10,... | collective-permute-start | bytes 884744 | tf_op jit(solution)/shard_map/ppermute | solution.py:915
  85.8 15.4 %collective-permute-start.15 = (bf16[4,2,96,384]{3,2,1,0:T(8,128)(2,1)}, bf16[4,2,96,384]{3,2,1,0:T(8,128)(2,1)S(1)}, u32[]{:S(2)}, u32[]{:S(2)}) collective-permute-start(bf16[4,2,96,384]{3,2,1,0:T(8,128)(2,1)} %get-tuple-element.110.second), channel_id=1, source_target_pairs={{0,1},{1,0},{2,3},{3,2},{4,5},{5,4},{6,7},{7,6},{8,9},{9,8},{10,11... | collective-permute-start | bytes 1769480 | tf_op jit(solution)/shard_map/ppermute | solution.py:915
  86.8 15.2 %collective-permute-start.14 = (bf16[4,2,96,384]{3,2,1,0:T(8,128)(2,1)}, bf16[4,2,96,384]{3,2,1,0:T(8,128)(2,1)S(1)}, u32[]{:S(2)}, u32[]{:S(2)}) collective-permute-start(bf16[4,2,96,384]{3,2,1,0:T(8,128)(2,1)} %get-tuple-element.108.refs_7_.first), channel_id=1, source_target_pairs={{0,2},{1,3},{2,0},{3,1},{4,6},{5,7},{6,4},{7,5},{8,10},{9,11},{10,... | collective-permute-start | bytes 1769480 | tf_op jit(solution)/shard_map/ppermute | solution.py:915
  158.6 26.2 %collective-permute-start.21 = (bf16[4,2,24,1920]{3,2,1,0:T(8,128)(2,1)}, bf16[4,2,24,1920]{3,2,1,0:T(8,128)(2,1)S(1)}, u32[]{:S(2)}, u32[]{:S(2)}) collective-permute-start(bf16[4,2,24,1920]{3,2,1,0:T(8,128)(2,1)} %get-tuple-element.127), channel_id=1, source_target_pairs={{0,2},{1,3},{2,0},{3,1},{4,6},{5,7},{6,4},{7,5},{8,10},{9,11},{10,... | collective-permute-start | bytes 2211848 | tf_op jit(solution)/shard_map/ppermute | solution.py:915
  159.0 25.8 %collective-permute-start.20 = (bf16[4,2,24,1920]{3,2,1,0:T(8,128)(2,1)}, bf16[4,2,24,1920]{3,2,1,0:T(8,128)(2,1)S(1)}, u32[]{:S(2)}, u32[]{:S(2)}) collective-permute-start(bf16[4,2,24,1920]{3,2,1,0:T(8,128)(2,1)} %get-tuple-element.124.refs_1_), channel_id=1, source_target_pairs={{0,1},{1,0},{2,3},{3,2},{4,5},{5,4},{6,7},{7,6},{8,9},{9,8},{10,11... | collective-permute-start | bytes 2211848 | tf_op jit(solution)/shard_map/ppermute | solution.py:915
  183.2 23.0 %collective-permute-start.24 = (bf16[384,2304]{1,0:T(8,128)(2,1)}, bf16[384,2304]{1,0:T(8,128)(2,1)S(1)}, u32[]{:S(2)}, u32[]{:S(2)}) collective-permute-start(bf16[384,2304]{1,0:T(8,128)(2,1)} %get-tuple-element.132.refs_0_), channel_id=1, source_target_pairs={{0,16},{16,0},{1,17},{17,1},{2,18},{18,2},{3,19},{19,3},{4,20},{20... | collective-permute-start | bytes 5308424 | tf_op jit(solution)/shard_map/ppermute | solution.py:919
  183.2 21.4 %collective-permute-start.19 = (bf16[7,32,768]{2,1,0:T(8,128)(2,1)S(1)}, bf16[7,32,768]{2,1,0:T(8,128)(2,1)S(1)}, u32[]{:S(2)}, u32[]{:S(2)}) collective-permute-start(bf16[7,32,768]{2,1,0:T(8,128)(2,1)S(1)} %copy-done.6), channel_id=1, source_target_pairs={{1,0},{3,2},{5,4},{7,6},{9,8},{11,10},{13,12},{15,14},{17,16},{19,... | collective-permute-start | bytes 1032200 | tf_op jit(solution)/shard_map/ppermute | solution.py:1265
  189.8 22.1 %collective-permute-start.23 = (bf16[4,24,1920]{2,1,0:T(8,128)(2,1)}, bf16[4,24,1920]{2,1,0:T(8,128)(2,1)S(1)}, u32[]{:S(2)}, u32[]{:S(2)}) collective-permute-start(bf16[4,24,1920]{2,1,0:T(8,128)(2,1)} %get-tuple-element.136), channel_id=1, source_target_pairs={{0,1},{1,0},{2,3},{3,2},{4,5},{5,4},{6,7},{7,6},{8,9},{9,8},{10,11... | collective-permute-start | bytes 1105928 | tf_op jit(solution)/shard_map/ppermute | solution.py:915
  192.5 19.5 %collective-permute-start.22 = (bf16[4,24,1920]{2,1,0:T(8,128)(2,1)}, bf16[4,24,1920]{2,1,0:T(8,128)(2,1)S(1)}, u32[]{:S(2)}, u32[]{:S(2)}) collective-permute-start(bf16[4,24,1920]{2,1,0:T(8,128)(2,1)} %get-tuple-element.134.refs_8_), channel_id=1, source_target_pairs={{0,2},{1,3},{2,0},{3,1},{4,6},{5,7},{6,4},{7,5},{8,10},{9,11},{10,... | collective-permute-start | bytes 1105928 | tf_op jit(solution)/shard_map/ppermute | solution.py:915
  211.3 17.3 %collective-permute-start.29 = (bf16[4,2,24,1408]{3,2,1,0:T(8,128)(2,1)}, bf16[4,2,24,1408]{3,2,1,0:T(8,128)(2,1)S(1)}, u32[]{:S(2)}, u32[]{:S(2)}) collective-permute-start(bf16[4,2,24,1408]{3,2,1,0:T(8,128)(2,1)} %get-tuple-element.149), channel_id=1, source_target_pairs={{0,1},{1,0},{2,3},{3,2},{4,5},{5,4},{6,7},{7,6},{8,9},{9,8},{10,11... | collective-permute-start | bytes 1622024 | tf_op jit(solution)/shard_map/ppermute | solution.py:915
  211.3 17.3 %collective-permute-start.30 = (bf16[4,2,24,1280]{3,2,1,0:T(8,128)(2,1)}, bf16[4,2,24,1280]{3,2,1,0:T(8,128)(2,1)S(1)}, u32[]{:S(2)}, u32[]{:S(2)}) collective-permute-start(bf16[4,2,24,1280]{3,2,1,0:T(8,128)(2,1)} %get-tuple-element.151), channel_id=1, source_target_pairs={{0,2},{1,3},{2,0},{3,1},{4,6},{5,7},{6,4},{7,5},{8,10},{9,11},{10,... | collective-permute-start | bytes 1474568 | tf_op jit(solution)/shard_map/ppermute | solution.py:915
  217.0 19.5 %collective-permute-start.33 = (bf16[24,3840]{1,0:T(8,128)(2,1)}, bf16[24,3840]{1,0:T(8,128)(2,1)S(1)}, u32[]{:S(2)}, u32[]{:S(2)}) collective-permute-start(bf16[24,3840]{1,0:T(8,128)(2,1)} %get-tuple-element.157), channel_id=1, source_target_pairs={{0,8},{1,9},{2,10},{3,11},{4,12},{5,13},{6,14},{7,15},{8,0},{9,1},... | collective-permute-start | bytes 552968 | tf_op jit(solution)/shard_map/ppermute | solution.py:924
  219.6 17.0 %collective-permute-start.34 = (bf16[24,3840]{1,0:T(8,128)(2,1)}, bf16[24,3840]{1,0:T(8,128)(2,1)S(1)}, u32[]{:S(2)}, u32[]{:S(2)}) collective-permute-start(bf16[24,3840]{1,0:T(8,128)(2,1)} %get-tuple-element.158), channel_id=1, source_target_pairs={{0,12},{1,13},{2,14},{3,15},{4,8},{5,9},{6,10},{7,11},{8,4},{9,5},... | collective-permute-start | bytes 552968 | tf_op jit(solution)/shard_map/ppermute | solution.py:924
  235.2 16.0 %collective-permute-start.28 = (bf16[7,32,768]{2,1,0:T(8,128)(2,1)S(1)}, bf16[7,32,768]{2,1,0:T(8,128)(2,1)S(1)}, u32[]{:S(2)}, u32[]{:S(2)}) collective-permute-start(bf16[7,32,768]{2,1,0:T(8,128)(2,1)S(1)} %copy-done.4), channel_id=1, source_target_pairs={{1,0},{3,2},{5,4},{7,6},{9,8},{11,10},{13,12},{15,14},{17,16},{19,... | collective-permute-start | bytes 1032200 | tf_op jit(solution)/shard_map/ppermute | solution.py:1265
  248.8 13.2 %collective-permute-start.36 = (bf16[24,2688]{1,0:T(8,128)(2,1)}, bf16[24,2688]{1,0:T(8,128)(2,1)S(1)}, u32[]{:S(2)}, u32[]{:S(2)}) collective-permute-start(bf16[24,2688]{1,0:T(8,128)(2,1)} %get-tuple-element.163), channel_id=1, source_target_pairs={{0,8},{1,9},{2,10},{3,11},{4,12},{5,13},{6,14},{7,15},{8,0},{9,1},... | collective-permute-start | bytes 387080 | tf_op jit(solution)/shard_map/ppermute | solution.py:924
  249.8 12.2 %collective-permute-start.37 = (bf16[24,2688]{1,0:T(8,128)(2,1)}, bf16[24,2688]{1,0:T(8,128)(2,1)S(1)}, u32[]{:S(2)}, u32[]{:S(2)}) collective-permute-start(bf16[24,2688]{1,0:T(8,128)(2,1)} %get-tuple-element.164), channel_id=1, source_target_pairs={{0,12},{1,13},{2,14},{3,15},{4,8},{5,9},{6,10},{7,11},{8,4},{9,5},... | collective-permute-start | bytes 387080 | tf_op jit(solution)/shard_map/ppermute | solution.py:924
  (65 other events, 279.4 us)
Sparse Core Ops, SparseCore 0:
  10.9 76.5 all-gather.1
  141.3 122.8 reduce-scatter.1

commit v5 on v4

--- a/solution.py
+++ b/solution.py
@@ -821,11 +821,26 @@
     )(img.reshape(1), norm, joint, mixed, expand, tables, *earlier)
 
 
-def place_kernel(depth, slots, place_ref, ready_ref, *refs):
+def wide_kernel(part_ref, out_ref):
+    out_ref[...] = part_ref[...].astype(F32)
+
+
+def wide(part, *earlier):
+    vmem = pl.BlockSpec(memory_space=pltpu.VMEM)
+    return pl.pallas_call(
+        ordered(wide_kernel, 1, earlier),
+        in_specs=[vmem] + [ANY] * len(earlier),
+        out_specs=vmem,
+        out_shape=jax.ShapeDtypeStruct(part.shape, F32),
+        cost_estimate=cost(0.3),
+        name="wide",
+    )(part, *earlier)
+
+
+def place_kernel(depth, slots, place_ref, *refs):
     parts = refs[:depth]
-    wide_ref, triple_ref, height_ref, width_ref = refs[depth : depth + 4]
-    vector_refs = refs[depth + 4 :]
-    wide_ref[...] = ready_ref[...].astype(F32)
+    triple_ref, height_ref, width_ref = refs[depth : depth + 3]
+    vector_refs = refs[depth + 3 :]
     block = triple_ref.shape[0]
     pairs = HEADS // 2
     width = pairs * 128
@@ -864,21 +879,21 @@
         width_ref[slot : slot + 1] = line[:, 64:]
 
 
-def place(bits, ready, parts, slots, *earlier):
+def place(bits, parts, slots, *earlier):
     vmem = pl.BlockSpec(memory_space=pltpu.VMEM)
     block = parts[0].shape[0]
     width = HEADS * HEAD_DIM
-    shapes = [ready.shape, (block, 3 * width)] + [(slots, HEAD_DIM)] * 2
+    shapes = [(block, 3 * width)] + [(slots, HEAD_DIM)] * 2
     shapes += [(1, block)] * 6 + [(1, 2 * block), (1, 4 * block)]
     return pl.pallas_call(
-        ordered(partial(place_kernel, len(parts), slots), 2 + len(parts), earlier),
-        in_specs=[pl.BlockSpec(memory_space=pltpu.SMEM)] + [vmem] * (1 + len(parts)) + [ANY] * len(earlier),
+        ordered(partial(place_kernel, len(parts), slots), 1 + len(parts), earlier),
+        in_specs=[pl.BlockSpec(memory_space=pltpu.SMEM)] + [vmem] * len(parts) + [ANY] * len(earlier),
         out_specs=[vmem] * len(shapes),
         out_shape=[jax.ShapeDtypeStruct(shape, F32) for shape in shapes],
         compiler_params=pltpu.CompilerParams(vmem_limit_bytes=VMEM_LIMIT),
         cost_estimate=cost(1.9),
         name="place",
-    )(bits, ready, *parts, *earlier)
+    )(bits, *parts, *earlier)
 
 
 def settle_kernel(cut, *refs):
@@ -1367,17 +1382,18 @@
     then(first_sum.fold_three(*last))
     first_parts = first_sum.swap_last()
     block_output = then(unpack(parity, out_win, out_rows, tokens.shape, *last))
-    grad_rows = to_even(then(send_rows(grad_win, moved, *last, *first_parts[1:2])))
-    then(last_sum.fold_two(*last))
+    grad_rows = to_even(then(send_rows(grad_win, moved, *last)))
+    then(last_sum.fold_two(*last, *first_parts[1:2]))
     last_sum.swap_far()
     expand_shard, output_shard = then(settle(first_parts, expand_far.shape[1], *last))
     then(last_sum.fold_three(*last))
     last_parts = last_sum.swap_last()
     input_grad = then(unpack(parity, grad_win, grad_rows, tokens.shape, *last))
     (
-        reduce_shard, triple_shard, height_grad, width_grad, pre_gain_grad, pre_bias_grad, output_bias_grad,
+        triple_shard, height_grad, width_grad, pre_gain_grad, pre_bias_grad, output_bias_grad,
         post_gain_grad, post_bias_grad, reduce_bias_grad, triple_bias_grad, expand_bias_grad,
-    ) = place(last_sum.bits, reduce_part, last_parts, height_table.shape[0], *last)
+    ) = then(place(last_sum.bits, last_parts, height_table.shape[0], *last))
+    reduce_shard = wide(reduce_part, *last)
     return (
         block_output,
         input_grad,

time: 274 us -> 275 us (level)
  waiting for transfers between devices: 34.5 us -> 30.5 us
  transfers between devices with their start and end apart: 40 -> 40, of which waited for: 13 -> 14; matrix products, arithmetic and copies ran while one was open for 2% -> 2% of each run, Pallas kernels for 45% -> 45%
where the time goes in v5:
time: 275 us; the launch traced here: 274 us
  Pallas kernels  154 us (56%)
  starting transfers between devices  49.1 us (18%)
  waiting for transfers between devices  30.5 us (11%)
  local copies, waits for them, and re-layouts  21.8 us (8%)
  between operations  14.4 us (5%)
  other arithmetic  4.29 us (2%)
    pallas_call x1, Pallas kernels, mlp(): pl.pallas_call(ordered(mlp_kernel, 7, earlier), grid_spec=pltpu.PrefetchS...  28.3 us
    ppermute x12, starting transfers between devices, swap_depth(): lax.ppermute(block, 'rows', [(place, place ^ 4 * step) for place in range...  21.4 us
    pallas_call x6, Pallas kernels, fold_call(): pl.pallas_call(kernel, in_specs=[pl.BlockSpec(memory_space=pltpu.SMEM)] +...  20.7 us
    ppermute x16, starting transfers between devices, swap_rows(): lax.ppermute(block, 'rows', [(place, place ^ 1 << bit) for place in range...  19.9 us
    unnamed x100, local copies, waits for them, and re-layouts  18.1 us
    pallas_call x6, Pallas kernels, call(): pl.pallas_call(kernel, in_specs=[pl.BlockSpec(memory_space=pltpu.SMEM)] +...  14.8 us
    pallas_call x1, Pallas kernels, attend_back(): pl.pallas_call(kernel, grid=(count,), in_specs=[column(begin), column(pai...  14.6 us
    ppermute x12, waiting for transfers between devices, swap_depth(): lax.ppermute(block, 'rows', [(place, place ^ 4 * step) for place in range...  13.6 us
  transfers between devices with their start and end apart: 40, of which 14 were waited for; matrix products, arithmetic and copies ran while one was open for 2% of the time, Pallas kernels for 45%

profile of v5, /device:TPU:0, one launch (start us, length us, event | category | flops | bytes accessed | tf_op | source)
XLA Modules:
  0.0 273.8 jit_solution(1120903855089597311)
XLA Ops:
  10.6 3.0 %collective-permute-start.2 = (bf16[24,2432]{1,0:T(8,128)(2,1)}, bf16[24,2432]{1,0:T(8,128)(2,1)S(1)}, u32[]{:S(2)}, u32[]{:S(2)}) collective-permute-start(bf16[24,2432]{1,0:T(8,128)(2,1)} %carry.1.refs_1_.refs_0_), channel_id=1, source_target_pairs={{0,4},{1,5},{2,6},{3,7},{4,0},{5,1},{6,2},{7,3},{8,12},{9,13},{10,... | collective-permute-start | bytes 350216 | tf_op jit(solution)/shard_map/ppermute | solution.py:939
  20.4 3.8 %collective-permute-start = (bf16[14,32,768]{2,1,0:T(8,128)(2,1)S(1)}, bf16[14,32,768]{2,1,0:T(8,128)(2,1)S(1)}, u32[]{:S(2)}, u32[]{:S(2)}) collective-permute-start(bf16[14,32,768]{2,1,0:T(8,128)(2,1)S(1)} %pad_maximum_fusion), channel_id=1, source_target_pairs={{0,1},{2,3},{4,5},{6,7},{8,9},{10,11},{12,13},{14,15},{16,17},{18,... | collective-permute-start | bytes 2064392 | tf_op jit(solution)/shard_map/ppermute | solution.py:1275
  40.9 2.9 %pack.2.refs_4_.refs_1_.refs_3_ = bf16[624,768]{1,0:T(8,128)(2,1)} custom-call(s32[1]{0:T(128)} %bitcast.refs_0_, bf16[21,42,768]{2,1,0:T(8,128)(2,1)} %refs_1_.2, bf16[14,32,768]{2,1,0:T(8,128)(2,1)} %copy-done.21, f32[624,1]{1,0:T(8,128)} %reshape.154.refs_3_.refs_2_.refs_4_.refs_5_, bf16[4,24,1152]{2,1,0:T(8,128)(2,1)} %get-tuple-element.96.refs_4_.refs_0_), custom_call_target="tpu_custom_call" | custom-call | flops 3000000000 | bytes 1 | tf_op jit(solution)/shard_map/pack/pallas_call | solution.py:378
  43.8 3.7 %collective-permute-done.4.refs_1_ = bf16[4,24,1152]{2,1,0:T(8,128)(2,1)S(1)} collective-permute-done((bf16[4,24,1152]{2,1,0:T(8,128)(2,1)}, bf16[4,24,1152]{2,1,0:T(8,128)(2,1)S(1)}, u32[]{:S(2)}, u32[]{:S(2)}) %collective-permute-start.4) | collective-permute-done | bytes 221216 | tf_op jit(solution)/shard_map/ppermute | solution.py:930
  56.7 3.0 %pack.3.refs_0_.refs_2_.refs_4_ = bf16[624,768]{1,0:T(8,128)(2,1)} custom-call(s32[1]{0:T(128)} %bitcast.refs_0_, bf16[21,42,768]{2,1,0:T(8,128)(2,1)} %refs_1_.3, bf16[14,32,768]{2,1,0:T(8,128)(2,1)} %copy-done.21, f32[624,1]{1,0:T(8,128)} %reshape.154.refs_3_.refs_2_.refs_4_.refs_5_, bf16[4,2,24,1152]{3,2,1,0:T(8,128)(2,1)} %get-tuple-element.98.refs_4_.first), custom_call_target="tpu_custom_call" | custom-call | flops 3000000000 | bytes 1 | tf_op jit(solution)/shard_map/pack/pallas_call | solution.py:378
  63.7 2.8 %join_three.2 = bf16[4,2,2,24,2432]{4,3,2,1,0:T(8,128)(2,1)} custom-call(s32[3]{0:T(128)} %pad_add_fusion.bits_ref.refs_0_, bf16[4,2,24,1152]{3,2,1,0:T(8,128)(2,1)} %get-tuple-element.98.refs_4_.first, bf16[4,2,24,1152]{3,2,1,0:T(8,128)(2,1)} %copy-done.28, bf16[4,2,24,1280]{3,2,1,0:T(8,128)(2,1)} %get-tuple-element.99.second, ...), custom_call_target="tpu_custom_call" | custom-call | flops 2300000000 | bytes 1 | tf_op jit(solution)/shard_map/join_three/pallas_call | solution.py:1083
  75.3 7.2 %project.1 = (bf16[624,768]{1,0:T(8,128)(2,1)}, bf16[624,2304]{1,0:T(8,128)(2,1)}) custom-call(s32[1]{0:T(128)} %bitcast.1.refs_0_, bf16[624,768]{1,0:T(8,128)(2,1)} %pack.2.refs_4_.refs_1_.refs_3_, f32[624,1]{1,0:T(8,128)} %reshape.154.refs_3_.refs_2_.refs_4_.refs_5_, f32[8,768]{1,0:T(8,128)} %get-tuple-element.101.refs_3_.refs_2_.refs_6_, ...), custom_call_target="tpu_custom_call" | custom-call | flops 7000000000 | bytes 1 | tf_op jit(solution)/shard_map/project/pallas_call | solution.py:565
  87.2 11.2 %attend.1 = (bf16[624,768]{1,0:T(8,128)(2,1)}, f32[6,8,1536]{2,1,0:T(8,128)}, bf16[624,768]{1,0:T(8,128)(2,1)}) custom-call(bf16[624,2304]{1,0:T(8,128)(2,1)} %get-tuple-element.104.refs_0_.refs_1_.refs_2_, bf16[624,2304]{1,0:T(8,128)(2,1)} %get-tuple-element.104.refs_0_.refs_1_.refs_2_, bf16[624,2304]{1,0:T(8,128)(2,1)} %get-tuple-element.104.refs_0_.refs_1_.refs_2_, ...), custom_call_target="tpu_custom_call" | custom-call | flops 11000000512 | bytes 1 | tf_op jit(solution)/shard_map/attend/pallas_call | solution.py:280
  98.4 2.8 %collective-permute-done.15.second_far = bf16[4,2,96,384]{3,2,1,0:T(8,128)(2,1)S(1)} collective-permute-done((bf16[4,2,96,384]{3,2,1,0:T(8,128)(2,1)}, bf16[4,2,96,384]{3,2,1,0:T(8,128)(2,1)S(1)}, u32[]{:S(2)}, u32[]{:S(2)}) %collective-permute-start.15) | collective-permute-done | bytes 589856 | tf_op jit(solution)/shard_map/ppermute | solution.py:930
  102.9 3.3 %join_three.3 = bf16[4,2,2,96,768]{4,3,2,1,0:T(8,128)(2,1)} custom-call(s32[3]{0:T(128)} %pad_add_fusion.bits_ref.refs_0_, bf16[4,2,96,384]{3,2,1,0:T(8,128)(2,1)} %get-tuple-element.107.refs_7_.first, bf16[4,2,96,384]{3,2,1,0:T(8,128)(2,1)} %copy-done.24, bf16[4,2,96,384]{3,2,1,0:T(8,128)(2,1)} %get-tuple-element.109.second, ...), custom_call_target="tpu_custom_call" | custom-call | flops 2300000000 | bytes 1 | tf_op jit(solution)/shard_map/join_three/pallas_call | solution.py:1083
  106.2 4.8 %mix.1 = (f32[624,768]{1,0:T(8,128)}, bf16[624,768]{1,0:T(8,128)(2,1)}) custom-call(bf16[624,768]{1,0:T(8,128)(2,1)} %get-tuple-element.108.refs_0_.refs_8_, bf16[768,3840]{1,0:T(8,128)(2,1)} %all-gather.2.cloned.1.call-done.refs_1_.refs_3_.refs_7_, f32[8,768]{1,0:T(8,128)} %get-tuple-element.101.refs_3_.refs_2_.refs_6_, ...), custom_call_target="tpu_custom_call" | custom-call | flops 4600000000 | bytes 1 | tf_op jit(solution)/shard_map/mix/pallas_call | solution.py:664
  112.3 28.3 %mlp.1 = (f32[624,768]{1,0:T(8,128)}, f32[624,768]{1,0:T(8,128)}, bf16[3072,768]{1,0:T(8,128)(2,1)}, bf16[384,3072]{1,0:T(8,128)(2,1)}, bf16[384,3072]{1,0:T(8,128)(2,1)}, /*index=5*/f32[1,3072]{1,0:T(1,128)}) custom-call(s32[1]{0:T(128)} %bitcast.1.refs_0_, bf16[624,768]{1,0:T(8,128)(2,1)} %get-tuple-element.111.refs_1_, ...), custom_call_target="tpu_custom_call" | custom-call | flops 28999999488 | bytes 1 | tf_op jit(solution)/shard_map/mlp/pallas_call | solution.py:512
  141.2 8.6 %mix_back.1 = (f32[624,768]{1,0:T(8,128)}, bf16[624,768]{1,0:T(8,128)(2,1)}, bf16[384,768]{1,0:T(8,128)(2,1)}, bf16[384,768]{1,0:T(8,128)(2,1)}, bf16[624,768]{1,0:T(8,128)(2,1)}, /*index=5*/f32[4,768]{1,0:T(4,128)}) custom-call(s32[1]{0:T(128)} %bitcast.1.refs_0_, f32[624,768]{1,0:T(8,128)} %get-tuple-element.114.refs_1_, ...), custom_call_target="tpu_custom_call" | custom-call | flops 7000000000 | bytes 1 | tf_op jit(solution)/shard_map/mix_back/pallas_call | solution.py:714
  153.5 5.0 %fold_one.2 = (bf16[4,2,24,1920]{3,2,1,0:T(8,128)(2,1)}, f32[4,2,24,1920]{3,2,1,0:T(8,128)}, bf16[4,2,24,1920]{3,2,1,0:T(8,128)(2,1)}, f32[4,2,24,1920]{3,2,1,0:T(8,128)}) custom-call(s32[3]{0:T(128)} %pad_add_fusion.bits_ref.refs_0_, bf16[4,2,2,24,3072]{4,3,2,1,0:T(8,128)(2,1)} %bitcast.58, bf16[4,2,2,24,768]{4,3,2,1,0:T(8,128)(2,1)} %bitcast.59, ...), custom_call_target="tpu_custom_call" | custom-call | flops 2300000000 | bytes 1 | tf_op jit(solution)/shard_map/fold_one/pallas_call | solution.py:1196
  162.3 14.6 %attend_back.1 = (bf16[624,2304]{1,0:T(8,128)(2,1)}, f32[6,128,128]{2,1,0:T(8,128)}, f32[2,768]{1,0:T(2,128)}) custom-call(bf16[624,2304]{1,0:T(8,128)(2,1)} %get-tuple-element.104.refs_0_.refs_1_.refs_2_, bf16[624,2304]{1,0:T(8,128)(2,1)} %get-tuple-element.104.refs_0_.refs_1_.refs_2_, bf16[624,2304]{1,0:T(8,128)(2,1)} %get-tuple-element.104.refs_0_.refs_1_.refs_2_, ...), custom_call_target="tpu_custom_call" | custom-call | flops 8999999488 | bytes 1 | tf_op jit(solution)/shard_map/attend_back/pallas_call | solution.py:305
  176.9 6.4 %entry_grads.1 = (bf16[384,2304]{1,0:T(8,128)(2,1)}, bf16[384,2304]{1,0:T(8,128)(2,1)}) custom-call(s32[1]{0:T(128)} %bitcast.1.refs_0_, bf16[624,768]{1,0:T(8,128)(2,1)} %get-tuple-element.106.refs_4_.refs_1_, bf16[624,2304]{1,0:T(8,128)(2,1)} %get-tuple-element.129.refs_2_.refs_5_, f32[2,768]{1,0:T(2,128)} %get-tuple-element.130.refs_3_.refs_2_), custom_call_target="tpu_custom_call" | custom-call | flops 5000000000 | bytes 1 | tf_op jit(solution)/shard_map/entry_grads/pallas_call | solution.py:754
  186.0 3.8 %fold_two.2 = (bf16[4,24,1920]{2,1,0:T(8,128)(2,1)}, f32[4,24,1920]{2,1,0:T(8,128)}, bf16[4,24,1920]{2,1,0:T(8,128)(2,1)}, f32[4,24,1920]{2,1,0:T(8,128)}) custom-call(s32[3]{0:T(128)} %pad_add_fusion.bits_ref.refs_0_, f32[4,2,24,1920]{3,2,1,0:T(8,128)} %get-tuple-element.124.a_near, bf16[4,2,24,1920]{3,2,1,0:T(8,128)(2,1)} %copy-done.20, ...), custom_call_target="tpu_custom_call" | custom-call | flops 2300000000 | bytes 1 | tf_op jit(solution)/shard_map/fold_two/pallas_call | solution.py:1196
  193.9 8.6 %project_back.1 = (bf16[624,768]{1,0:T(8,128)(2,1)}, f32[2,768]{1,0:T(2,128)}) custom-call(s32[1]{0:T(128)} %bitcast.1.refs_0_, bf16[624,768]{1,0:T(8,128)(2,1)} %pack.2.refs_4_.refs_1_.refs_3_, f32[624,1]{1,0:T(8,128)} %reshape.154.refs_3_.refs_2_.refs_4_.refs_5_, f32[8,768]{1,0:T(8,128)} %get-tuple-element.101.refs_3_.refs_2_.refs_6_, ...), custom_call_target="tpu_custom_call" | custom-call | flops 11000000512 | bytes 1 | tf_op jit(solution)/shard_map/project_back/pallas_call | solution.py:631
  207.4 3.8 %fold_one.3 = (bf16[4,2,24,1408]{3,2,1,0:T(8,128)(2,1)}, f32[4,2,24,1152]{3,2,1,0:T(8,128)}, bf16[4,2,24,1280]{3,2,1,0:T(8,128)(2,1)}, f32[4,2,24,1280]{3,2,1,0:T(8,128)}, bf16[24,256]{1,0:T(8,128)(2,1)}) custom-call(s32[3]{0:T(128)} %pad_add_fusion.bits_ref.refs_0_, bf16[4,2,2,24,2304]{4,3,2,1,0:T(8,128)(2,1)} %bitcast.34, ...), custom_call_target="tpu_custom_call" | custom-call | flops 300000000 | bytes 1 | tf_op jit(solution)/shard_map/fold_one/pallas_call | solution.py:1196
  219.8 2.9 %unpack.2.refs_1_ = bf16[21,42,768]{2,1,0:T(8,128)(2,1)} custom-call(s32[1]{0:T(128)} %bitcast.refs_0_, bf16[624,768]{1,0:T(8,128)(2,1)} %get-tuple-element.117.refs_0_.refs_1_, bf16[7,32,768]{2,1,0:T(8,128)(2,1)} %copy-done.3, f32[24,3840]{1,0:T(8,128)} %get-tuple-element.144.refs_3_.refs_0_), custom_call_target="tpu_custom_call" | custom-call | flops 500000000 | bytes 1 | tf_op jit(solution)/shard_map/unpack/pallas_call | solution.py:407
  226.8 3.1 %fold_two.3 = (bf16[4,24,1408]{2,1,0:T(8,128)(2,1)}, f32[4,24,1152]{2,1,0:T(8,128)}, bf16[4,24,1280]{2,1,0:T(8,128)(2,1)}, f32[4,24,1280]{2,1,0:T(8,128)}, bf16[24,256]{1,0:T(8,128)(2,1)}) custom-call(s32[3]{0:T(128)} %pad_add_fusion.bits_ref.refs_0_, f32[4,2,24,1152]{3,2,1,0:T(8,128)} %get-tuple-element.146.a_near, bf16[4,2,24,1408]{3,2,1,0:T(8,128)(2,1)} %copy-done.25, ...), custom_call_target="tpu_custom_call" | custom-call | flops 2300000000 | bytes 1 | tf_op jit(solution)/shard_map/fold_two/pallas_call | solution.py:1196
  243.6 5.1 %collective-permute-start.35 = (bf16[24,2688]{1,0:T(8,128)(2,1)}, bf16[24,2688]{1,0:T(8,128)(2,1)S(1)}, u32[]{:S(2)}, u32[]{:S(2)}) collective-permute-start(bf16[24,2688]{1,0:T(8,128)(2,1)} %get-tuple-element.160), channel_id=1, source_target_pairs={{0,4},{1,5},{2,6},{3,7},{4,0},{5,1},{6,2},{7,3},{8,12},{9,13},{10,... | collective-permute-start | bytes 387080 | tf_op jit(solution)/shard_map/ppermute | solution.py:939
  252.0 2.9 %unpack.3.refs_5_ = bf16[21,42,768]{2,1,0:T(8,128)(2,1)} custom-call(s32[1]{0:T(128)} %bitcast.refs_0_, bf16[624,768]{1,0:T(8,128)(2,1)} %get-tuple-element.145.refs_0_.refs_1_, bf16[7,32,768]{2,1,0:T(8,128)(2,1)} %copy-done.4, f32[24,2688]{1,0:T(8,128)} %get-tuple-element.159.refs_3_.refs_1_), custom_call_target="tpu_custom_call" | custom-call | flops 500000000 | bytes 1 | tf_op jit(solution)/shard_map/unpack/pallas_call | solution.py:407
  254.9 7.1 %collective-permute-done.36.refs_3_ = bf16[24,2688]{1,0:T(8,128)(2,1)S(1)} collective-permute-done((bf16[24,2688]{1,0:T(8,128)(2,1)}, bf16[24,2688]{1,0:T(8,128)(2,1)S(1)}, u32[]{:S(2)}, u32[]{:S(2)}) %collective-permute-start.36) | collective-permute-done | bytes 129056 | tf_op jit(solution)/shard_map/ppermute | solution.py:939
  (206 shorter events, 110.7 us)
Async XLA Ops:
  7.2 99.0 %all-gather.2.cloned.1.call-start = ((), (), s32[]{:S(2)}) async-start(), calls=%async_computation.1 | async-start | bytes 6082560 | tf_op jit(solution)/shard_map/all_gather | solution.py:1328
  8.9 256.4 %reduce-scatter.2.cloned.1.call-start = ((), (), s32[]{:S(2)}) async-start(), calls=%async_computation.2 | async-start | bytes 4866048 | tf_op jit(solution)/shard_map/reduce_scatter | solution.py:1357
  10.6 18.6 %collective-permute-start.2 = (bf16[24,2432]{1,0:T(8,128)(2,1)}, bf16[24,2432]{1,0:T(8,128)(2,1)S(1)}, u32[]{:S(2)}, u32[]{:S(2)}) collective-permute-start(bf16[24,2432]{1,0:T(8,128)(2,1)} %carry.1.refs_1_.refs_0_), channel_id=1, source_target_pairs={{0,4},{1,5},{2,6},{3,7},{4,0},{5,1},{6,2},{7,3},{8,12},{9,13},{10,... | collective-permute-start | bytes 350216 | tf_op jit(solution)/shard_map/ppermute | solution.py:939
  17.8 26.0 %collective-permute-start.7 = (bf16[96,768]{1,0:T(8,128)(2,1)}, bf16[96,768]{1,0:T(8,128)(2,1)S(1)}, u32[]{:S(2)}, u32[]{:S(2)}) collective-permute-start(bf16[96,768]{1,0:T(8,128)(2,1)} %stack.10.refs_4_.refs_0_), channel_id=1, source_target_pairs={{0,4},{1,5},{2,6},{3,7},{4,0},{5,1},{6,2},{7,3},{8,12},{9,13},{10,... | collective-permute-start | bytes 442376 | tf_op jit(solution)/shard_map/ppermute | solution.py:939
  18.4 25.5 %collective-permute-start.6 = (bf16[96,768]{1,0:T(8,128)(2,1)}, bf16[96,768]{1,0:T(8,128)(2,1)S(1)}, u32[]{:S(2)}, u32[]{:S(2)}) collective-permute-start(bf16[96,768]{1,0:T(8,128)(2,1)} %stack.10.refs_4_.refs_0_), channel_id=1, source_target_pairs={{0,8},{1,9},{2,10},{3,11},{4,12},{5,13},{6,14},{7,15},{8,0},{9,1},... | collective-permute-start | bytes 442376 | tf_op jit(solution)/shard_map/ppermute | solution.py:939
  20.4 19.6 %collective-permute-start = (bf16[14,32,768]{2,1,0:T(8,128)(2,1)S(1)}, bf16[14,32,768]{2,1,0:T(8,128)(2,1)S(1)}, u32[]{:S(2)}, u32[]{:S(2)}) collective-permute-start(bf16[14,32,768]{2,1,0:T(8,128)(2,1)S(1)} %pad_maximum_fusion), channel_id=1, source_target_pairs={{0,1},{2,3},{4,5},{6,7},{8,9},{10,11},{12,13},{14,15},{16,17},{18,... | collective-permute-start | bytes 2064392 | tf_op jit(solution)/shard_map/ppermute | solution.py:1275
  34.3 13.2 %collective-permute-start.4 = (bf16[4,24,1152]{2,1,0:T(8,128)(2,1)}, bf16[4,24,1152]{2,1,0:T(8,128)(2,1)S(1)}, u32[]{:S(2)}, u32[]{:S(2)}) collective-permute-start(bf16[4,24,1152]{2,1,0:T(8,128)(2,1)} %get-tuple-element.96.refs_4_.refs_0_), channel_id=1, source_target_pairs={{0,1},{1,0},{2,3},{3,2},{4,5},{5,4},{6,7},{7,6},{8,9},{9,8},{10,11... | collective-permute-start | bytes 663560 | tf_op jit(solution)/shard_map/ppermute | solution.py:930
  35.7 11.8 %collective-permute-start.5 = (bf16[4,24,1280]{2,1,0:T(8,128)(2,1)}, bf16[4,24,1280]{2,1,0:T(8,128)(2,1)S(1)}, u32[]{:S(2)}, u32[]{:S(2)}) collective-permute-start(bf16[4,24,1280]{2,1,0:T(8,128)(2,1)} %get-tuple-element.97.refs_2_), channel_id=1, source_target_pairs={{0,2},{1,3},{2,0},{3,1},{4,6},{5,7},{6,4},{7,5},{8,10},{9,11},{10,... | collective-permute-start | bytes 737288 | tf_op jit(solution)/shard_map/ppermute | solution.py:930
  69.7 12.8 %collective-permute-start.13 = (bf16[4,96,384]{2,1,0:T(8,128)(2,1)}, bf16[4,96,384]{2,1,0:T(8,128)(2,1)S(1)}, u32[]{:S(2)}, u32[]{:S(2)}) collective-permute-start(bf16[4,96,384]{2,1,0:T(8,128)(2,1)} %get-tuple-element.105.refs_2_), channel_id=1, source_target_pairs={{0,2},{1,3},{2,0},{3,1},{4,6},{5,7},{6,4},{7,5},{8,10},{9,11},{10,... | collective-permute-start | bytes 884744 | tf_op jit(solution)/shard_map/ppermute | solution.py:930
  85.8 15.4 %collective-permute-start.15 = (bf16[4,2,96,384]{3,2,1,0:T(8,128)(2,1)}, bf16[4,2,96,384]{3,2,1,0:T(8,128)(2,1)S(1)}, u32[]{:S(2)}, u32[]{:S(2)}) collective-permute-start(bf16[4,2,96,384]{3,2,1,0:T(8,128)(2,1)} %get-tuple-element.109.second), channel_id=1, source_target_pairs={{0,1},{1,0},{2,3},{3,2},{4,5},{5,4},{6,7},{7,6},{8,9},{9,8},{10,11... | collective-permute-start | bytes 1769480 | tf_op jit(solution)/shard_map/ppermute | solution.py:930
  86.8 15.2 %collective-permute-start.14 = (bf16[4,2,96,384]{3,2,1,0:T(8,128)(2,1)}, bf16[4,2,96,384]{3,2,1,0:T(8,128)(2,1)S(1)}, u32[]{:S(2)}, u32[]{:S(2)}) collective-permute-start(bf16[4,2,96,384]{3,2,1,0:T(8,128)(2,1)} %get-tuple-element.107.refs_7_.first), channel_id=1, source_target_pairs={{0,2},{1,3},{2,0},{3,1},{4,6},{5,7},{6,4},{7,5},{8,10},{9,11},{10,... | collective-permute-start | bytes 1769480 | tf_op jit(solution)/shard_map/ppermute | solution.py:930
  158.6 26.2 %collective-permute-start.21 = (bf16[4,2,24,1920]{3,2,1,0:T(8,128)(2,1)}, bf16[4,2,24,1920]{3,2,1,0:T(8,128)(2,1)S(1)}, u32[]{:S(2)}, u32[]{:S(2)}) collective-permute-start(bf16[4,2,24,1920]{3,2,1,0:T(8,128)(2,1)} %get-tuple-element.126), channel_id=1, source_target_pairs={{0,2},{1,3},{2,0},{3,1},{4,6},{5,7},{6,4},{7,5},{8,10},{9,11},{10,... | collective-permute-start | bytes 2211848 | tf_op jit(solution)/shard_map/ppermute | solution.py:930
  159.0 25.8 %collective-permute-start.20 = (bf16[4,2,24,1920]{3,2,1,0:T(8,128)(2,1)}, bf16[4,2,24,1920]{3,2,1,0:T(8,128)(2,1)S(1)}, u32[]{:S(2)}, u32[]{:S(2)}) collective-permute-start(bf16[4,2,24,1920]{3,2,1,0:T(8,128)(2,1)} %get-tuple-element.123.refs_1_), channel_id=1, source_target_pairs={{0,1},{1,0},{2,3},{3,2},{4,5},{5,4},{6,7},{7,6},{8,9},{9,8},{10,11... | collective-permute-start | bytes 2211848 | tf_op jit(solution)/shard_map/ppermute | solution.py:930
  183.2 23.0 %collective-permute-start.24 = (bf16[384,2304]{1,0:T(8,128)(2,1)}, bf16[384,2304]{1,0:T(8,128)(2,1)S(1)}, u32[]{:S(2)}, u32[]{:S(2)}) collective-permute-start(bf16[384,2304]{1,0:T(8,128)(2,1)} %get-tuple-element.131.refs_0_), channel_id=1, source_target_pairs={{0,16},{16,0},{1,17},{17,1},{2,18},{18,2},{3,19},{19,3},{4,20},{20... | collective-permute-start | bytes 5308424 | tf_op jit(solution)/shard_map/ppermute | solution.py:934
  183.2 21.4 %collective-permute-start.19 = (bf16[7,32,768]{2,1,0:T(8,128)(2,1)S(1)}, bf16[7,32,768]{2,1,0:T(8,128)(2,1)S(1)}, u32[]{:S(2)}, u32[]{:S(2)}) collective-permute-start(bf16[7,32,768]{2,1,0:T(8,128)(2,1)S(1)} %copy-done.6), channel_id=1, source_target_pairs={{1,0},{3,2},{5,4},{7,6},{9,8},{11,10},{13,12},{15,14},{17,16},{19,... | collective-permute-start | bytes 1032200 | tf_op jit(solution)/shard_map/ppermute | solution.py:1280
  189.8 22.1 %collective-permute-start.23 = (bf16[4,24,1920]{2,1,0:T(8,128)(2,1)}, bf16[4,24,1920]{2,1,0:T(8,128)(2,1)S(1)}, u32[]{:S(2)}, u32[]{:S(2)}) collective-permute-start(bf16[4,24,1920]{2,1,0:T(8,128)(2,1)} %get-tuple-element.135), channel_id=1, source_target_pairs={{0,1},{1,0},{2,3},{3,2},{4,5},{5,4},{6,7},{7,6},{8,9},{9,8},{10,11... | collective-permute-start | bytes 1105928 | tf_op jit(solution)/shard_map/ppermute | solution.py:930
  192.5 19.5 %collective-permute-start.22 = (bf16[4,24,1920]{2,1,0:T(8,128)(2,1)}, bf16[4,24,1920]{2,1,0:T(8,128)(2,1)S(1)}, u32[]{:S(2)}, u32[]{:S(2)}) collective-permute-start(bf16[4,24,1920]{2,1,0:T(8,128)(2,1)} %get-tuple-element.133.refs_8_), channel_id=1, source_target_pairs={{0,2},{1,3},{2,0},{3,1},{4,6},{5,7},{6,4},{7,5},{8,10},{9,11},{10,... | collective-permute-start | bytes 1105928 | tf_op jit(solution)/shard_map/ppermute | solution.py:930
  211.3 14.7 %collective-permute-start.28 = (bf16[4,2,24,1408]{3,2,1,0:T(8,128)(2,1)}, bf16[4,2,24,1408]{3,2,1,0:T(8,128)(2,1)S(1)}, u32[]{:S(2)}, u32[]{:S(2)}) collective-permute-start(bf16[4,2,24,1408]{3,2,1,0:T(8,128)(2,1)} %get-tuple-element.147), channel_id=1, source_target_pairs={{0,1},{1,0},{2,3},{3,2},{4,5},{5,4},{6,7},{7,6},{8,9},{9,8},{10,11... | collective-permute-start | bytes 1622024 | tf_op jit(solution)/shard_map/ppermute | solution.py:930
  211.3 14.5 %collective-permute-start.29 = (bf16[4,2,24,1280]{3,2,1,0:T(8,128)(2,1)}, bf16[4,2,24,1280]{3,2,1,0:T(8,128)(2,1)S(1)}, u32[]{:S(2)}, u32[]{:S(2)}) collective-permute-start(bf16[4,2,24,1280]{3,2,1,0:T(8,128)(2,1)} %get-tuple-element.149), channel_id=1, source_target_pairs={{0,2},{1,3},{2,0},{3,1},{4,6},{5,7},{6,4},{7,5},{8,10},{9,11},{10,... | collective-permute-start | bytes 1474568 | tf_op jit(solution)/shard_map/ppermute | solution.py:930
  217.0 19.2 %collective-permute-start.33 = (bf16[24,3840]{1,0:T(8,128)(2,1)}, bf16[24,3840]{1,0:T(8,128)(2,1)S(1)}, u32[]{:S(2)}, u32[]{:S(2)}) collective-permute-start(bf16[24,3840]{1,0:T(8,128)(2,1)} %get-tuple-element.156), channel_id=1, source_target_pairs={{0,8},{1,9},{2,10},{3,11},{4,12},{5,13},{6,14},{7,15},{8,0},{9,1},... | collective-permute-start | bytes 552968 | tf_op jit(solution)/shard_map/ppermute | solution.py:939
  219.6 16.6 %collective-permute-start.34 = (bf16[24,3840]{1,0:T(8,128)(2,1)}, bf16[24,3840]{1,0:T(8,128)(2,1)S(1)}, u32[]{:S(2)}, u32[]{:S(2)}) collective-permute-start(bf16[24,3840]{1,0:T(8,128)(2,1)} %get-tuple-element.157), channel_id=1, source_target_pairs={{0,12},{1,13},{2,14},{3,15},{4,8},{5,9},{6,10},{7,11},{8,4},{9,5},... | collective-permute-start | bytes 552968 | tf_op jit(solution)/shard_map/ppermute | solution.py:939
  232.5 18.7 %collective-permute-start.27 = (bf16[7,32,768]{2,1,0:T(8,128)(2,1)S(1)}, bf16[7,32,768]{2,1,0:T(8,128)(2,1)S(1)}, u32[]{:S(2)}, u32[]{:S(2)}) collective-permute-start(bf16[7,32,768]{2,1,0:T(8,128)(2,1)S(1)} %copy-done.5), channel_id=1, source_target_pairs={{1,0},{3,2},{5,4},{7,6},{9,8},{11,10},{13,12},{15,14},{17,16},{19,... | collective-permute-start | bytes 1032200 | tf_op jit(solution)/shard_map/ppermute | solution.py:1280
  248.8 13.2 %collective-permute-start.36 = (bf16[24,2688]{1,0:T(8,128)(2,1)}, bf16[24,2688]{1,0:T(8,128)(2,1)S(1)}, u32[]{:S(2)}, u32[]{:S(2)}) collective-permute-start(bf16[24,2688]{1,0:T(8,128)(2,1)} %get-tuple-element.161), channel_id=1, source_target_pairs={{0,8},{1,9},{2,10},{3,11},{4,12},{5,13},{6,14},{7,15},{8,0},{9,1},... | collective-permute-start | bytes 387080 | tf_op jit(solution)/shard_map/ppermute | solution.py:939
  249.8 12.2 %collective-permute-start.37 = (bf16[24,2688]{1,0:T(8,128)(2,1)}, bf16[24,2688]{1,0:T(8,128)(2,1)S(1)}, u32[]{:S(2)}, u32[]{:S(2)}) collective-permute-start(bf16[24,2688]{1,0:T(8,128)(2,1)} %get-tuple-element.162), channel_id=1, source_target_pairs={{0,12},{1,13},{2,14},{3,15},{4,8},{5,9},{6,10},{7,11},{8,4},{9,5},... | collective-permute-start | bytes 387080 | tf_op jit(solution)/shard_map/ppermute | solution.py:939
  (65 other events, 266.0 us)
Sparse Core Ops, SparseCore 0:
  10.9 76.5 all-gather.1
  141.3 122.8 reduce-scatter.1
